TPU v7x, 32 devices: a whole 2x2x4 slice. The times are simulated.
32 devices in a mesh: req: 8 (over z, y), tp: 4 (over x, core).
Axes of the slice: x: 2, y: 2, z: 4, core: 2. Of those that a mesh axis runs over, the one named last changes fastest.
Arguments:
- tokens: bfloat16 [3072, 3200], P('req'), may hold values from -6 to 6
- norm_gain: float32 [3200], replicated, may hold values from 0.5 to 2
- w_qkv: bfloat16 [3200, 6144], P('req', 'tp'), may hold values from -1 to 1
- q_gain: float32 [2048], P('tp'), may hold values from 0.5 to 2.5
- k_gain: float32 [2048], P('tp'), may hold values from 0.5 to 2.5
- w_out: bfloat16 [2048, 3200], P('tp', 'req'), may hold values from -0.125 to 0.125
- grids: int32 [24, 2], P('req'), may hold values from 2 to 16, as said below
- owners: int32 [768], P('req'), may hold values from 0 to 7, as said below
- proj_gain: float32 [4, 3200], P(None, 'tp'), may hold values from 0.5 to 2
- proj_bias: float32 [4, 3200], P(None, 'tp'), may hold values from -3 to 3
Outputs:
- received: bfloat16 [1536, 4, 3200], P('req', None, 'tp')
Inputs may be any that keep to these rules, and one draw needn't show every extreme that they name: `grids`: each image spans at least 2 half grid rows. The images of one device together take at most 96 merged slots, and on one device in every draw exactly 96. `owners`: no device's merged slots, live or padding, name one owner more than 24 times; in every draw one owner is named exactly 24 times by every device.
All inputs are finite; a program needn't handle non-finite values.
Results may differ from a plain program's by a relative error of at most 0.009.
Values may be sent and summed in bfloat16 or wider, within the bound.
No kernel may reach another device: no remote copies, remote signals or barrier semaphores. Data moves between devices by JAX's collectives and lax.ppermute only.
A program may use at most 128 MiB of HBM per device.

v0:
```python
import math

import jax
import jax.numpy as jnp
from jax import lax
from jax.sharding import PartitionSpec as P

D = 3200
HEADS = 16
HEAD_DIM = 128


def merge_layout(grid, token_count, slot_count):
    half_rows = grid[:, 0]
    half_cols = grid[:, 1]
    image_slots = half_rows * half_cols
    slot_ends = jnp.cumsum(image_slots)
    slot_starts = slot_ends - image_slots
    slot_ids = jnp.arange(slot_count, dtype=jnp.int32)
    image_ids = jnp.sum((slot_ids[:, None] >= slot_ends[None, :]).astype(jnp.int32), axis=1)
    image_count = grid.shape[0]
    is_live = image_ids < image_count
    one_hot = (image_ids[:, None] == jnp.arange(image_count, dtype=jnp.int32)[None, :]).astype(
        jnp.int32
    )
    cols_here = jnp.maximum(jnp.sum(one_hot * half_cols[None, :], axis=1), 1)
    start_here = jnp.sum(one_hot * slot_starts[None, :], axis=1)
    offset = slot_ids - start_here
    row_half = offset // cols_here
    col_half = offset % cols_here
    first_row = 4 * start_here + 4 * row_half * cols_here + 2 * col_half
    patch_rows = jnp.stack(
        [first_row, first_row + 1, first_row + 2 * cols_here, first_row + 2 * cols_here + 1], axis=1
    )
    patch_rows = jnp.where(is_live[:, None], patch_rows, 0)
    token_ids = jnp.arange(token_count, dtype=jnp.int32)
    segment = jnp.sum((token_ids[:, None] >= 4 * slot_ends[None, :]).astype(jnp.int32), axis=1)
    return (patch_rows, is_live, segment)


def owner_ranks(owner_ids, is_live):
    slot_ids = jnp.arange(owner_ids.shape[0], dtype=jnp.int32)
    earlier = (
        (owner_ids[:, None] == owner_ids[None, :])
        & (slot_ids[None, :] < slot_ids[:, None])
        & is_live[None, :]
    )
    return jnp.sum(earlier.astype(jnp.int32), axis=1)


def body(tokens, norm_gain, w_qkv, q_gain, k_gain, w_out, grids, owners, proj_gain, proj_bias):
    token_count = tokens.shape[0]
    slot_count = owners.shape[0]
    quarter = proj_gain.shape[1]
    head_share = q_gain.shape[0]
    head_count = head_share // HEAD_DIM
    head_width = HEADS * HEAD_DIM
    score_scale = 1.0 / math.sqrt(HEAD_DIM)
    feature_total = 4 * D
    devices_req = lax.axis_size("req")
    capacity = max(2, (2 * slot_count + devices_req - 1) // devices_req)
    patch_rows, is_live, segment = merge_layout(grids, token_count, slot_count)
    token_float = tokens.astype(jnp.float32)
    mean_square = jnp.mean(token_float * token_float, axis=1, keepdims=True)
    normed = (token_float * lax.rsqrt(mean_square + 1e-06) * norm_gain).astype(jnp.bfloat16)
    projected = jnp.dot(
        normed, lax.all_gather(w_qkv, "req", axis=0, tiled=True), preferred_element_type=jnp.float32
    )
    projected = projected.reshape(token_count, head_count, 3, HEAD_DIM)
    queries = projected[:, :, 0]
    key_vecs = projected[:, :, 1]
    values = projected[:, :, 2].astype(jnp.bfloat16)
    q_gains = q_gain.reshape(head_count, HEAD_DIM)
    k_gains = k_gain.reshape(head_count, HEAD_DIM)
    local_q = jnp.sum(queries * queries, axis=(1, 2))
    local_k = jnp.sum(key_vecs * key_vecs, axis=(1, 2))
    q_total, k_total = lax.psum((local_q, local_k), "tp")
    q_scale = lax.rsqrt(q_total / head_width + 1e-06)
    k_scale = lax.rsqrt(k_total / head_width + 1e-06)
    q_normed = queries * q_scale[:, None, None] * q_gains
    k_normed = key_vecs * k_scale[:, None, None] * k_gains
    scores = (
        jnp.einsum("qhd,khd->hqk", q_normed, k_normed, precision=lax.Precision.HIGHEST)
        * score_scale
    )
    same_image = segment[:, None] == segment[None, :]
    scores = jnp.where(same_image[None], scores, -1e30)
    row_top = jnp.max(scores, axis=2, keepdims=True)
    weights_raw = jnp.exp(scores - row_top)
    probs = (weights_raw / jnp.sum(weights_raw, axis=2, keepdims=True)).astype(jnp.bfloat16)
    attended = jnp.einsum("hqk,khd->qhd", probs, values, preferred_element_type=jnp.float32)
    attended = attended.astype(jnp.bfloat16).reshape(token_count, head_share)
    partial_sum = jnp.dot(
        attended,
        lax.all_gather(w_out, "req", axis=1, tiled=True),
        preferred_element_type=jnp.float32,
    )
    mine = lax.psum_scatter(
        partial_sum.astype(jnp.bfloat16), "tp", scatter_dimension=1, tiled=True
    ).astype(jnp.float32)
    token_mine = lax.dynamic_slice_in_dim(token_float, lax.axis_index("tp") * quarter, quarter, 1)
    hidden = (token_mine + mine).astype(jnp.bfloat16)
    merged = jnp.where(is_live[:, None, None], hidden[patch_rows], jnp.zeros((), jnp.bfloat16))
    ranks = owner_ranks(owners, is_live)
    target_owner = jnp.where(is_live, owners, devices_req)
    send_slots = jnp.zeros((devices_req, capacity, 4, quarter), jnp.bfloat16)
    send_slots = send_slots.at[target_owner, ranks].set(merged, mode="drop")
    owner_ids = jnp.arange(devices_req, dtype=jnp.int32)
    dest_counts = jnp.sum(
        ((owners[None, :] == owner_ids[:, None]) & is_live[None, :]).astype(jnp.int32), axis=1
    )
    dest_counts = dest_counts[:, None]
    arrived, source_counts = (
        lax.all_to_all(send_slots, "req", split_axis=0, concat_axis=0, tiled=True),
        lax.all_to_all(dest_counts, "req", split_axis=0, concat_axis=0, tiled=True),
    )
    slot_live = jnp.arange(capacity, dtype=jnp.int32)[None, :] < source_counts
    arrived_float = arrived.astype(jnp.float32)
    row_sum = jnp.sum(arrived_float, axis=(2, 3))
    row_sq = jnp.sum(arrived_float * arrived_float, axis=(2, 3))
    row_sum, row_sq = lax.psum((row_sum, row_sq), "tp")
    mean_value = row_sum / feature_total
    variance = row_sq / feature_total - mean_value * mean_value
    normed_out = (arrived_float - mean_value[:, :, None, None]) * lax.rsqrt(variance + 1e-05)[
        :, :, None, None
    ] * proj_gain + proj_bias
    normed_out = jnp.where(slot_live[:, :, None, None], normed_out, 0.0).astype(jnp.bfloat16)
    result = normed_out.reshape(devices_req * capacity, 4, quarter)
    return result


def solution(mesh):
    placed = (
        P("req", None),
        P(),
        P("req", "tp"),
        P("tp"),
        P("tp"),
        P("tp", "req"),
        P("req", None),
        P("req"),
        P(None, "tp"),
        P(None, "tp"),
    )
    return jax.shard_map(
        body, mesh=mesh, in_specs=placed, out_specs=P("req", None, "tp"), check_vma=False
    )
```

profile of v0, /device:TPU:0, one launch (start us, length us, event | category | flops | bytes accessed | tf_op | source)
XLA Modules:
  0.0 329.6 jit_solution(1134401229598648105)
XLA Ops:
  6.5 0.7 all-gather.3.cloned.1.call-update
  7.3 0.7 all-gather.5.cloned.1.call-update
  8.1 4.2 %copy.44 = bf16[384,3200]{0,1:T(8,128)(2,1)S(1)} copy(bf16[384,3200]{1,0:T(8,128)(2,1)} %param.10) | data formatting | bytes 4915200 | tf_op args[0]
  12.3 0.2 reduce-window.7
  12.6 0.6 multiply_reduce_fusion
  13.4 141.7 %all-gather.3.cloned.1.call-done = bf16[3200,1536]{1,0:T(8,128)(2,1)} async-done(((bf16[400,1536]{1,0:T(8,128)(2,1)}), bf16[3200,1536]{1,0:T(8,128)(2,1)}) %all-gather.3.cloned.1.call-update) | async-done | bytes 9830416 | tf_op jit(solution)/shard_map/all_gather | solution.py:67
  155.1 8.4 %fusion.7 = f32[384,1536]{0,1:T(8,128)S(1)} fusion(bf16[3200,1536]{1,0:T(8,128)(2,1)} %all-gather.3.cloned.1.call-done, f32[3200]{0:T(1024)S(1)} %copy-done.8, f32[384]{0:T(512)S(1)} %add_rsqrt_fusion.3, bf16[384,3200]{0,1:T(8,128)(2,1)S(1)} %copy.44), kind=kOutput, calls=%fused_computation.15 | convolution fusion | flops 3779788800 | bytes 14661632 | tf_op jit(solution)/shard_map/dot_general | solution.py:66
  163.6 1.4 copy-done
  165.1 6.6 %all-reduce.1 = (f32[384]{0:T(512)S(1)}, f32[384]{0:T(512)S(1)}) all-reduce(f32[384]{0:T(512)S(1)} %get-tuple-element.6, f32[384]{0:T(512)S(1)} %get-tuple-element.5), channel_id=1, replica_groups=mesh['req'=8,'tp'=4] {'tp'}, use_global_device_ids=true, to_apply=%region_9.10 | all-reduce | flops 768 | bytes 6144 | tf_op jit(solution)/shard_map/psum | solution.py:77
  171.7 3.7 %fusion.15 = f32[4,384,384]{1,2,0:T(8,128)S(1)} fusion(f32[384,4,3,128]{0,3,2,1:T(8,128)} %bitcast.110, f32[4,128]{1,0:T(4,128)S(1)} %bitcast.112, f32[384]{0:T(512)S(1)} %get-tuple-element.25, f32[4,128]{1,0:T(4,128)S(1)} %bitcast.113, f32[384]{0:T(512)S(1)} %get-tuple-element.26), kind=kOutput, calls=%fused_computation.31 | convolution fusion | flops 906756096 | bytes 3939328 | tf_op jit(solution)/shard_map/qhd,khd->hqk/dot_general | solution.py:83
  175.4 1.4 copy-done.1
  176.7 0.8 fusion.45
  177.5 2.9 convolution_convert_fusion.1
  180.4 37.1 %all-gather.5.cloned.1.call-done = bf16[512,3200]{0,1:T(8,128)(2,1)} async-done(((bf16[512,400]{0,1:T(8,128)(2,1)}), bf16[512,3200]{0,1:T(8,128)(2,1)}) %all-gather.5.cloned.1.call-update) | async-done | bytes 3276816 | tf_op jit(solution)/shard_map/all_gather | solution.py:95
  217.5 5.3 %convolution_convert_fusion = bf16[384,3200]{0,1:T(8,128)(2,1)} fusion(bf16[512,3200]{0,1:T(8,128)(2,1)} %all-gather.5.cloned.1.call-done, bf16[384,512]{0,1:T(8,128)(2,1)S(1)} %bitcast.116), kind=kOutput, calls=%fused_computation.3 | convolution fusion | flops 1259520000 | bytes 6127616 | tf_op jit(solution)/shard_map/dot_general | solution.py:93
  222.9 0.5 copy-done.4
  223.5 0.7 copy.43
  224.2 3.4 %all-to-all-start = ((s32[8,1,1]{2,1,0:T(1,128)}), s32[8,1,1]{2,1,0:T(1,128)S(1)}, u32[]{:S(2)}, u32[]{:S(2)}) async-start(s32[8,1,1]{2,1,0:T(1,128)} %copy.43), calls=%async_computation | async-start | bytes 8192 | tf_op jit(solution)/shard_map/all_to_all | solution.py:115
  227.7 2.6 convert_element_type.50
  230.9 24.3 %reduce-scatter.2.cloned.1.call-done = bf16[384,800]{0,1:T(8,128)(2,1)} async-done(((bf16[384,3200]{0,1:T(8,128)(2,1)}), bf16[384,800]{0,1:T(8,128)(2,1)}) %reduce-scatter.2.cloned.1.call-update) | async-done | bytes 614416 | tf_op jit(solution)/shard_map/reduce_scatter | solution.py:98
  255.3 1.6 add_convert_fusion
  256.9 0.4 copy.51
  257.2 2.3 gather_fusion
  259.7 0.4 broadcast_select_fusion
  260.1 1.4 broadcast_in_dim.55
  261.5 12.7 %scatter_fusion = bf16[8,24,4,800]{3,2,1,0:T(4,128)(2,1)} fusion(bf16[8,24,4,800]{3,2,1,0:T(4,128)(2,1)} %broadcast_in_dim.55, s32[96]{0:T(128)S(1)} %fusion.36, bf16[96,4,800]{2,1,0:T(4,128)(2,1)S(1)} %broadcast_select_fusion), kind=kCustom, calls=%fused_computation.1 | custom fusion | bytes 1843968 | tf_op jit(solution)/shard_map/scatter | solution.py:107
  274.2 5.7 %all-to-all-start.1 = ((bf16[8,24,4,800]{3,2,1,0:T(4,128)(2,1)}), bf16[8,24,4,800]{3,2,1,0:T(4,128)(2,1)S(1)}, u32[]{:S(2)}, u32[]{:S(2)}) async-start(bf16[8,24,4,800]{3,2,1,0:T(4,128)(2,1)} %scatter_fusion), calls=%async_computation.2 | async-start | bytes 2752512 | tf_op jit(solution)/shard_map/all_to_all | solution.py:114
  279.8 0.2 reduce
  280.2 32.5 %all-to-all-done.1 = bf16[8,24,4,800]{3,2,1,0:T(4,128)(2,1)S(1)} async-done(((bf16[8,24,4,800]{3,2,1,0:T(4,128)(2,1)}), bf16[8,24,4,800]{3,2,1,0:T(4,128)(2,1)S(1)}, u32[]{:S(2)}, u32[]{:S(2)}) %all-to-all-start.1) | async-done | bytes 1228832 | tf_op jit(solution)/shard_map/all_to_all | solution.py:114
  312.6 1.9 convert_reduce_fusion
  314.5 6.1 %all-reduce = (f32[8,24]{1,0:T(8,128)S(1)}, f32[8,24]{1,0:T(8,128)S(1)}) all-reduce(f32[8,24]{1,0:T(8,128)S(1)} %get-tuple-element.8, f32[8,24]{1,0:T(8,128)S(1)} %get-tuple-element.7), channel_id=1, replica_groups=mesh['req'=8,'tp'=4] {'tp'}, use_global_device_ids=true, to_apply=%region_19.20 | all-reduce | flops 384 | bytes 3072 | tf_op jit(solution)/shard_map/psum | solution.py:121
  320.6 2.4 fusion.5
  (41 shorter events, 1.6 us)
Async XLA Ops:
  6.5 148.6 %all-gather.3.cloned.1.call-start = ((), (), s32[]{:S(2)}) async-start(), calls=%async_computation.3 | async-start | bytes 11059200 | tf_op jit(solution)/shard_map/all_gather | solution.py:67
  7.3 210.2 %all-gather.5.cloned.1.call-start = ((), (), s32[]{:S(2)}) async-start(), calls=%async_computation.4 | async-start | bytes 3686400 | tf_op jit(solution)/shard_map/all_gather | solution.py:95
  8.0 4.3 %copy-start.5 = (s32[3,2]{0,1:T(2,128)S(1)}, s32[3,2]{0,1:T(2,128)}, u32[]{:S(2)}) copy-start(s32[3,2]{0,1:T(2,128)} %param.16) | copy-start | bytes 76
  8.0 247.2 %reduce-scatter.2.cloned.1.call-start = ((), (), s32[]{:S(2)}) async-start(), calls=%async_computation.5 | async-start | bytes 3072000 | tf_op jit(solution)/shard_map/reduce_scatter | solution.py:98
  12.3 142.8 %copy-start.8 = (f32[3200]{0:T(1024)S(1)}, f32[3200]{0:T(1024)}, u32[]{:S(2)}) copy-start(f32[3200]{0:T(1024)} %param.11) | copy-start | bytes 38404
  13.4 158.3 %copy-start.6 = (f32[512]{0:T(512)S(1)}, f32[512]{0:T(512)}, u32[]{:S(2)}) copy-start(f32[512]{0:T(512)} %param.14) | copy-start | bytes 6148
  13.4 158.3 %copy-start.7 = (f32[512]{0:T(512)S(1)}, f32[512]{0:T(512)}, u32[]{:S(2)}) copy-start(f32[512]{0:T(512)} %param.13) | copy-start | bytes 6148
  163.6 1.4 copy-start
  175.4 1.4 copy-start.1
  222.8 0.7 copy-start.4
  224.2 50.0 %all-to-all-start = ((s32[8,1,1]{2,1,0:T(1,128)}), s32[8,1,1]{2,1,0:T(1,128)S(1)}, u32[]{:S(2)}, u32[]{:S(2)}) async-start(s32[8,1,1]{2,1,0:T(1,128)} %copy.43), calls=%async_computation | async-start | bytes 8192 | tf_op jit(solution)/shard_map/all_to_all | solution.py:115
  274.2 46.4 %copy-start.2 = (f32[4,800]{1,0:T(4,128)S(1)}, f32[4,800]{1,0:T(4,128)}, u32[]{:S(2)}) copy-start(f32[4,800]{1,0:T(4,128)} %param.19) | copy-start | bytes 38404
  274.2 46.4 %copy-start.3 = (f32[4,800]{1,0:T(4,128)S(1)}, f32[4,800]{1,0:T(4,128)}, u32[]{:S(2)}) copy-start(f32[4,800]{1,0:T(4,128)} %param.18) | copy-start | bytes 38404
  274.2 38.4 %all-to-all-start.1 = ((bf16[8,24,4,800]{3,2,1,0:T(4,128)(2,1)}), bf16[8,24,4,800]{3,2,1,0:T(4,128)(2,1)S(1)}, u32[]{:S(2)}, u32[]{:S(2)}) async-start(bf16[8,24,4,800]{3,2,1,0:T(4,128)(2,1)} %scatter_fusion), calls=%async_computation.2 | async-start | bytes 2752512 | tf_op jit(solution)/shard_map/all_to_all | solution.py:114
Sparse Core Ops, SparseCore 0:
  9.5 145.5 all-gather.2
  157.3 60.1 all-gather.4
  222.9 32.2 reduce-scatter.1
where the time goes:
time: 330 us
  waiting for transfers between devices  237 us (72%)
  local copies, waits for them, and re-layouts  25.4 us (8%)
  matrix products  20.3 us (6%)
  between operations  13.3 us (4%)
  blocking collectives  12.6 us (4%)
  other arithmetic  11.8 us (4%)
  starting transfers between devices  9.14 us (3%)
    all_gather x1, waiting for transfers between devices, body(): lax.all_gather(w_qkv, 'req', axis=0, tiled=True)  142 us
    all_gather x1, waiting for transfers between devices, body(): lax.all_gather(w_out, 'req', axis=1, tiled=True)  37.1 us
    all_to_all x1, waiting for transfers between devices, body(): lax.all_to_all(send_slots, 'req', split_axis=0, concat_axis=0, tiled=True)  32.5 us
    reduce_scatter x1, waiting for transfers between devices, body(): lax.psum_scatter(partial_sum.astype(jnp.bfloat16), 'tp', scatter_dimensio...  24.3 us
    scatter x1, local copies, waits for them, and re-layouts, body(): send_slots = send_slots.at[target_owner, ranks].set(merged, mode='drop')  12.7 us
    dot_general x1, matrix products, body(): jnp.dot(normed, lax.all_gather(w_qkv, 'req', axis=0, tiled=True), preferr...  8.42 us
    unnamed x19, local copies, waits for them, and re-layouts  7.58 us
  transfers between devices with their start and end apart: 5, of which 4 were waited for; matrix products, arithmetic and copies ran while one was open for 14% of the time, Pallas kernels for 0%

commit v1 on v0

v1 whole, which is shorter than its diff:
```python
import math

import jax
import jax.numpy as jnp
from jax import lax
from jax.sharding import PartitionSpec as P

D = 3200
HEADS = 16
HEAD_DIM = 128
BF16 = jnp.bfloat16
F32 = jnp.float32


def merge_layout(grid, token_count, slot_count):
    half_rows = grid[:, 0]
    half_cols = grid[:, 1]
    image_slots = half_rows * half_cols
    slot_ends = jnp.cumsum(image_slots)
    slot_starts = slot_ends - image_slots
    slot_ids = jnp.arange(slot_count, dtype=jnp.int32)
    image_ids = jnp.sum((slot_ids[:, None] >= slot_ends[None, :]).astype(jnp.int32), axis=1)
    image_count = grid.shape[0]
    is_live = image_ids < image_count
    one_hot = (image_ids[:, None] == jnp.arange(image_count, dtype=jnp.int32)[None, :]).astype(
        jnp.int32
    )
    cols_here = jnp.maximum(jnp.sum(one_hot * half_cols[None, :], axis=1), 1)
    start_here = jnp.sum(one_hot * slot_starts[None, :], axis=1)
    offset = slot_ids - start_here
    row_half = offset // cols_here
    col_half = offset % cols_here
    first_row = 4 * start_here + 4 * row_half * cols_here + 2 * col_half
    patch_rows = jnp.stack(
        [first_row, first_row + 1, first_row + 2 * cols_here, first_row + 2 * cols_here + 1], axis=1
    )
    patch_rows = jnp.where(is_live[:, None], patch_rows, 0)
    token_ids = jnp.arange(token_count, dtype=jnp.int32)
    segment = jnp.sum((token_ids[:, None] >= 4 * slot_ends[None, :]).astype(jnp.int32), axis=1)
    return (patch_rows, is_live, segment)


def owner_ranks(owner_ids, is_live):
    slot_ids = jnp.arange(owner_ids.shape[0], dtype=jnp.int32)
    earlier = (
        (owner_ids[:, None] == owner_ids[None, :])
        & (slot_ids[None, :] < slot_ids[:, None])
        & is_live[None, :]
    )
    return jnp.sum(earlier.astype(jnp.int32), axis=1)


def dest_tokens(patch_rows, is_live, owners, capacity, devices_req):
    ranks = owner_ranks(owners, is_live)
    target = jnp.where(is_live, owners * capacity + ranks, -1)
    rows = jnp.arange(devices_req * capacity, dtype=jnp.int32)
    hit = (target[None, :] == rows[:, None]).astype(jnp.int32)
    return jnp.sum(hit[:, :, None] * (patch_rows[None] + 1), axis=1) - 1


def swap(value, axis, bit):
    count = lax.axis_size(axis)
    return lax.ppermute(value, axis, [(i, i ^ bit) for i in range(count)])


def ring(value):
    count = lax.axis_size("req")
    return lax.ppermute(value, "req", [(i, (i + 2) % count) for i in range(count)])


def after(value, *first):
    return lax.optimization_barrier((value,) + first)[0]


def body(tokens, norm_gain, w_qkv, q_gain, k_gain, w_out, grids, owners, proj_gain, proj_bias):
    token_count = tokens.shape[0]
    slot_count = owners.shape[0]
    quarter = proj_gain.shape[1]
    head_share = q_gain.shape[0]
    head_count = head_share // HEAD_DIM
    head_width = HEADS * HEAD_DIM
    score_scale = 1.0 / math.sqrt(HEAD_DIM)
    feature_total = 4 * D
    devices_req = lax.axis_size("req")
    devices_tp = lax.axis_size("tp")
    depth = w_qkv.shape[0]
    planes = devices_req // 2
    use_ring = planes == devices_tp
    capacity = max(2, (2 * slot_count + devices_req - 1) // devices_req)
    me = lax.axis_index("req")
    plane, side = me // 2, me % 2
    column = lax.axis_index("tp")

    w_parts = w_qkv.reshape(depth, head_count, 3, HEAD_DIM)
    w_q, w_k, w_v = (w_parts[:, :, i].reshape(depth, head_share) for i in range(3))
    w_o = w_out.T
    if use_ring:
        q_blocks, k_blocks, v_blocks, o_blocks = [w_q], [w_k], [w_v], [w_o]
        for step in range(1, planes):
            q_blocks.append(ring(q_blocks[-1]))
            k_blocks.append(ring(k_blocks[-1]))
        v_blocks[0] = after(w_v, q_blocks[2])
        o_blocks[0] = after(w_o, k_blocks[2])
        for step in range(1, planes):
            v_blocks.append(ring(v_blocks[-1]))
            o_blocks.append(ring(o_blocks[-1]))

    patch_rows, is_live, segment = merge_layout(grids, token_count, slot_count)
    row_tokens = dest_tokens(patch_rows, is_live, owners, capacity, devices_req)
    token_float = tokens.astype(F32)
    mean_square = jnp.mean(token_float * token_float, axis=1, keepdims=True)
    normed = (token_float * lax.rsqrt(mean_square + 1e-06) * norm_gain).astype(BF16)

    by_side = normed.reshape(token_count, planes, 2, depth)
    mine = lax.dynamic_index_in_dim(by_side, side, 2, keepdims=False)
    others = lax.dynamic_index_in_dim(by_side, 1 - side, 2, keepdims=False)
    theirs = swap(others.reshape(token_count, planes * depth), "req", 1)
    both = jnp.concatenate([mine.reshape(token_count, planes * depth), theirs], axis=0)

    if use_ring:
        both_blocks = both.reshape(2 * token_count, planes, depth).transpose(1, 0, 2)

        def project(blocks):
            total = None
            for step, block in enumerate(blocks):
                rows = lax.dynamic_index_in_dim(
                    both_blocks, (plane + planes - step) % planes, 0, keepdims=False
                )
                term = jnp.dot(rows, block, preferred_element_type=F32)
                total = term if total is None else total + term
            return total
    else:
        groups = [list(range(i, devices_req, 2)) for i in range(2)]

        def project(block):
            whole = lax.all_gather(block, "req", axis=0, tiled=True, axis_index_groups=groups)
            return jnp.dot(both, whole, preferred_element_type=F32)

        q_blocks, k_blocks, v_blocks = w_q, w_k, w_v

    def projected(blocks):
        total = project(blocks)
        return total[:token_count] + swap(total[token_count:].astype(BF16), "req", 1).astype(F32)

    queries = projected(q_blocks)
    key_vecs = projected(k_blocks)
    values = projected(v_blocks).astype(BF16).reshape(token_count, head_count, HEAD_DIM)
    local_q = jnp.sum(queries * queries, axis=1)
    local_k = jnp.sum(key_vecs * key_vecs, axis=1)
    q_total, k_total = lax.psum((local_q, local_k), "tp")
    q_scale = lax.rsqrt(q_total / head_width + 1e-06)
    k_scale = lax.rsqrt(k_total / head_width + 1e-06)
    q_normed = (queries * q_scale[:, None] * q_gain).reshape(token_count, head_count, HEAD_DIM)
    k_normed = (key_vecs * k_scale[:, None] * k_gain).reshape(token_count, head_count, HEAD_DIM)
    scores = (
        jnp.einsum("qhd,khd->hqk", q_normed, k_normed, precision=lax.Precision.HIGHEST)
        * score_scale
    )
    same_image = segment[:, None] == segment[None, :]
    scores = jnp.where(same_image[None], scores, -1e30)
    row_top = jnp.max(scores, axis=2, keepdims=True)
    weights_raw = jnp.exp(scores - row_top)
    probs = (weights_raw / jnp.sum(weights_raw, axis=2, keepdims=True)).astype(BF16)
    attended = jnp.einsum("hqk,khd->qhd", probs, values, preferred_element_type=F32)
    attended = attended.astype(BF16).reshape(token_count, head_share)

    contract_last = (((1,), (1,)), ((), ()))
    if use_ring:
        terms = []
        for block in o_blocks:
            peer = swap(block, "req", 1)
            low = jnp.where(side == 0, block, peer)
            high = jnp.where(side == 0, peer, block)
            pair = jnp.concatenate([low, high], axis=0)
            terms.append(
                lax.dot_general(attended, pair, contract_last, preferred_element_type=F32)
            )
        terms = jnp.stack(terms).astype(BF16)

        def term_of(index):
            return lax.dynamic_index_in_dim(
                terms, (plane + planes - index) % planes, 0, keepdims=False
            )
    else:
        whole = lax.all_gather(w_o, "req", axis=0, tiled=True)
        terms = lax.dot_general(attended, whole, contract_last, preferred_element_type=F32)
        terms = terms.astype(BF16).reshape(token_count, devices_tp, quarter).transpose(1, 0, 2)

        def term_of(index):
            return lax.dynamic_index_in_dim(terms, index, 0, keepdims=False)

    far = column ^ 2
    sent = jnp.stack([term_of(column ^ 1), term_of(far ^ 1)])
    got = swap(sent, "tp", 1).astype(F32)
    mine_near = term_of(column).astype(F32) + got[0]
    mine_far = term_of(far).astype(F32) + got[1]
    attn_out = mine_near + swap(mine_far.astype(BF16), "tp", 2).astype(F32)

    token_mine = lax.dynamic_slice_in_dim(tokens, column * quarter, quarter, 1).astype(F32)
    hidden = (token_mine + attn_out).astype(BF16)

    token_ids = jnp.arange(token_count, dtype=jnp.int32)
    chosen = row_tokens.reshape(-1)[:, None] == token_ids[None, :]
    packed = jnp.dot(chosen.astype(BF16), hidden, preferred_element_type=F32).astype(BF16)
    packed = packed.reshape(devices_req, capacity * 4, quarter)
    arrived = lax.all_to_all(packed, "req", split_axis=0, concat_axis=0, tiled=True)

    hidden_float = hidden.astype(F32)
    token_sums = jnp.stack(
        [jnp.sum(hidden_float, axis=1), jnp.sum(hidden_float * hidden_float, axis=1)]
    )
    token_sums = lax.psum(token_sums, "tp")
    in_row = jnp.any(row_tokens[:, :, None] == token_ids[None, None, :], axis=1)
    row_sums = jnp.sum(jnp.where(in_row[None], token_sums[:, None, :], 0.0), axis=2)
    mean_value = row_sums[0] / feature_total
    variance = row_sums[1] / feature_total - mean_value * mean_value
    row_live = (row_tokens[:, 0] >= 0).astype(F32)
    inverse = lax.rsqrt(variance + 1e-05) * row_live
    stats = jnp.stack([inverse, -mean_value * inverse, row_live]).reshape(3, devices_req, capacity)
    stats = lax.all_to_all(stats, "req", split_axis=1, concat_axis=1, tiled=True)
    stats = stats.reshape(3, devices_req * capacity, 1, 1)

    arrived = arrived.reshape(devices_req * capacity, 4, quarter).astype(F32)
    result = (arrived * stats[0] + stats[1]) * proj_gain + stats[2] * proj_bias
    return result.astype(BF16)


def solution(mesh):
    placed = (
        P("req", None),
        P(),
        P("req", "tp"),
        P("tp"),
        P("tp"),
        P("tp", "req"),
        P("req", None),
        P("req"),
        P(None, "tp"),
        P(None, "tp"),
    )
    return jax.shard_map(
        body, mesh=mesh, in_specs=placed, out_specs=P("req", None, "tp"), check_vma=False
    )
```

time: 330 us -> 258 us (0.78)
  waiting for transfers between devices: 237 us -> 125 us
  starting transfers between devices: 9.14 us -> 28.5 us
  other arithmetic: 11.8 us -> 28.2 us
  between operations: 13.3 us -> 0.58 us
  local copies, waits for them, and re-layouts: 25.4 us -> 37.5 us
  matrix products: 20.3 us -> 25.3 us
    all_gather x2 -> x0, waiting for transfers between devices: 179 us -> none  [the longest x1 142 us: body(): lax.all_gather(w_qkv, 'req', axis=0, tiled=True)]
    ppermute x0 -> x22, waiting for transfers between devices: none -> 90.4 us  [the longest x12 67.5 us: ring(): lax.ppermute(value, 'req', [(i, (i + 2) % count) for i in range(count)])]
    reduce_scatter x1 -> x0, waiting for transfers between devices: 24.3 us -> none  [body(): lax.psum_scatter(partial_sum.astype(jnp.bfloat16), 'tp', scatter_dimensio...]
    ppermute x0 -> x22, starting transfers between devices: none -> 18.6 us  [the longest x10 10.1 us: swap(): return lax.ppermute(value, axis, [(i, i ^ bit) for i in range(count)])]
    scatter x1 -> x0, local copies, waits for them, and re-layouts: 12.7 us -> none  [body(): send_slots = send_slots.at[target_owner, ranks].set(merged, mode='drop')]
    slice x0 -> x5, local copies, waits for them, and re-layouts: none -> 11.1 us  [the longest x1 10.9 us: body(): w_parts[:, :, i].reshape(depth, head_share)]
    dot_general x3 -> x18, matrix products: 16.6 us -> 23.3 us  [the longest x12 14.1 us: project(): term = jnp.dot(rows, block, preferred_element_type=F32)]
    select_n x2 -> x5, other arithmetic: 0.4 us -> 5.13 us  [the longest x4 5.12 us: body(): low = jnp.where(side == 0, block, peer)]
  transfers between devices with their start and end apart: 5 -> 24, of which waited for: 4 -> 13; matrix products, arithmetic and copies ran while one was open for 14% -> 23% of each run, Pallas kernels for 0% -> 0%
where the time goes in v1:
time: 258 us; the launch traced here: 257 us
  waiting for transfers between devices  125 us (48%)
  local copies, waits for them, and re-layouts  37.5 us (15%)
  starting transfers between devices  28.5 us (11%)
  other arithmetic  28.2 us (11%)
  matrix products  25.3 us (10%)
  blocking collectives  12.2 us (5%)
    ppermute x12, waiting for transfers between devices, ring(): lax.ppermute(value, 'req', [(i, (i + 2) % count) for i in range(count)])  67.5 us
    all_to_all x1, waiting for transfers between devices, body(): lax.all_to_all(packed, 'req', split_axis=0, concat_axis=0, tiled=True)  31.3 us
    ppermute x10, waiting for transfers between devices, swap(): return lax.ppermute(value, axis, [(i, i ^ bit) for i in range(count)])  22.9 us
    dot_general x12, matrix products, project(): term = jnp.dot(rows, block, preferred_element_type=F32)  14.1 us
    unnamed x60, local copies, waits for them, and re-layouts  12.1 us
    slice x1, local copies, waits for them, and re-layouts, body(): w_parts[:, :, i].reshape(depth, head_share)  10.9 us
    ppermute x10, starting transfers between devices, swap(): return lax.ppermute(value, axis, [(i, i ^ bit) for i in range(count)])  10.1 us
    ppermute x12, starting transfers between devices, ring(): lax.ppermute(value, 'req', [(i, (i + 2) % count) for i in range(count)])  8.45 us
  transfers between devices with their start and end apart: 24, of which 13 were waited for; matrix products, arithmetic and copies ran while one was open for 23% of the time, Pallas kernels for 0%

profile of v1, /device:TPU:0, one launch (start us, length us, event | category | flops | bytes accessed | tf_op | source)
XLA Modules:
  0.0 257.0 jit_solution(13142753643494620086)
XLA Ops:
  0.0 4.2 %copy.37 = bf16[384,3200]{0,1:T(8,128)(2,1)S(1)} copy(bf16[384,3200]{1,0:T(8,128)(2,1)} %param.10) | data formatting | bytes 4915200 | tf_op args[0]
  4.9 2.5 fusion.3
  7.4 3.4 %constant_dynamic-slice_fusion.2 = (bf16[384,4,1,400]{0,3,2,1:T(8,128)(2,1)}, bf16[384,4,400]{0,2,1:T(8,128)(2,1)}) fusion(bf16[384,4,2,400]{0,3,2,1:T(8,128)(2,1)} %bitcast.128, s32[]{:T(128)S(6)} %select_n.261, s32[]{:T(128)S(6)} %select_n.260), kind=kLoop, calls=%fused_computation.116 | loop fusion | bytes 4915208 | tf_op jit(solution)/shard_map/jit(dynamic_index_in_dim)/dynamic_slice | solution.py:116
  10.8 3.0 %collective-permute-start = (bf16[384,1600]{0,1:T(8,128)(2,1)}, bf16[384,1600]{0,1:T(8,128)(2,1)}, u32[]{:S(2)}, u32[]{:S(2)}) collective-permute-start(bf16[384,1600]{0,1:T(8,128)(2,1)} %bitcast.7), channel_id=1, source_target_pairs={{0,4},{4,0},{8,12},{12,8},{16,20},{20,16},{24,28},{28,24},{1,5},{5... | collective-permute-start | bytes 3686408 | tf_op jit(solution)/shard_map/ppermute | solution.py:63
  13.7 4.7 %reshape.398 = bf16[400,4,3,128]{3,2,1,0:T(4,128)(2,1)} reshape(bf16[400,1536]{1,0:T(8,128)(2,1)} %param.12) | data formatting | bytes 2457600 | tf_op jit(solution)/shard_map/reshape | solution.py:94
  18.4 10.9 %slice_reduce_fusion.2 = (bf16[400,4,128]{2,1,0:T(4,128)(2,1)S(1)}, bf16[400,4,128]{2,1,0:T(4,128)(2,1)S(1)}, bf16[400,4,128]{2,1,0:T(4,128)(2,1)}) fusion(bf16[400,4,3,128]{3,2,1,0:T(4,128)(2,1)} %reshape.398), kind=kLoop, calls=%fused_computation.53 | loop fusion | bytes 2457600 | tf_op jit(solution)/shard_map/slice | solution.py:95
  36.1 8.5 %collective-permute-done.1 = bf16[400,512]{1,0:T(8,128)(2,1)} collective-permute-done((bf16[400,512]{1,0:T(8,128)(2,1)}, bf16[400,512]{1,0:T(8,128)(2,1)}, u32[]{:S(2)}, u32[]{:S(2)}) %collective-permute-start.1) | collective-permute-done | bytes 409632 | tf_op jit(solution)/shard_map/ppermute | solution.py:68
  44.6 8.8 %collective-permute-done.9 = bf16[400,512]{1,0:T(8,128)(2,1)} collective-permute-done((bf16[400,512]{1,0:T(8,128)(2,1)}, bf16[400,512]{1,0:T(8,128)(2,1)}, u32[]{:S(2)}, u32[]{:S(2)}) %collective-permute-start.9) | collective-permute-done | bytes 409632 | tf_op jit(solution)/shard_map/ppermute | solution.py:68
  54.4 15.1 %collective-permute-done.10 = bf16[400,512]{1,0:T(8,128)(2,1)S(1)} collective-permute-done((bf16[400,512]{1,0:T(8,128)(2,1)}, bf16[400,512]{1,0:T(8,128)(2,1)S(1)}, u32[]{:S(2)}, u32[]{:S(2)}) %collective-permute-start.10) | collective-permute-done | bytes 409632 | tf_op jit(solution)/shard_map/ppermute | solution.py:68
  72.8 2.1 collective-permute-start.11
  82.1 19.3 %collective-permute-done.7 = bf16[400,512]{1,0:T(8,128)(2,1)S(1)} collective-permute-done((bf16[400,512]{1,0:T(8,128)(2,1)S(1)}, bf16[400,512]{1,0:T(8,128)(2,1)S(1)}, u32[]{:S(2)}, u32[]{:S(2)}) %collective-permute-start.7) | collective-permute-done | bytes 409632 | tf_op jit(solution)/shard_map/ppermute | solution.py:68
  105.0 2.9 %collective-permute-done.11 = bf16[400,512]{1,0:T(8,128)(2,1)S(1)} collective-permute-done((bf16[400,512]{1,0:T(8,128)(2,1)S(1)}, bf16[400,512]{1,0:T(8,128)(2,1)S(1)}, u32[]{:S(2)}, u32[]{:S(2)}) %collective-permute-start.11) | collective-permute-done | bytes 409632 | tf_op jit(solution)/shard_map/ppermute | solution.py:68
  109.5 2.8 %fusion.71 = f32[768,512]{0,1:T(8,128)} fusion(bf16[768,400]{0,1:T(8,128)(2,1)S(1)} %get-tuple-element.32, bf16[400,512]{1,0:T(8,128)(2,1)} %collective-permute-done.3), kind=kOutput, calls=%fused_computation.170 | convolution fusion | flops 314572800 | bytes 2596864 | tf_op jit(solution)/shard_map/dot_general | solution.py:129
  114.7 6.0 %collective-permute-done.12 = bf16[384,512]{0,1:T(8,128)(2,1)S(1)} collective-permute-done((bf16[384,512]{0,1:T(8,128)(2,1)S(1)}, bf16[384,512]{0,1:T(8,128)(2,1)S(1)}, u32[]{:S(2)}, u32[]{:S(2)}) %collective-permute-start.12) | collective-permute-done | bytes 393248 | tf_op jit(solution)/shard_map/ppermute | solution.py:63
  121.6 6.1 %all-reduce = (f32[384]{0:T(512)S(1)}, f32[384]{0:T(512)S(1)}) all-reduce(f32[384]{0:T(512)S(1)} %multiply_reduce_fusion.1, f32[384]{0:T(512)S(1)} %multiply_reduce_fusion), channel_id=1, replica_groups=mesh['req'=8,'tp'=4] {'tp'}, use_global_device_ids=true, to_apply=%region_9.10 | all-reduce | flops 768 | bytes 6144 | tf_op jit(solution)/shard_map/psum | solution.py:150
  129.5 2.1 fusion.77
  136.7 9.4 %collective-permute-done.5 = bf16[400,512]{1,0:T(8,128)(2,1)S(1)} collective-permute-done((bf16[400,512]{1,0:T(8,128)(2,1)}, bf16[400,512]{1,0:T(8,128)(2,1)S(1)}, u32[]{:S(2)}, u32[]{:S(2)}) %collective-permute-start.5) | collective-permute-done | bytes 409632 | tf_op jit(solution)/shard_map/ppermute | solution.py:68
  147.7 2.1 broadcast_select_fusion.5
  149.7 3.6 %collective-permute-done.18 = bf16[400,512]{1,0:T(8,128)(2,1)S(1)} collective-permute-done((bf16[400,512]{1,0:T(8,128)(2,1)}, bf16[400,512]{1,0:T(8,128)(2,1)S(1)}, u32[]{:S(2)}, u32[]{:S(2)}) %collective-permute-start.18) | collective-permute-done | bytes 409632 | tf_op jit(solution)/shard_map/ppermute | solution.py:68
  157.2 3.5 %convolution_convert_fusion.5 = bf16[4,128,384]{2,1,0:T(8,128)(2,1)} fusion(bf16[384,4,128]{0,2,1:T(8,128)(2,1)} %bitcast.141, f32[4,384]{1,0:T(4,128)S(1)} %fusion.69, f32[4,384,384]{1,2,0:T(8,128)} %copy-done.10, pred[384,384]{0,1:T(8,128)(4,1)S(1)} %copy-done.19), kind=kOutput, calls=%fused_computation.34 | convolution fusion | flops 154142592 | bytes 3299328 | tf_op jit(solution)/shard_map/hqk,khd->qhd/dot_general | solution.py:164
  168.7 2.8 %collective-permute-done.20 = bf16[2,384,800]{1,2,0:T(8,128)(2,1)} collective-permute-done((bf16[2,384,800]{1,2,0:T(8,128)(2,1)}, bf16[2,384,800]{1,2,0:T(8,128)(2,1)}, u32[]{:S(2)}, u32[]{:S(2)}) %collective-permute-start.20) | collective-permute-done | bytes 1228832 | tf_op jit(solution)/shard_map/ppermute | solution.py:63
  171.4 2.9 %convert_element_type.119 = f32[2,384,800]{1,2,0:T(8,128)} convert(bf16[2,384,800]{1,2,0:T(8,128)(2,1)} %collective-permute-done.20) | non-fusion elementwise | flops 614400 | bytes 3686400 | tf_op jit(solution)/shard_map/convert_element_type | solution.py:194
  174.3 2.4 fusion.32
  179.0 13.8 %collective-permute-done.21 = bf16[384,800]{0,1:T(8,128)(2,1)S(1)} collective-permute-done((bf16[384,800]{0,1:T(8,128)(2,1)}, bf16[384,800]{0,1:T(8,128)(2,1)S(1)}, u32[]{:S(2)}, u32[]{:S(2)}) %collective-permute-start.21) | collective-permute-done | bytes 614432 | tf_op jit(solution)/shard_map/ppermute | solution.py:63
  192.8 2.7 %convert_reduce_fusion = (f32[384]{0:T(512)S(1)}, f32[384]{0:T(512)S(1)}, bf16[384,800]{0,1:T(8,128)(2,1)}) fusion(bf16[384,800]{0,1:T(8,128)(2,1)S(1)} %collective-permute-done.21, f32[2,384,800]{1,2,0:T(8,128)} %convert_element_type.119, bf16[4,384,800]{1,2,0:T(8,128)(2,1)} %copy-done, s32[]{:T(128)S(6)} %select_n.282, bf16[384,3200]{0,1:T(8,128)(2,1)S(1)} %copy.37, ...), kind=kLoop, calls=%fused_computation.25 | loop fusion | flops 3378432 | bytes 3689480 | tf_op jit(solution)/shard_map/reduce_sum | solution.py:210
  195.5 6.1 %psum.23 = f32[2,384]{1,0:T(2,128)S(1)} all-reduce(f32[2,384]{1,0:T(2,128)S(1)} %pad_maximum_fusion.3), channel_id=1, replica_groups=mesh['req'=8,'tp'=4] {'tp'}, use_global_device_ids=true, to_apply=%region_17.18 | all-reduce | flops 768 | bytes 6144 | tf_op jit(solution)/shard_map/psum | solution.py:212
  203.9 5.7 %all-to-all-start.1 = ((f32[3,8,24]{2,0,1:T(4,128)}), f32[3,8,24]{2,0,1:T(4,128)S(1)}, u32[]{:S(2)}, u32[]{:S(2)}) async-start(f32[3,8,24]{2,0,1:T(4,128)} %copy.43), calls=%async_computation.1 | async-start | bytes 32768 | tf_op jit(solution)/shard_map/all_to_all | solution.py:220
  213.1 3.0 %all-to-all-done.1 = f32[3,8,24]{2,0,1:T(4,128)S(1)} async-done(((f32[3,8,24]{2,0,1:T(4,128)}), f32[3,8,24]{2,0,1:T(4,128)S(1)}, u32[]{:S(2)}, u32[]{:S(2)}) %all-to-all-start.1) | async-done | bytes 2336 | tf_op jit(solution)/shard_map/all_to_all | solution.py:220
  216.1 4.3 %all-to-all-start = ((bf16[8,96,800]{2,1,0:T(8,128)(2,1)}), bf16[8,96,800]{2,1,0:T(8,128)(2,1)}, u32[]{:S(2)}, u32[]{:S(2)}) async-start(bf16[8,96,800]{2,1,0:T(8,128)(2,1)} %bitcast.26), calls=%async_computation | async-start | bytes 2752512 | tf_op jit(solution)/shard_map/all_to_all | solution.py:206
  220.7 31.3 %all-to-all-done = bf16[8,96,800]{2,1,0:T(8,128)(2,1)} async-done(((bf16[8,96,800]{2,1,0:T(8,128)(2,1)}), bf16[8,96,800]{2,1,0:T(8,128)(2,1)}, u32[]{:S(2)}, u32[]{:S(2)}) %all-to-all-start) | async-done | bytes 1228832 | tf_op jit(solution)/shard_map/all_to_all | solution.py:206
  252.0 2.7 %reshape.404 = f32[192,4,800]{2,1,0:T(4,128)S(1)} reshape(bf16[8,96,800]{2,1,0:T(8,128)(2,1)} %all-to-all-done) | data formatting | bytes 3686400 | tf_op jit(solution)/shard_map/convert_element_type | solution.py:223
  254.7 2.3 add_convert_fusion
  (162 shorter events, 55.9 us)
Async XLA Ops:
  10.8 62.1 %collective-permute-start = (bf16[384,1600]{0,1:T(8,128)(2,1)}, bf16[384,1600]{0,1:T(8,128)(2,1)}, u32[]{:S(2)}, u32[]{:S(2)}) collective-permute-start(bf16[384,1600]{0,1:T(8,128)(2,1)} %bitcast.7), channel_id=1, source_target_pairs={{0,4},{4,0},{8,12},{12,8},{16,20},{20,16},{24,28},{28,24},{1,5},{5... | collective-permute-start | bytes 3686408 | tf_op jit(solution)/shard_map/ppermute | solution.py:63
  29.3 45.7 %copy-start.8 = (bf16[400,4,128]{2,1,0:T(4,128)(2,1)}, bf16[400,4,128]{2,1,0:T(4,128)(2,1)S(1)}, u32[]{:S(2)}) copy-start(bf16[400,4,128]{2,1,0:T(4,128)(2,1)S(1)} %get-tuple-element.10) | copy-start | bytes 1228804
  30.1 14.5 %collective-permute-start.1 = (bf16[400,512]{1,0:T(8,128)(2,1)}, bf16[400,512]{1,0:T(8,128)(2,1)}, u32[]{:S(2)}, u32[]{:S(2)}) collective-permute-start(bf16[400,512]{1,0:T(8,128)(2,1)} %bitcast.125), channel_id=1, source_target_pairs={{0,8},{4,12},{8,16},{12,20},{16,24},{20,28},{24,0},{28,4},{1,9},{5... | collective-permute-start | bytes 1228808 | tf_op jit(solution)/shard_map/ppermute | solution.py:68
  32.5 20.9 %collective-permute-start.9 = (bf16[400,512]{1,0:T(8,128)(2,1)}, bf16[400,512]{1,0:T(8,128)(2,1)}, u32[]{:S(2)}, u32[]{:S(2)}) collective-permute-start(bf16[400,512]{1,0:T(8,128)(2,1)} %bitcast.127), channel_id=1, source_target_pairs={{0,8},{4,12},{8,16},{12,20},{16,24},{20,28},{24,0},{28,4},{1,9},{5... | collective-permute-start | bytes 1228808 | tf_op jit(solution)/shard_map/ppermute | solution.py:68
  44.6 25.3 %collective-permute-start.2 = (bf16[400,512]{1,0:T(8,128)(2,1)}, bf16[400,512]{1,0:T(8,128)(2,1)S(1)}, u32[]{:S(2)}, u32[]{:S(2)}) collective-permute-start(bf16[400,512]{1,0:T(8,128)(2,1)} %collective-permute-done.1), channel_id=1, source_target_pairs={{0,8},{4,12},{8,16},{12,20},{16,24},{20,28},{24,0},{28,4},{1,9},{5... | collective-permute-start | bytes 1228808 | tf_op jit(solution)/shard_map/ppermute | solution.py:68
  53.4 16.1 %collective-permute-start.10 = (bf16[400,512]{1,0:T(8,128)(2,1)}, bf16[400,512]{1,0:T(8,128)(2,1)S(1)}, u32[]{:S(2)}, u32[]{:S(2)}) collective-permute-start(bf16[400,512]{1,0:T(8,128)(2,1)} %collective-permute-done.9), channel_id=1, source_target_pairs={{0,8},{4,12},{8,16},{12,20},{16,24},{20,28},{24,0},{28,4},{1,9},{5... | collective-permute-start | bytes 1228808 | tf_op jit(solution)/shard_map/ppermute | solution.py:68
  69.5 42.8 %collective-permute-start.14 = (bf16[400,512]{1,0:T(8,128)(2,1)}, bf16[400,512]{1,0:T(8,128)(2,1)}, u32[]{:S(2)}, u32[]{:S(2)}) collective-permute-start(bf16[400,512]{1,0:T(8,128)(2,1)} %bitcast.138), channel_id=1, source_target_pairs={{0,8},{4,12},{8,16},{12,20},{16,24},{20,28},{24,0},{28,4},{1,9},{5... | collective-permute-start | bytes 1228808 | tf_op jit(solution)/shard_map/ppermute | solution.py:68
  69.5 42.8 %collective-permute-start.13 = (bf16[400,512]{1,0:T(8,128)(2,1)}, bf16[400,512]{1,0:T(8,128)(2,1)S(1)}, u32[]{:S(2)}, u32[]{:S(2)}) collective-permute-start(bf16[400,512]{1,0:T(8,128)(2,1)} %bitcast.139), channel_id=1, source_target_pairs={{0,4},{4,0},{8,12},{12,8},{16,20},{20,16},{24,28},{28,24},{1,5},{5... | collective-permute-start | bytes 1228808 | tf_op jit(solution)/shard_map/ppermute | solution.py:63
  70.0 39.5 %collective-permute-start.3 = (bf16[400,512]{1,0:T(8,128)(2,1)}, bf16[400,512]{1,0:T(8,128)(2,1)}, u32[]{:S(2)}, u32[]{:S(2)}) collective-permute-start(bf16[400,512]{1,0:T(8,128)(2,1)} %bitcast.136), channel_id=1, source_target_pairs={{0,8},{4,12},{8,16},{12,20},{16,24},{20,28},{24,0},{28,4},{1,9},{5... | collective-permute-start | bytes 1228808 | tf_op jit(solution)/shard_map/ppermute | solution.py:68
  71.3 30.2 %collective-permute-start.7 = (bf16[400,512]{1,0:T(8,128)(2,1)S(1)}, bf16[400,512]{1,0:T(8,128)(2,1)S(1)}, u32[]{:S(2)}, u32[]{:S(2)}) collective-permute-start(bf16[400,512]{1,0:T(8,128)(2,1)S(1)} %collective-permute-done.2), channel_id=1, source_target_pairs={{0,8},{4,12},{8,16},{12,20},{16,24},{20,28},{24,0},{28,4},{1,9},{5... | collective-permute-start | bytes 1228808 | tf_op jit(solution)/shard_map/ppermute | solution.py:68
  72.8 35.0 %collective-permute-start.11 = (bf16[400,512]{1,0:T(8,128)(2,1)S(1)}, bf16[400,512]{1,0:T(8,128)(2,1)S(1)}, u32[]{:S(2)}, u32[]{:S(2)}) collective-permute-start(bf16[400,512]{1,0:T(8,128)(2,1)S(1)} %collective-permute-done.10), channel_id=1, source_target_pairs={{0,8},{4,12},{8,16},{12,20},{16,24},{20,28},{24,0},{28,4},{1,9},{5... | collective-permute-start | bytes 1228808 | tf_op jit(solution)/shard_map/ppermute | solution.py:68
  76.8 31.1 %copy-start.1 = (bf16[768,400]{0,1:T(8,128)(2,1)}, bf16[768,400]{0,1:T(8,128)(2,1)S(1)}, u32[]{:S(2)}) copy-start(bf16[768,400]{0,1:T(8,128)(2,1)S(1)} %get-tuple-element.30) | copy-start | bytes 1843204
  102.1 12.5 %copy-start.3 = (f32[768,512]{0,1:T(8,128)}, f32[768,512]{0,1:T(8,128)S(1)}, u32[]{:S(2)}) copy-start(f32[768,512]{0,1:T(8,128)S(1)} %add_add_fusion.1) | copy-start | bytes 4718596
  102.2 12.4 %collective-permute-start.8 = (bf16[384,512]{0,1:T(8,128)(2,1)S(1)}, bf16[384,512]{0,1:T(8,128)(2,1)S(1)}, u32[]{:S(2)}, u32[]{:S(2)}) collective-permute-start(bf16[384,512]{0,1:T(8,128)(2,1)S(1)} %slice.154), channel_id=1, source_target_pairs={{0,4},{4,0},{8,12},{12,8},{16,20},{20,16},{24,28},{28,24},{1,5},{5... | collective-permute-start | bytes 1179656 | tf_op jit(solution)/shard_map/ppermute | solution.py:63
  108.6 12.1 %collective-permute-start.12 = (bf16[384,512]{0,1:T(8,128)(2,1)S(1)}, bf16[384,512]{0,1:T(8,128)(2,1)S(1)}, u32[]{:S(2)}, u32[]{:S(2)}) collective-permute-start(bf16[384,512]{0,1:T(8,128)(2,1)S(1)} %slice.153), channel_id=1, source_target_pairs={{0,4},{4,0},{8,12},{12,8},{16,20},{20,16},{24,28},{28,24},{1,5},{5... | collective-permute-start | bytes 1179656 | tf_op jit(solution)/shard_map/ppermute | solution.py:63
  109.5 22.2 %collective-permute-start.4 = (bf16[400,512]{1,0:T(8,128)(2,1)}, bf16[400,512]{1,0:T(8,128)(2,1)}, u32[]{:S(2)}, u32[]{:S(2)}) collective-permute-start(bf16[400,512]{1,0:T(8,128)(2,1)} %collective-permute-done.3), channel_id=1, source_target_pairs={{0,8},{4,12},{8,16},{12,20},{16,24},{20,28},{24,0},{28,4},{1,9},{5... | collective-permute-start | bytes 1228808 | tf_op jit(solution)/shard_map/ppermute | solution.py:68
  112.3 23.3 %collective-permute-start.16 = (bf16[400,512]{1,0:T(8,128)(2,1)}, bf16[400,512]{1,0:T(8,128)(2,1)}, u32[]{:S(2)}, u32[]{:S(2)}) collective-permute-start(bf16[400,512]{1,0:T(8,128)(2,1)} %collective-permute-done.14), channel_id=1, source_target_pairs={{0,8},{4,12},{8,16},{12,20},{16,24},{20,28},{24,0},{28,4},{1,9},{5... | collective-permute-start | bytes 1228808 | tf_op jit(solution)/shard_map/ppermute | solution.py:68
  112.3 35.4 %collective-permute-start.15 = (bf16[400,512]{1,0:T(8,128)(2,1)}, bf16[400,512]{1,0:T(8,128)(2,1)}, u32[]{:S(2)}, u32[]{:S(2)}) collective-permute-start(bf16[400,512]{1,0:T(8,128)(2,1)} %collective-permute-done.14), channel_id=1, source_target_pairs={{0,4},{4,0},{8,12},{12,8},{16,20},{20,16},{24,28},{28,24},{1,5},{5... | collective-permute-start | bytes 1228808 | tf_op jit(solution)/shard_map/ppermute | solution.py:63
  114.6 13.1 %copy-start.25 = (f32[512]{0:T(512)S(1)}, f32[512]{0:T(512)}, u32[]{:S(2)}) copy-start(f32[512]{0:T(512)} %param.13) | copy-start | bytes 6148
  114.7 14.4 %copy-start.26 = (f32[512]{0:T(512)S(1)}, f32[512]{0:T(512)}, u32[]{:S(2)}) copy-start(f32[512]{0:T(512)} %param.14) | copy-start | bytes 6148
  131.6 14.5 %collective-permute-start.5 = (bf16[400,512]{1,0:T(8,128)(2,1)}, bf16[400,512]{1,0:T(8,128)(2,1)S(1)}, u32[]{:S(2)}, u32[]{:S(2)}) collective-permute-start(bf16[400,512]{1,0:T(8,128)(2,1)} %collective-permute-done.4), channel_id=1, source_target_pairs={{0,8},{4,12},{8,16},{12,20},{16,24},{20,28},{24,0},{28,4},{1,9},{5... | collective-permute-start | bytes 1228808 | tf_op jit(solution)/shard_map/ppermute | solution.py:68
  133.0 13.1 %copy-start.7 = (f32[768,512]{0,1:T(8,128)S(1)}, f32[768,512]{0,1:T(8,128)}, u32[]{:S(2)}) copy-start(f32[768,512]{0,1:T(8,128)} %fusion.71) | copy-start | bytes 4718596
  135.6 17.7 %collective-permute-start.18 = (bf16[400,512]{1,0:T(8,128)(2,1)}, bf16[400,512]{1,0:T(8,128)(2,1)S(1)}, u32[]{:S(2)}, u32[]{:S(2)}) collective-permute-start(bf16[400,512]{1,0:T(8,128)(2,1)} %collective-permute-done.16), channel_id=1, source_target_pairs={{0,8},{4,12},{8,16},{12,20},{16,24},{20,28},{24,0},{28,4},{1,9},{5... | collective-permute-start | bytes 1228808 | tf_op jit(solution)/shard_map/ppermute | solution.py:68
  135.9 18.2 %collective-permute-start.17 = (bf16[400,512]{1,0:T(8,128)(2,1)}, bf16[400,512]{1,0:T(8,128)(2,1)S(1)}, u32[]{:S(2)}, u32[]{:S(2)}) collective-permute-start(bf16[400,512]{1,0:T(8,128)(2,1)} %collective-permute-done.16), channel_id=1, source_target_pairs={{0,4},{4,0},{8,12},{12,8},{16,20},{20,16},{24,28},{28,24},{1,5},{5... | collective-permute-start | bytes 1228808 | tf_op jit(solution)/shard_map/ppermute | solution.py:63
  146.8 9.5 %collective-permute-start.6 = (bf16[384,512]{0,1:T(8,128)(2,1)S(1)}, bf16[384,512]{0,1:T(8,128)(2,1)S(1)}, u32[]{:S(2)}, u32[]{:S(2)}) collective-permute-start(bf16[384,512]{0,1:T(8,128)(2,1)S(1)} %slice.155), channel_id=1, source_target_pairs={{0,4},{4,0},{8,12},{12,8},{16,20},{20,16},{24,28},{28,24},{1,5},{5... | collective-permute-start | bytes 1179656 | tf_op jit(solution)/shard_map/ppermute | solution.py:63
  153.3 11.1 %collective-permute-start.19 = (bf16[400,512]{1,0:T(8,128)(2,1)S(1)}, bf16[400,512]{1,0:T(8,128)(2,1)S(1)}, u32[]{:S(2)}, u32[]{:S(2)}) collective-permute-start(bf16[400,512]{1,0:T(8,128)(2,1)S(1)} %collective-permute-done.18), channel_id=1, source_target_pairs={{0,4},{4,0},{8,12},{12,8},{16,20},{20,16},{24,28},{28,24},{1,5},{5... | collective-permute-start | bytes 1228808 | tf_op jit(solution)/shard_map/ppermute | solution.py:63
  168.2 3.3 %collective-permute-start.20 = (bf16[2,384,800]{1,2,0:T(8,128)(2,1)}, bf16[2,384,800]{1,2,0:T(8,128)(2,1)}, u32[]{:S(2)}, u32[]{:S(2)}) collective-permute-start(bf16[2,384,800]{1,2,0:T(8,128)(2,1)} %pad_maximum_fusion.1), channel_id=1, source_target_pairs={{0,1},{1,0},{2,3},{3,2},{4,5},{5,4},{6,7},{7,6},{8,9},{9,8},{10,11... | collective-permute-start | bytes 3686408 | tf_op jit(solution)/shard_map/ppermute | solution.py:63
  176.7 16.1 %collective-permute-start.21 = (bf16[384,800]{0,1:T(8,128)(2,1)}, bf16[384,800]{0,1:T(8,128)(2,1)S(1)}, u32[]{:S(2)}, u32[]{:S(2)}) collective-permute-start(bf16[384,800]{0,1:T(8,128)(2,1)} %fusion.32), channel_id=1, source_target_pairs={{0,2},{1,3},{2,0},{3,1},{4,6},{5,7},{6,4},{7,5},{8,10},{9,11},{10,... | collective-permute-start | bytes 1843208 | tf_op jit(solution)/shard_map/ppermute | solution.py:63
  203.9 12.3 %all-to-all-start.1 = ((f32[3,8,24]{2,0,1:T(4,128)}), f32[3,8,24]{2,0,1:T(4,128)S(1)}, u32[]{:S(2)}, u32[]{:S(2)}) async-start(f32[3,8,24]{2,0,1:T(4,128)} %copy.43), calls=%async_computation.1 | async-start | bytes 32768 | tf_op jit(solution)/shard_map/all_to_all | solution.py:220
  216.1 35.9 %all-to-all-start = ((bf16[8,96,800]{2,1,0:T(8,128)(2,1)}), bf16[8,96,800]{2,1,0:T(8,128)(2,1)}, u32[]{:S(2)}, u32[]{:S(2)}) async-start(bf16[8,96,800]{2,1,0:T(8,128)(2,1)} %bitcast.26), calls=%async_computation | async-start | bytes 2752512 | tf_op jit(solution)/shard_map/all_to_all | solution.py:206
  220.7 34.0 %copy-start.21 = (f32[4,800]{1,0:T(4,128)S(1)}, f32[4,800]{1,0:T(4,128)}, u32[]{:S(2)}) copy-start(f32[4,800]{1,0:T(4,128)} %param.19) | copy-start | bytes 38404
  220.7 34.0 %copy-start.22 = (f32[4,800]{1,0:T(4,128)S(1)}, f32[4,800]{1,0:T(4,128)}, u32[]{:S(2)}) copy-start(f32[4,800]{1,0:T(4,128)} %param.18) | copy-start | bytes 38404
  (20 other events, 72.6 us)

commit v2 on v1

--- a/solution.py
+++ b/solution.py
@@ -3,6 +3,8 @@
 import jax
 import jax.numpy as jnp
 from jax import lax
+from jax.experimental import pallas as pl
+from jax.experimental.pallas import tpu as pltpu
 from jax.sharding import PartitionSpec as P
 
 D = 3200
@@ -66,6 +68,42 @@
 def ring(value):
     count = lax.axis_size("req")
     return lax.ppermute(value, "req", [(i, (i + 2) % count) for i in range(count)])
+
+
+def split_kernel(w_ref, q_ref, k_ref, v_ref):
+    for head in range(q_ref.shape[1] // HEAD_DIM):
+        to = pl.ds(head * HEAD_DIM, HEAD_DIM)
+        for i, ref in enumerate((q_ref, k_ref, v_ref)):
+            ref[:, to] = w_ref[:, pl.ds((3 * head + i) * HEAD_DIM, HEAD_DIM)]
+
+
+def split_heads(w_qkv):
+    depth, columns = w_qkv.shape
+    part = jax.ShapeDtypeStruct((depth, columns // 3), w_qkv.dtype)
+    return pl.pallas_call(
+        split_kernel,
+        out_shape=(part,) * 3,
+        in_specs=[pl.BlockSpec(memory_space=pltpu.VMEM)],
+        out_specs=(pl.BlockSpec(memory_space=pltpu.VMEM),) * 3,
+        compiler_params=pltpu.CompilerParams(vmem_limit_bytes=16 << 20),
+        cost_estimate=pl.CostEstimate(
+            flops=0, bytes_accessed=4 * depth * columns, transcendentals=0
+        ),
+        name="split_heads",
+    )(w_qkv)
+
+
+def scatter_rows(packed, me, by_permutes):
+    if not by_permutes:
+        return lax.all_to_all(packed, "req", split_axis=0, concat_axis=0, tiled=True)
+    count = packed.shape[0]
+    arrived = jnp.zeros_like(packed)
+    for bits in range(count):
+        block = lax.dynamic_index_in_dim(packed, me ^ bits, 0, keepdims=False)
+        if bits:
+            block = swap(block, "req", bits)
+        arrived = lax.dynamic_update_index_in_dim(arrived, block, me ^ bits, 0)
+    return arrived
 
 
 def after(value, *first):
@@ -91,16 +129,19 @@
     plane, side = me // 2, me % 2
     column = lax.axis_index("tp")
 
-    w_parts = w_qkv.reshape(depth, head_count, 3, HEAD_DIM)
-    w_q, w_k, w_v = (w_parts[:, :, i].reshape(depth, head_share) for i in range(3))
+    if depth % 16 == 0:
+        w_q, w_k, w_v = split_heads(w_qkv)
+    else:
+        w_parts = w_qkv.reshape(depth, head_count, 3, HEAD_DIM)
+        w_q, w_k, w_v = (w_parts[:, :, i].reshape(depth, head_share) for i in range(3))
     w_o = w_out.T
     if use_ring:
         q_blocks, k_blocks, v_blocks, o_blocks = [w_q], [w_k], [w_v], [w_o]
         for step in range(1, planes):
             q_blocks.append(ring(q_blocks[-1]))
             k_blocks.append(ring(k_blocks[-1]))
-        v_blocks[0] = after(w_v, q_blocks[2])
-        o_blocks[0] = after(w_o, k_blocks[2])
+        v_blocks[0] = after(w_v, q_blocks[-1])
+        o_blocks[0] = after(w_o, k_blocks[-1])
         for step in range(1, planes):
             v_blocks.append(ring(v_blocks[-1]))
             o_blocks.append(ring(o_blocks[-1]))
@@ -118,17 +159,14 @@
     both = jnp.concatenate([mine.reshape(token_count, planes * depth), theirs], axis=0)
 
     if use_ring:
-        both_blocks = both.reshape(2 * token_count, planes, depth).transpose(1, 0, 2)
 
         def project(blocks):
-            total = None
+            whole = jnp.zeros((planes * depth, head_share), BF16)
             for step, block in enumerate(blocks):
-                rows = lax.dynamic_index_in_dim(
-                    both_blocks, (plane + planes - step) % planes, 0, keepdims=False
-                )
-                term = jnp.dot(rows, block, preferred_element_type=F32)
-                total = term if total is None else total + term
-            return total
+                first_row = (plane + planes - step) % planes * depth
+                whole = lax.dynamic_update_slice_in_dim(whole, block, first_row, 0)
+            return jnp.dot(both, whole, preferred_element_type=F32)
+
     else:
         groups = [list(range(i, devices_req, 2)) for i in range(2)]
 
@@ -203,13 +241,16 @@
     chosen = row_tokens.reshape(-1)[:, None] == token_ids[None, :]
     packed = jnp.dot(chosen.astype(BF16), hidden, preferred_element_type=F32).astype(BF16)
     packed = packed.reshape(devices_req, capacity * 4, quarter)
-    arrived = lax.all_to_all(packed, "req", split_axis=0, concat_axis=0, tiled=True)
+    arrived = scatter_rows(packed, me, use_ring)
 
     hidden_float = hidden.astype(F32)
     token_sums = jnp.stack(
         [jnp.sum(hidden_float, axis=1), jnp.sum(hidden_float * hidden_float, axis=1)]
     )
-    token_sums = lax.psum(token_sums, "tp")
+    if use_ring:
+        token_sums = token_sums + sum(swap(token_sums, "tp", bit) for bit in range(1, devices_tp))
+    else:
+        token_sums = lax.psum(token_sums, "tp")
     in_row = jnp.any(row_tokens[:, :, None] == token_ids[None, None, :], axis=1)
     row_sums = jnp.sum(jnp.where(in_row[None], token_sums[:, None, :], 0.0), axis=2)
     mean_value = row_sums[0] / feature_total

time: 258 us -> 228 us (0.88); the launches traced: 257 us -> 224 us
  waiting for transfers between devices: 125 us -> 102 us
  starting transfers between devices: 28.5 us -> 41.1 us
  local copies, waits for them, and re-layouts: 37.5 us -> 26.3 us
  matrix products: 25.3 us -> 18.4 us
  blocking collectives: 12.2 us -> 6.75 us
    all_to_all x1 -> x0, waiting for transfers between devices: 31.3 us -> none  [body(): lax.all_to_all(packed, 'req', split_axis=0, concat_axis=0, tiled=True)]
    ppermute x10 -> x20, waiting for transfers between devices: 22.9 us -> 42.7 us  [swap(): return lax.ppermute(value, axis, [(i, i ^ bit) for i in range(count)])]
    ppermute x10 -> x20, starting transfers between devices: 10.1 us -> 28.8 us  [swap(): return lax.ppermute(value, axis, [(i, i ^ bit) for i in range(count)])]
    slice x1 -> x0, local copies, waits for them, and re-layouts: 10.9 us -> none  [body(): w_parts[:, :, i].reshape(depth, head_share)]
    ppermute x12, waiting for transfers between devices: 67.5 us -> 58.4 us  [ring(): lax.ppermute(value, 'req', [(i, (i + 2) % count) for i in range(count)])]
    dynamic_update_slice x0 -> x18, local copies, waits for them, and re-layouts: none -> 7.17 us  [the longest x7 4.78 us: scatter_rows(): arrived = lax.dynamic_update_index_in_dim(arrived, block, me ^ bits, 0)]
    psum x1 -> x0, blocking collectives: 6.1 us -> none  [body(): token_sums = lax.psum(token_sums, 'tp')]
    dot_general x12 -> x3, matrix products: 14.1 us -> 9.18 us  [project(): return jnp.dot(both, whole, preferred_element_type=F32)]
  transfers between devices with their start and end apart: 24 -> 33, of which waited for: 13 -> 18; matrix products, arithmetic and copies ran while one was open for 23% -> 23% of each run, Pallas kernels for 0% -> 0%
where the time goes in v2:
time: 228 us; the launch traced here: 224 us
  waiting for transfers between devices  102 us (45%)
  starting transfers between devices  41.1 us (18%)
  other arithmetic  28.5 us (12%)
  local copies, waits for them, and re-layouts  26.3 us (12%)
  matrix products  18.4 us (8%)
  blocking collectives  6.75 us (3%)
    ppermute x12, waiting for transfers between devices, ring(): lax.ppermute(value, 'req', [(i, (i + 2) % count) for i in range(count)])  58.4 us
    ppermute x20, waiting for transfers between devices, swap(): return lax.ppermute(value, axis, [(i, i ^ bit) for i in range(count)])  42.7 us
    ppermute x20, starting transfers between devices, swap(): return lax.ppermute(value, axis, [(i, i ^ bit) for i in range(count)])  28.8 us
    unnamed x55, local copies, waits for them, and re-layouts  9.89 us
    dot_general x3, matrix products, project(): return jnp.dot(both, whole, preferred_element_type=F32)  9.18 us
    ppermute x12, starting transfers between devices, ring(): lax.ppermute(value, 'req', [(i, (i + 2) % count) for i in range(count)])  9.06 us
    psum x1, blocking collectives, body(): q_total, k_total = lax.psum((local_q, local_k), 'tp')  6.75 us
    select_n x4, other arithmetic, body(): low = jnp.where(side == 0, block, peer)  6 us
  transfers between devices with their start and end apart: 33, of which 18 were waited for; matrix products, arithmetic and copies ran while one was open for 23% of the time, Pallas kernels for 0%

profile of v2, /device:TPU:0, one launch (start us, length us, event | category | flops | bytes accessed | tf_op | source)
XLA Modules:
  0.0 223.9 jit_solution(17887924405059751690)
XLA Ops:
  1.5 3.1 %collective-permute-start.9 = (bf16[400,512]{1,0:T(8,128)(2,1)S(1)}, bf16[400,512]{1,0:T(8,128)(2,1)S(1)}, u32[]{:S(2)}, u32[]{:S(2)}) collective-permute-start(bf16[400,512]{1,0:T(8,128)(2,1)S(1)} %get-tuple-element.13), channel_id=1, source_target_pairs={{0,8},{4,12},{8,16},{12,20},{16,24},{20,28},{24,0},{28,4},{1,9},{5... | collective-permute-start | bytes 1228808 | tf_op jit(solution)/shard_map/ppermute | solution.py:70
  6.2 4.3 %copy.37 = bf16[384,3200]{0,1:T(8,128)(2,1)} copy(bf16[384,3200]{1,0:T(8,128)(2,1)} %param.10) | data formatting | bytes 4915200 | tf_op args[0]
  10.4 2.3 %fusion.1 = f32[384]{0:T(512)S(1)} fusion(bf16[384,3200]{0,1:T(8,128)(2,1)} %copy.37), kind=kLoop, calls=%fused_computation.3 | loop fusion | flops 3686016 | bytes 2459136 | tf_op jit(solution)/shard_map/reduce_sum | solution.py:152
  12.8 2.7 %fusion.3 = bf16[384,3200]{0,1:T(8,128)(2,1)S(1)} fusion(bf16[384,3200]{0,1:T(8,128)(2,1)} %copy.37, f32[3200]{0:T(1024)S(1)} %copy-done.14, f32[384]{0:T(512)S(1)} %add_rsqrt_fusion.2), kind=kLoop, calls=%fused_computation.5 | loop fusion | flops 4915200 | bytes 4929536 | tf_op jit(solution)/shard_map/convert_element_type | solution.py:153
  21.4 4.4 %collective-permute-done.1 = bf16[400,512]{1,0:T(8,128)(2,1)} collective-permute-done((bf16[400,512]{1,0:T(8,128)(2,1)S(1)}, bf16[400,512]{1,0:T(8,128)(2,1)}, u32[]{:S(2)}, u32[]{:S(2)}) %collective-permute-start.1) | collective-permute-done | bytes 409632 | tf_op jit(solution)/shard_map/ppermute | solution.py:70
  26.9 7.6 %collective-permute-done.10 = bf16[400,512]{1,0:T(8,128)(2,1)S(1)} collective-permute-done((bf16[400,512]{1,0:T(8,128)(2,1)S(1)}, bf16[400,512]{1,0:T(8,128)(2,1)S(1)}, u32[]{:S(2)}, u32[]{:S(2)}) %collective-permute-start.10) | collective-permute-done | bytes 409632 | tf_op jit(solution)/shard_map/ppermute | solution.py:70
  34.5 8.7 %collective-permute-done.2 = bf16[400,512]{1,0:T(8,128)(2,1)S(1)} collective-permute-done((bf16[400,512]{1,0:T(8,128)(2,1)}, bf16[400,512]{1,0:T(8,128)(2,1)S(1)}, u32[]{:S(2)}, u32[]{:S(2)}) %collective-permute-start.2) | collective-permute-done | bytes 409632 | tf_op jit(solution)/shard_map/ppermute | solution.py:70
  44.4 7.6 %collective-permute-done.11 = bf16[400,512]{1,0:T(8,128)(2,1)S(1)} collective-permute-done((bf16[400,512]{1,0:T(8,128)(2,1)S(1)}, bf16[400,512]{1,0:T(8,128)(2,1)S(1)}, u32[]{:S(2)}, u32[]{:S(2)}) %collective-permute-start.11) | collective-permute-done | bytes 409632 | tf_op jit(solution)/shard_map/ppermute | solution.py:70
  52.0 7.9 %collective-permute-done.3 = bf16[400,512]{1,0:T(8,128)(2,1)S(1)} collective-permute-done((bf16[400,512]{1,0:T(8,128)(2,1)S(1)}, bf16[400,512]{1,0:T(8,128)(2,1)S(1)}, u32[]{:S(2)}, u32[]{:S(2)}) %collective-permute-start.3) | collective-permute-done | bytes 409632 | tf_op jit(solution)/shard_map/ppermute | solution.py:70
  60.0 2.9 %fusion.32 = f32[768,512]{0,1:T(8,128)S(1)} fusion(bf16[1600,512]{1,0:T(8,128)(2,1)S(1)} %get-tuple-element.55, bf16[384,1600]{0,1:T(8,128)(2,1)} %collective-permute-done, bf16[384,1600]{0,1:T(8,128)(2,1)S(1)} %bitcast.117), kind=kOutput, calls=%fused_computation.63 | convolution fusion | flops 1263206400 | bytes 5668864 | tf_op jit(solution)/shard_map/dot_general | solution.py:168
  64.6 3.3 %fusion.33 = f32[768,512]{0,1:T(8,128)S(1)} fusion(bf16[1600,512]{1,0:T(8,128)(2,1)S(1)} %get-tuple-element.56, bf16[384,1600]{0,1:T(8,128)(2,1)} %collective-permute-done, bf16[384,1600]{0,1:T(8,128)(2,1)} %bitcast.118), kind=kOutput, calls=%fused_computation.64 | convolution fusion | flops 1263206400 | bytes 5668864 | tf_op jit(solution)/shard_map/dot_general | solution.py:168
  76.7 6.9 %collective-permute-done.8 = bf16[384,512]{0,1:T(8,128)(2,1)S(1)} collective-permute-done((bf16[384,512]{0,1:T(8,128)(2,1)S(1)}, bf16[384,512]{0,1:T(8,128)(2,1)S(1)}, u32[]{:S(2)}, u32[]{:S(2)}) %collective-permute-start.8) | collective-permute-done | bytes 393248 | tf_op jit(solution)/shard_map/ppermute | solution.py:65
  85.1 6.8 %all-reduce = (f32[384]{0:T(512)}, f32[384]{0:T(512)}) all-reduce(f32[384]{0:T(512)} %multiply_reduce_fusion.1, f32[384]{0:T(512)} %multiply_reduce_fusion), channel_id=1, replica_groups=mesh['req'=8,'tp'=4] {'tp'}, use_global_device_ids=true, to_apply=%region_9.10 | all-reduce | flops 768 | bytes 6144 | tf_op jit(solution)/shard_map/psum | solution.py:188
  94.0 2.0 fusion.66
  99.7 8.7 %collective-permute-done.5 = bf16[400,512]{1,0:T(8,128)(2,1)S(1)} collective-permute-done((bf16[400,512]{1,0:T(8,128)(2,1)}, bf16[400,512]{1,0:T(8,128)(2,1)S(1)}, u32[]{:S(2)}, u32[]{:S(2)}) %collective-permute-start.5) | collective-permute-done | bytes 409632 | tf_op jit(solution)/shard_map/ppermute | solution.py:70
  109.4 2.0 broadcast_select_fusion.7
  111.5 5.7 %collective-permute-done.16 = bf16[400,512]{1,0:T(8,128)(2,1)S(1)} collective-permute-done((bf16[400,512]{1,0:T(8,128)(2,1)}, bf16[400,512]{1,0:T(8,128)(2,1)S(1)}, u32[]{:S(2)}, u32[]{:S(2)}) %collective-permute-start.16) | collective-permute-done | bytes 409632 | tf_op jit(solution)/shard_map/ppermute | solution.py:70
  118.7 7.2 %collective-permute-done.6 = bf16[400,512]{1,0:T(8,128)(2,1)S(1)} collective-permute-done((bf16[400,512]{1,0:T(8,128)(2,1)S(1)}, bf16[400,512]{1,0:T(8,128)(2,1)S(1)}, u32[]{:S(2)}, u32[]{:S(2)}) %collective-permute-start.6) | collective-permute-done | bytes 409632 | tf_op jit(solution)/shard_map/ppermute | solution.py:70
  126.0 3.0 %fusion.34 = f32[768,512]{0,1:T(8,128)S(1)} fusion(bf16[1600,512]{1,0:T(8,128)(2,1)S(1)} %constant_dynamic-update-slice_fusion.8, bf16[384,1600]{0,1:T(8,128)(2,1)} %collective-permute-done, bf16[384,1600]{0,1:T(8,128)(2,1)S(1)} %bitcast.119), kind=kOutput, calls=%fused_computation.65 | convolution fusion | flops 1263206400 | bytes 5668864 | tf_op jit(solution)/shard_map/dot_general | solution.py:168
  135.6 4.2 %collective-permute-done.7 = bf16[384,512]{0,1:T(8,128)(2,1)S(1)} collective-permute-done((bf16[384,512]{0,1:T(8,128)(2,1)S(1)}, bf16[384,512]{0,1:T(8,128)(2,1)S(1)}, u32[]{:S(2)}, u32[]{:S(2)}) %collective-permute-start.7) | collective-permute-done | bytes 393248 | tf_op jit(solution)/shard_map/ppermute | solution.py:65
  140.6 2.7 %convolution_convert_fusion.5 = bf16[4,128,384]{2,1,0:T(8,128)(2,1)} fusion(bf16[384,4,128]{0,2,1:T(8,128)(2,1)} %bitcast.120, f32[4,384]{1,0:T(4,128)S(1)} %fusion.65, f32[4,384,384]{1,2,0:T(8,128)S(1)} %fusion.66, pred[384,384]{0,1:T(8,128)(4,1)S(1)} %copy-done.13), kind=kOutput, calls=%fused_computation.24 | convolution fusion | flops 154142592 | bytes 3299328 | tf_op jit(solution)/shard_map/hqk,khd->qhd/dot_general | solution.py:202
  150.9 2.5 %collective-permute-done.20 = bf16[2,384,800]{1,2,0:T(8,128)(2,1)} collective-permute-done((bf16[2,384,800]{1,2,0:T(8,128)(2,1)S(1)}, bf16[2,384,800]{1,2,0:T(8,128)(2,1)}, u32[]{:S(2)}, u32[]{:S(2)}) %collective-permute-start.20) | collective-permute-done | bytes 1228832 | tf_op jit(solution)/shard_map/ppermute | solution.py:65
  154.9 2.0 fusion.35
  159.3 13.7 %collective-permute-done.21 = bf16[384,800]{0,1:T(8,128)(2,1)S(1)} collective-permute-done((bf16[384,800]{0,1:T(8,128)(2,1)}, bf16[384,800]{0,1:T(8,128)(2,1)S(1)}, u32[]{:S(2)}, u32[]{:S(2)}) %collective-permute-start.21) | collective-permute-done | bytes 614432 | tf_op jit(solution)/shard_map/ppermute | solution.py:65
  183.9 3.3 %all-to-all-start = ((f32[3,8,24]{2,0,1:T(4,128)}), f32[3,8,24]{2,0,1:T(4,128)S(1)}, u32[]{:S(2)}, u32[]{:S(2)}) async-start(f32[3,8,24]{2,0,1:T(4,128)} %copy.43), calls=%async_computation | async-start | bytes 32768 | tf_op jit(solution)/shard_map/all_to_all | solution.py:261
  190.7 2.4 %collective-permute-start.25 = (bf16[96,800]{1,0:T(8,128)(2,1)S(1)}, bf16[96,800]{1,0:T(8,128)(2,1)S(1)}, u32[]{:S(2)}, u32[]{:S(2)}) collective-permute-start(bf16[96,800]{1,0:T(8,128)(2,1)S(1)} %get-tuple-element.38), channel_id=1, source_target_pairs={{0,16},{4,20},{8,24},{12,28},{16,0},{20,4},{24,8},{28,12},{1,17},{... | collective-permute-start | bytes 460808 | tf_op jit(solution)/shard_map/ppermute | solution.py:65
  194.2 3.0 %collective-permute-start.27 = (bf16[96,800]{1,0:T(8,128)(2,1)S(1)}, bf16[96,800]{1,0:T(8,128)(2,1)S(1)}, u32[]{:S(2)}, u32[]{:S(2)}) collective-permute-start(bf16[96,800]{1,0:T(8,128)(2,1)S(1)} %get-tuple-element.36), channel_id=1, source_target_pairs={{0,24},{4,28},{8,16},{12,20},{16,8},{20,12},{24,0},{28,4},{1,25},{... | collective-permute-start | bytes 460808 | tf_op jit(solution)/shard_map/ppermute | solution.py:65
  197.9 2.9 %collective-permute-done.23 = bf16[96,800]{1,0:T(8,128)(2,1)S(1)} collective-permute-done((bf16[96,800]{1,0:T(8,128)(2,1)S(1)}, bf16[96,800]{1,0:T(8,128)(2,1)S(1)}, u32[]{:S(2)}, u32[]{:S(2)}) %collective-permute-start.23) | collective-permute-done | bytes 153632 | tf_op jit(solution)/shard_map/ppermute | solution.py:65
  200.8 3.5 %collective-permute-start.28 = (bf16[96,800]{1,0:T(8,128)(2,1)S(1)}, bf16[96,800]{1,0:T(8,128)(2,1)S(1)}, u32[]{:S(2)}, u32[]{:S(2)}) collective-permute-start(bf16[96,800]{1,0:T(8,128)(2,1)S(1)} %get-tuple-element.35), channel_id=1, source_target_pairs={{0,28},{4,24},{8,20},{12,16},{16,12},{20,8},{24,4},{28,0},{1,29},{... | collective-permute-start | bytes 460808 | tf_op jit(solution)/shard_map/ppermute | solution.py:65
  206.5 10.4 %collective-permute-done.26 = bf16[96,800]{1,0:T(8,128)(2,1)S(1)} collective-permute-done((bf16[96,800]{1,0:T(8,128)(2,1)S(1)}, bf16[96,800]{1,0:T(8,128)(2,1)S(1)}, u32[]{:S(2)}, u32[]{:S(2)}) %collective-permute-start.26) | collective-permute-done | bytes 153632 | tf_op jit(solution)/shard_map/ppermute | solution.py:65
  219.0 2.7 %reshape.391 = f32[192,4,800]{2,1,0:T(4,128)S(1)} reshape(bf16[8,96,800]{2,1,0:T(8,128)(2,1)} %bitcast_dynamic-update-slice_fusion) | data formatting | bytes 3686400 | tf_op jit(solution)/shard_map/convert_element_type | solution.py:264
  221.7 2.3 %add_convert_fusion = bf16[192,4,800]{2,1,0:T(4,128)(2,1)} fusion(f32[192,4,800]{2,1,0:T(4,128)S(1)} %reshape.391, f32[4,800]{1,0:T(4,128)S(1)} %copy-done.15, f32[192]{0:T(256)S(1)} %mul.374, f32[4,800]{1,0:T(4,128)S(1)} %copy-done.16, f32[192]{0:T(256)S(1)} %add.459, f32[192]{0:T(256)S(1)} %mul.369), kind=kLoop, calls=%fused_computation.6 | loop fusion | flops 3686400 | bytes 3714304 | tf_op jit(solution)/shard_map/convert_element_type | solution.py:266
  (188 shorter events, 70.4 us)
Async XLA Ops:
  1.5 18.3 %collective-permute-start.9 = (bf16[400,512]{1,0:T(8,128)(2,1)S(1)}, bf16[400,512]{1,0:T(8,128)(2,1)S(1)}, u32[]{:S(2)}, u32[]{:S(2)}) collective-permute-start(bf16[400,512]{1,0:T(8,128)(2,1)S(1)} %get-tuple-element.13), channel_id=1, source_target_pairs={{0,8},{4,12},{8,16},{12,20},{16,24},{20,28},{24,0},{28,4},{1,9},{5... | collective-permute-start | bytes 1228808 | tf_op jit(solution)/shard_map/ppermute | solution.py:70
  4.6 21.2 %collective-permute-start.1 = (bf16[400,512]{1,0:T(8,128)(2,1)S(1)}, bf16[400,512]{1,0:T(8,128)(2,1)}, u32[]{:S(2)}, u32[]{:S(2)}) collective-permute-start(bf16[400,512]{1,0:T(8,128)(2,1)S(1)} %get-tuple-element.11), channel_id=1, source_target_pairs={{0,8},{4,12},{8,16},{12,20},{16,24},{20,28},{24,0},{28,4},{1,9},{5... | collective-permute-start | bytes 1228808 | tf_op jit(solution)/shard_map/ppermute | solution.py:70
  16.8 43.2 %collective-permute-start = (bf16[384,1600]{0,1:T(8,128)(2,1)}, bf16[384,1600]{0,1:T(8,128)(2,1)}, u32[]{:S(2)}, u32[]{:S(2)}) collective-permute-start(bf16[384,1600]{0,1:T(8,128)(2,1)} %bitcast.7), channel_id=1, source_target_pairs={{0,4},{4,0},{8,12},{12,8},{16,20},{20,16},{24,28},{28,24},{1,5},{5... | collective-permute-start | bytes 3686408 | tf_op jit(solution)/shard_map/ppermute | solution.py:65
  19.8 14.7 %collective-permute-start.10 = (bf16[400,512]{1,0:T(8,128)(2,1)S(1)}, bf16[400,512]{1,0:T(8,128)(2,1)S(1)}, u32[]{:S(2)}, u32[]{:S(2)}) collective-permute-start(bf16[400,512]{1,0:T(8,128)(2,1)S(1)} %collective-permute-done.9), channel_id=1, source_target_pairs={{0,8},{4,12},{8,16},{12,20},{16,24},{20,28},{24,0},{28,4},{1,9},{5... | collective-permute-start | bytes 1228808 | tf_op jit(solution)/shard_map/ppermute | solution.py:70
  25.8 17.4 %collective-permute-start.2 = (bf16[400,512]{1,0:T(8,128)(2,1)}, bf16[400,512]{1,0:T(8,128)(2,1)S(1)}, u32[]{:S(2)}, u32[]{:S(2)}) collective-permute-start(bf16[400,512]{1,0:T(8,128)(2,1)} %collective-permute-done.1), channel_id=1, source_target_pairs={{0,8},{4,12},{8,16},{12,20},{16,24},{20,28},{24,0},{28,4},{1,9},{5... | collective-permute-start | bytes 1228808 | tf_op jit(solution)/shard_map/ppermute | solution.py:70
  34.5 17.6 %collective-permute-start.11 = (bf16[400,512]{1,0:T(8,128)(2,1)S(1)}, bf16[400,512]{1,0:T(8,128)(2,1)S(1)}, u32[]{:S(2)}, u32[]{:S(2)}) collective-permute-start(bf16[400,512]{1,0:T(8,128)(2,1)S(1)} %collective-permute-done.10), channel_id=1, source_target_pairs={{0,8},{4,12},{8,16},{12,20},{16,24},{20,28},{24,0},{28,4},{1,9},{5... | collective-permute-start | bytes 1228808 | tf_op jit(solution)/shard_map/ppermute | solution.py:70
  43.2 16.7 %collective-permute-start.3 = (bf16[400,512]{1,0:T(8,128)(2,1)S(1)}, bf16[400,512]{1,0:T(8,128)(2,1)S(1)}, u32[]{:S(2)}, u32[]{:S(2)}) collective-permute-start(bf16[400,512]{1,0:T(8,128)(2,1)S(1)} %collective-permute-done.2), channel_id=1, source_target_pairs={{0,8},{4,12},{8,16},{12,20},{16,24},{20,28},{24,0},{28,4},{1,9},{5... | collective-permute-start | bytes 1228808 | tf_op jit(solution)/shard_map/ppermute | solution.py:70
  63.0 12.1 %collective-permute-start.12 = (bf16[384,512]{0,1:T(8,128)(2,1)S(1)}, bf16[384,512]{0,1:T(8,128)(2,1)S(1)}, u32[]{:S(2)}, u32[]{:S(2)}) collective-permute-start(bf16[384,512]{0,1:T(8,128)(2,1)S(1)} %slice.135), channel_id=1, source_target_pairs={{0,4},{4,0},{8,12},{12,8},{16,20},{20,16},{24,28},{28,24},{1,5},{5... | collective-permute-start | bytes 1179656 | tf_op jit(solution)/shard_map/ppermute | solution.py:65
  68.0 15.6 %collective-permute-start.8 = (bf16[384,512]{0,1:T(8,128)(2,1)S(1)}, bf16[384,512]{0,1:T(8,128)(2,1)S(1)}, u32[]{:S(2)}, u32[]{:S(2)}) collective-permute-start(bf16[384,512]{0,1:T(8,128)(2,1)S(1)} %slice.136), channel_id=1, source_target_pairs={{0,4},{4,0},{8,12},{12,8},{16,20},{20,16},{24,28},{28,24},{1,5},{5... | collective-permute-start | bytes 1179656 | tf_op jit(solution)/shard_map/ppermute | solution.py:65
  69.2 40.2 %collective-permute-start.13 = (bf16[400,512]{1,0:T(8,128)(2,1)}, bf16[400,512]{1,0:T(8,128)(2,1)}, u32[]{:S(2)}, u32[]{:S(2)}) collective-permute-start(bf16[400,512]{1,0:T(8,128)(2,1)} %bitcast.13), channel_id=1, source_target_pairs={{0,4},{4,0},{8,12},{12,8},{16,20},{20,16},{24,28},{28,24},{1,5},{5... | collective-permute-start | bytes 1228808 | tf_op jit(solution)/shard_map/ppermute | solution.py:65
  70.7 25.3 %collective-permute-start.14 = (bf16[400,512]{1,0:T(8,128)(2,1)}, bf16[400,512]{1,0:T(8,128)(2,1)}, u32[]{:S(2)}, u32[]{:S(2)}) collective-permute-start(bf16[400,512]{1,0:T(8,128)(2,1)} %bitcast.13), channel_id=1, source_target_pairs={{0,8},{4,12},{8,16},{12,20},{16,24},{20,28},{24,0},{28,4},{1,9},{5... | collective-permute-start | bytes 1228808 | tf_op jit(solution)/shard_map/ppermute | solution.py:70
  70.7 23.2 %collective-permute-start.4 = (bf16[400,512]{1,0:T(8,128)(2,1)S(1)}, bf16[400,512]{1,0:T(8,128)(2,1)}, u32[]{:S(2)}, u32[]{:S(2)}) collective-permute-start(bf16[400,512]{1,0:T(8,128)(2,1)S(1)} %get-tuple-element.12), channel_id=1, source_target_pairs={{0,8},{4,12},{8,16},{12,20},{16,24},{20,28},{24,0},{28,4},{1,9},{5... | collective-permute-start | bytes 1228808 | tf_op jit(solution)/shard_map/ppermute | solution.py:70
  93.9 14.5 %collective-permute-start.5 = (bf16[400,512]{1,0:T(8,128)(2,1)}, bf16[400,512]{1,0:T(8,128)(2,1)S(1)}, u32[]{:S(2)}, u32[]{:S(2)}) collective-permute-start(bf16[400,512]{1,0:T(8,128)(2,1)} %collective-permute-done.4), channel_id=1, source_target_pairs={{0,8},{4,12},{8,16},{12,20},{16,24},{20,28},{24,0},{28,4},{1,9},{5... | collective-permute-start | bytes 1228808 | tf_op jit(solution)/shard_map/ppermute | solution.py:70
  96.1 21.1 %collective-permute-start.16 = (bf16[400,512]{1,0:T(8,128)(2,1)}, bf16[400,512]{1,0:T(8,128)(2,1)S(1)}, u32[]{:S(2)}, u32[]{:S(2)}) collective-permute-start(bf16[400,512]{1,0:T(8,128)(2,1)} %collective-permute-done.14), channel_id=1, source_target_pairs={{0,8},{4,12},{8,16},{12,20},{16,24},{20,28},{24,0},{28,4},{1,9},{5... | collective-permute-start | bytes 1228808 | tf_op jit(solution)/shard_map/ppermute | solution.py:70
  98.1 32.5 %collective-permute-start.15 = (bf16[400,512]{1,0:T(8,128)(2,1)}, bf16[400,512]{1,0:T(8,128)(2,1)S(1)}, u32[]{:S(2)}, u32[]{:S(2)}) collective-permute-start(bf16[400,512]{1,0:T(8,128)(2,1)} %collective-permute-done.14), channel_id=1, source_target_pairs={{0,4},{4,0},{8,12},{12,8},{16,20},{20,16},{24,28},{28,24},{1,5},{5... | collective-permute-start | bytes 1228808 | tf_op jit(solution)/shard_map/ppermute | solution.py:65
  108.4 17.6 %collective-permute-start.6 = (bf16[400,512]{1,0:T(8,128)(2,1)S(1)}, bf16[400,512]{1,0:T(8,128)(2,1)S(1)}, u32[]{:S(2)}, u32[]{:S(2)}) collective-permute-start(bf16[400,512]{1,0:T(8,128)(2,1)S(1)} %collective-permute-done.5), channel_id=1, source_target_pairs={{0,8},{4,12},{8,16},{12,20},{16,24},{20,28},{24,0},{28,4},{1,9},{5... | collective-permute-start | bytes 1228808 | tf_op jit(solution)/shard_map/ppermute | solution.py:70
  117.1 17.5 %collective-permute-start.17 = (bf16[400,512]{1,0:T(8,128)(2,1)S(1)}, bf16[400,512]{1,0:T(8,128)(2,1)S(1)}, u32[]{:S(2)}, u32[]{:S(2)}) collective-permute-start(bf16[400,512]{1,0:T(8,128)(2,1)S(1)} %collective-permute-done.16), channel_id=1, source_target_pairs={{0,4},{4,0},{8,12},{12,8},{16,20},{20,16},{24,28},{28,24},{1,5},{5... | collective-permute-start | bytes 1228808 | tf_op jit(solution)/shard_map/ppermute | solution.py:65
  118.7 14.5 %collective-permute-start.18 = (bf16[400,512]{1,0:T(8,128)(2,1)S(1)}, bf16[400,512]{1,0:T(8,128)(2,1)S(1)}, u32[]{:S(2)}, u32[]{:S(2)}) collective-permute-start(bf16[400,512]{1,0:T(8,128)(2,1)S(1)} %collective-permute-done.16), channel_id=1, source_target_pairs={{0,8},{4,12},{8,16},{12,20},{16,24},{20,28},{24,0},{28,4},{1,9},{5... | collective-permute-start | bytes 1228808 | tf_op jit(solution)/shard_map/ppermute | solution.py:70
  129.0 10.8 %collective-permute-start.7 = (bf16[384,512]{0,1:T(8,128)(2,1)S(1)}, bf16[384,512]{0,1:T(8,128)(2,1)S(1)}, u32[]{:S(2)}, u32[]{:S(2)}) collective-permute-start(bf16[384,512]{0,1:T(8,128)(2,1)S(1)} %slice.137), channel_id=1, source_target_pairs={{0,4},{4,0},{8,12},{12,8},{16,20},{20,16},{24,28},{28,24},{1,5},{5... | collective-permute-start | bytes 1179656 | tf_op jit(solution)/shard_map/ppermute | solution.py:65
  133.1 13.7 %collective-permute-start.19 = (bf16[400,512]{1,0:T(8,128)(2,1)S(1)}, bf16[400,512]{1,0:T(8,128)(2,1)}, u32[]{:S(2)}, u32[]{:S(2)}) collective-permute-start(bf16[400,512]{1,0:T(8,128)(2,1)S(1)} %collective-permute-done.18), channel_id=1, source_target_pairs={{0,4},{4,0},{8,12},{12,8},{16,20},{20,16},{24,28},{28,24},{1,5},{5... | collective-permute-start | bytes 1228808 | tf_op jit(solution)/shard_map/ppermute | solution.py:65
  156.9 16.1 %collective-permute-start.21 = (bf16[384,800]{0,1:T(8,128)(2,1)}, bf16[384,800]{0,1:T(8,128)(2,1)S(1)}, u32[]{:S(2)}, u32[]{:S(2)}) collective-permute-start(bf16[384,800]{0,1:T(8,128)(2,1)} %fusion.35), channel_id=1, source_target_pairs={{0,2},{1,3},{2,0},{3,1},{4,6},{5,7},{6,4},{7,5},{8,10},{9,11},{10,... | collective-permute-start | bytes 1843208 | tf_op jit(solution)/shard_map/ppermute | solution.py:65
  174.7 7.2 %collective-permute-start.29 = (f32[2,384]{1,0:T(2,128)S(1)}, f32[2,384]{1,0:T(2,128)S(1)}, u32[]{:S(2)}, u32[]{:S(2)}) collective-permute-start(f32[2,384]{1,0:T(2,128)S(1)} %pad_maximum_fusion.7), channel_id=1, source_target_pairs={{0,1},{1,0},{2,3},{3,2},{4,5},{5,4},{6,7},{7,6},{8,9},{9,8},{10,11... | collective-permute-start | bytes 9224 | tf_op jit(solution)/shard_map/ppermute | solution.py:65
  174.8 7.1 %collective-permute-start.30 = (f32[2,384]{1,0:T(2,128)S(1)}, f32[2,384]{1,0:T(2,128)S(1)}, u32[]{:S(2)}, u32[]{:S(2)}) collective-permute-start(f32[2,384]{1,0:T(2,128)S(1)} %pad_maximum_fusion.7), channel_id=1, source_target_pairs={{0,2},{1,3},{2,0},{3,1},{4,6},{5,7},{6,4},{7,5},{8,10},{9,11},{10,... | collective-permute-start | bytes 9224 | tf_op jit(solution)/shard_map/ppermute | solution.py:65
  176.3 5.6 %collective-permute-start.31 = (f32[2,384]{1,0:T(2,128)S(1)}, f32[2,384]{1,0:T(2,128)S(1)}, u32[]{:S(2)}, u32[]{:S(2)}) collective-permute-start(f32[2,384]{1,0:T(2,128)S(1)} %pad_maximum_fusion.7), channel_id=1, source_target_pairs={{0,3},{1,2},{2,1},{3,0},{4,7},{5,6},{6,5},{7,4},{8,11},{9,10},{10,... | collective-permute-start | bytes 9224 | tf_op jit(solution)/shard_map/ppermute | solution.py:65
  180.3 13.9 %collective-permute-start.22 = (bf16[96,800]{1,0:T(8,128)(2,1)S(1)}, bf16[96,800]{1,0:T(8,128)(2,1)S(1)}, u32[]{:S(2)}, u32[]{:S(2)}) collective-permute-start(bf16[96,800]{1,0:T(8,128)(2,1)S(1)} %get-tuple-element.41), channel_id=1, source_target_pairs={{0,4},{4,0},{8,12},{12,8},{16,20},{20,16},{24,28},{28,24},{1,5},{5... | collective-permute-start | bytes 460808 | tf_op jit(solution)/shard_map/ppermute | solution.py:65
  183.9 10.0 %all-to-all-start = ((f32[3,8,24]{2,0,1:T(4,128)}), f32[3,8,24]{2,0,1:T(4,128)S(1)}, u32[]{:S(2)}, u32[]{:S(2)}) async-start(f32[3,8,24]{2,0,1:T(4,128)} %copy.43), calls=%async_computation | async-start | bytes 32768 | tf_op jit(solution)/shard_map/all_to_all | solution.py:261
  187.3 13.6 %collective-permute-start.23 = (bf16[96,800]{1,0:T(8,128)(2,1)S(1)}, bf16[96,800]{1,0:T(8,128)(2,1)S(1)}, u32[]{:S(2)}, u32[]{:S(2)}) collective-permute-start(bf16[96,800]{1,0:T(8,128)(2,1)S(1)} %get-tuple-element.40), channel_id=1, source_target_pairs={{0,8},{4,12},{8,0},{12,4},{16,24},{20,28},{24,16},{28,20},{1,9},{5... | collective-permute-start | bytes 460808 | tf_op jit(solution)/shard_map/ppermute | solution.py:65
  189.2 15.9 %collective-permute-start.24 = (bf16[96,800]{1,0:T(8,128)(2,1)S(1)}, bf16[96,800]{1,0:T(8,128)(2,1)S(1)}, u32[]{:S(2)}, u32[]{:S(2)}) collective-permute-start(bf16[96,800]{1,0:T(8,128)(2,1)S(1)} %get-tuple-element.39), channel_id=1, source_target_pairs={{0,12},{4,8},{8,4},{12,0},{16,28},{20,24},{24,20},{28,16},{1,13},{... | collective-permute-start | bytes 460808 | tf_op jit(solution)/shard_map/ppermute | solution.py:65
  190.7 15.2 %collective-permute-start.25 = (bf16[96,800]{1,0:T(8,128)(2,1)S(1)}, bf16[96,800]{1,0:T(8,128)(2,1)S(1)}, u32[]{:S(2)}, u32[]{:S(2)}) collective-permute-start(bf16[96,800]{1,0:T(8,128)(2,1)S(1)} %get-tuple-element.38), channel_id=1, source_target_pairs={{0,16},{4,20},{8,24},{12,28},{16,0},{20,4},{24,8},{28,12},{1,17},{... | collective-permute-start | bytes 460808 | tf_op jit(solution)/shard_map/ppermute | solution.py:65
  193.0 23.9 %collective-permute-start.26 = (bf16[96,800]{1,0:T(8,128)(2,1)S(1)}, bf16[96,800]{1,0:T(8,128)(2,1)S(1)}, u32[]{:S(2)}, u32[]{:S(2)}) collective-permute-start(bf16[96,800]{1,0:T(8,128)(2,1)S(1)} %get-tuple-element.37), channel_id=1, source_target_pairs={{0,20},{4,16},{8,28},{12,24},{16,4},{20,0},{24,12},{28,8},{1,21},{... | collective-permute-start | bytes 460808 | tf_op jit(solution)/shard_map/ppermute | solution.py:65
  194.2 23.4 %collective-permute-start.27 = (bf16[96,800]{1,0:T(8,128)(2,1)S(1)}, bf16[96,800]{1,0:T(8,128)(2,1)S(1)}, u32[]{:S(2)}, u32[]{:S(2)}) collective-permute-start(bf16[96,800]{1,0:T(8,128)(2,1)S(1)} %get-tuple-element.36), channel_id=1, source_target_pairs={{0,24},{4,28},{8,16},{12,20},{16,8},{20,12},{24,0},{28,4},{1,25},{... | collective-permute-start | bytes 460808 | tf_op jit(solution)/shard_map/ppermute | solution.py:65
  200.8 17.4 %collective-permute-start.28 = (bf16[96,800]{1,0:T(8,128)(2,1)S(1)}, bf16[96,800]{1,0:T(8,128)(2,1)S(1)}, u32[]{:S(2)}, u32[]{:S(2)}) collective-permute-start(bf16[96,800]{1,0:T(8,128)(2,1)S(1)} %get-tuple-element.35), channel_id=1, source_target_pairs={{0,28},{4,24},{8,20},{12,16},{16,12},{20,8},{24,4},{28,0},{1,29},{... | collective-permute-start | bytes 460808 | tf_op jit(solution)/shard_map/ppermute | solution.py:65
  (28 other events, 124.5 us)

commit v3 on v0

--- a/solution.py
+++ b/solution.py
@@ -3,11 +3,15 @@
 import jax
 import jax.numpy as jnp
 from jax import lax
+from jax.experimental import pallas as pl
+from jax.experimental.pallas import tpu as pltpu
 from jax.sharding import PartitionSpec as P
 
 D = 3200
 HEADS = 16
 HEAD_DIM = 128
+BF16 = jnp.bfloat16
+F32 = jnp.float32
 
 
 def merge_layout(grid, token_count, slot_count):
@@ -48,7 +52,261 @@
     return jnp.sum(earlier.astype(jnp.int32), axis=1)
 
 
-def body(tokens, norm_gain, w_qkv, q_gain, k_gain, w_out, grids, owners, proj_gain, proj_bias):
+def dest_tokens(patch_rows, is_live, owners, ranks, capacity, devices_req, first):
+    target = jnp.where(is_live, (owners ^ first) * capacity + ranks, -1)
+    rows = jnp.arange(devices_req * capacity, dtype=jnp.int32)
+    hit = (target[None, :] == rows[:, None]).astype(jnp.int32)
+    return jnp.sum(hit[:, :, None] * (patch_rows[None] + 1), axis=1) - 1
+
+
+def swap(value, axis, bit):
+    count = lax.axis_size(axis)
+    return lax.ppermute(value, axis, [(i, i ^ bit) for i in range(count)])
+
+
+def ring(value):
+    count = lax.axis_size("req")
+    return lax.ppermute(value, "req", [(i, (i + 2) % count) for i in range(count)])
+
+
+def call(kernel, name, out, operands, flops, scalars=0, raw=0, scratch=()):
+    def whole(x):
+        return pl.BlockSpec(x.shape, lambda i: (0,) * len(x.shape))
+
+    blocks = operands[scalars : len(operands) - raw]
+    moved = sum(x.size * x.dtype.itemsize for x in operands[scalars:] + tuple(out))
+    return pl.pallas_call(
+        kernel,
+        grid=(1,),
+        out_shape=tuple(out),
+        in_specs=[pl.BlockSpec(memory_space=pltpu.SMEM)] * scalars
+        + [whole(x) for x in blocks]
+        + [pl.BlockSpec(memory_space=pl.ANY)] * raw,
+        out_specs=tuple(whole(x) for x in out),
+        scratch_shapes=scratch,
+        compiler_params=pltpu.CompilerParams(vmem_limit_bytes=32 << 20),
+        cost_estimate=pl.CostEstimate(flops=flops, bytes_accessed=moved, transcendentals=0),
+        name=name,
+    )(*operands)
+
+
+def array(shape, dtype):
+    return jax.ShapeDtypeStruct(shape, dtype)
+
+
+def split_kernel(w_ref, q_ref, k_ref, v_ref):
+    for head in range(q_ref.shape[1] // HEAD_DIM):
+        to = pl.ds(head * HEAD_DIM, HEAD_DIM)
+        for i, ref in enumerate((q_ref, k_ref, v_ref)):
+            ref[:, to] = w_ref[:, pl.ds((3 * head + i) * HEAD_DIM, HEAD_DIM)]
+
+
+def norm_kernel(side_ref, tokens_ref, gain_ref, mine_ref, others_ref):
+    rows, width = tokens_ref.shape
+    depth = width // 8
+    step = 48
+
+    @pl.loop(0, rows // step)
+    def _(i):
+        at = pl.ds(pl.multiple_of(i * step, step), step)
+        values = tokens_ref[at, :].astype(F32)
+        inverse = lax.rsqrt(jnp.mean(values * values, axis=1, keepdims=True) + 1e-06)
+        normed = values * inverse * gain_ref[...]
+        for plane in range(width // (2 * depth)):
+            low = normed[:, 2 * plane * depth : (2 * plane + 1) * depth]
+            high = normed[:, (2 * plane + 1) * depth : (2 * plane + 2) * depth]
+            to = pl.ds(plane * depth, depth)
+            mine_ref[at, to] = jnp.where(side_ref[0] == 0, low, high).astype(BF16)
+            others_ref[at, to] = jnp.where(side_ref[0] == 0, high, low).astype(BF16)
+        filled = mine_ref.shape[1]
+        others_ref[at, filled:] = jnp.zeros((step, others_ref.shape[1] - filled), BF16)
+
+
+def norm_tokens(side, tokens, norm_gain):
+    rows, columns = tokens.shape[0], tokens.shape[1] // 2
+    out = (array((rows, columns), BF16), array((rows, pl.cdiv(columns, 128) * 128), BF16))
+    return call(norm_kernel, "norm_tokens", out, (side, tokens, norm_gain[None]), 0, scalars=1)
+
+
+def place_blocks(plane, block_refs, weights_ref, sems):
+    count, depth = len(block_refs), block_refs[0].shape[0]
+    copies = []
+    for i, ref in enumerate(block_refs):
+        first = lax.rem(plane + count - i, count) * depth
+        to = weights_ref.at[pl.ds(pl.multiple_of(first, 16), depth), :]
+        copies.append(pltpu.make_async_copy(ref, to, sems.at[i]))
+    for copy in copies:
+        copy.start()
+    for copy in copies:
+        copy.wait()
+
+
+def project_kernel(plane_ref, mine_ref, theirs_ref, *refs):
+    *block_refs, own_ref, peer_ref, weights_ref, sems = refs
+    place_blocks(plane_ref[0], block_refs, weights_ref, sems)
+    weights = weights_ref[...]
+    theirs = theirs_ref[:, : weights.shape[0]]
+    peer_ref[...] = jnp.dot(theirs, weights, preferred_element_type=F32).astype(BF16)
+    own_ref[...] = jnp.dot(mine_ref[...], weights, preferred_element_type=F32)
+
+
+def project(plane, mine, theirs, blocks):
+    rows, columns = mine.shape[0], blocks[0].shape[1]
+    depth = blocks[0].shape[0] * len(blocks)
+    return call(
+        project_kernel,
+        "project",
+        (array((rows, columns), F32), array((rows, columns), BF16)),
+        (plane, mine, theirs, *blocks),
+        4 * rows * depth * columns,
+        scalars=1,
+        raw=len(blocks),
+        scratch=(
+            pltpu.VMEM((depth, columns), BF16),
+            pltpu.SemaphoreType.DMA((len(blocks),)),
+        ),
+    )
+
+
+def scores_kernel(q_ref, q_got_ref, k_ref, k_got_ref, q_gain_ref, k_gain_ref, raw_ref, sums_ref):
+    queries = q_ref[...] + q_got_ref[...].astype(F32)
+    key_vecs = k_ref[...] + k_got_ref[...].astype(F32)
+    sums_ref[:, 0:1] = jnp.sum(queries * queries, axis=1, keepdims=True)
+    sums_ref[:, 1:2] = jnp.sum(key_vecs * key_vecs, axis=1, keepdims=True)
+    queries = queries * (q_gain_ref[...] * (1.0 / math.sqrt(HEAD_DIM)))
+    key_vecs = key_vecs * k_gain_ref[...]
+    for head in range(raw_ref.shape[0]):
+        part = slice(head * HEAD_DIM, (head + 1) * HEAD_DIM)
+        raw_ref[head] = lax.dot_general(
+            queries[:, part],
+            key_vecs[:, part],
+            (((1,), (1,)), ((), ())),
+            precision=lax.Precision.HIGHEST,
+            preferred_element_type=F32,
+        )
+
+
+def attend_kernel(raw_ref, q_scale_ref, k_scale_ref, seg_ref, seg_row_ref, v_ref, v_got_ref, out_ref):
+    same = seg_ref[...] == seg_row_ref[...]
+    values = (v_ref[...] + v_got_ref[...].astype(F32)).astype(BF16)
+    for head in range(raw_ref.shape[0]):
+        part = slice(head * HEAD_DIM, (head + 1) * HEAD_DIM)
+        scores = raw_ref[head] * q_scale_ref[...] * k_scale_ref[...]
+        scores = jnp.where(same, scores, -1e30)
+        raised = jnp.exp(scores - jnp.max(scores, axis=1, keepdims=True))
+        probs = (raised / jnp.sum(raised, axis=1, keepdims=True)).astype(BF16)
+        out_ref[:, part] = jnp.dot(
+            probs, values[:, part], preferred_element_type=F32
+        ).astype(BF16)
+
+
+def project_out_kernel(place_ref, attended_ref, *refs):
+    *block_refs, sent_ref, kept_far_ref, kept_ref, weights_ref, sems = refs
+    depth = block_refs[0].shape[0]
+    place_blocks(place_ref[0], block_refs, weights_ref, sems)
+    column = place_ref[2]
+    attended = attended_ref[...]
+
+    def term(index):
+        rows = weights_ref[pl.ds(pl.multiple_of(index * depth, 16), depth), :]
+        return lax.dot_general(
+            rows, attended, (((1,), (1,)), ((), ())), preferred_element_type=F32
+        )
+
+    sent_ref[0] = term(column ^ 3).astype(BF16)
+    sent_ref[1] = term(column ^ 1).astype(BF16)
+    kept_far_ref[...] = term(column ^ 2)
+    kept_ref[...] = term(column)
+
+
+def project_out(place, attended, blocks):
+    rows = attended.shape[0]
+    depth, width = blocks[0].shape
+    kept = array((depth, rows), F32)
+    return call(
+        project_out_kernel,
+        "project_out",
+        (array((2, depth, rows), BF16), kept, kept),
+        (place, attended, *blocks),
+        2 * rows * depth * width * len(blocks),
+        scalars=1,
+        raw=len(blocks),
+        scratch=(
+            pltpu.VMEM((depth * len(blocks), width), BF16),
+            pltpu.SemaphoreType.DMA((len(blocks),)),
+        ),
+    )
+
+
+def far_kernel(kept_ref, near_ref, far_ref):
+    far_ref[...] = (kept_ref[...] + near_ref[0].astype(F32)).astype(BF16)
+
+
+def pack_kernel(kept_ref, near_ref, far_ref, token_ref, chosen_ref, sums_ref, *block_refs):
+    attn_out = kept_ref[...] + near_ref[1].astype(F32) + far_ref[...].astype(F32)
+    hidden = (token_ref[...].astype(F32) + attn_out).astype(BF16)
+    depth = hidden.shape[0]
+    rows = block_refs[0].shape[0]
+    for patch in range(4):
+        first = patch * rows * len(block_refs)
+        picked = lax.dot_general(
+            chosen_ref[pl.ds(first, rows * len(block_refs)), :],
+            hidden,
+            (((1,), (1,)), ((), ())),
+            preferred_element_type=F32,
+        )
+        for i, ref in enumerate(block_refs):
+            part = picked[i * rows : (i + 1) * rows]
+            ref[:, pl.ds(patch * depth, depth)] = part.astype(BF16)
+    hidden = hidden.astype(F32)
+    sums_ref[0:1, :] = jnp.sum(hidden, axis=0, keepdims=True)
+    sums_ref[1:2, :] = jnp.sum(hidden * hidden, axis=0, keepdims=True)
+
+
+def pack(kept, near, far, token_part, chosen, count):
+    depth, token_count = far.shape
+    rows = chosen.shape[0] // 4 // count
+    out = (array((2, token_count), F32),) + (array((rows, 4 * depth), BF16),) * count
+    operands = (kept, near, far, token_part, chosen)
+    return call(pack_kernel, "pack", out, operands, 2 * chosen.size * depth)
+
+
+def finish_kernel(place_ref, stats_ref, gain_ref, bias_ref, *refs):
+    out_ref = refs[-1]
+    count = (len(refs) - 1) // 2
+    rows, _, quarter = out_ref.shape
+    rows = rows // count
+    depth = quarter // 2
+    for i in range(count):
+        source = place_ref[0] ^ i
+        to = pl.ds(source * rows, rows)
+        swapped = (source & 1) == 1
+        scale, shift, live = (stats_ref[j, to][:, 0:1] for j in range(3))
+        for patch in range(4):
+            part = slice(patch * depth, (patch + 1) * depth)
+            own = refs[i][:, part].astype(F32)
+            other = refs[count + i][:, part].astype(F32)
+            values = jnp.concatenate(
+                [jnp.where(swapped, other, own), jnp.where(swapped, own, other)], axis=1
+            )
+            gain, bias = gain_ref[patch : patch + 1, :], bias_ref[patch : patch + 1, :]
+            values = (values * scale + shift) * gain + live * bias
+            out_ref[to, patch, :] = values.astype(BF16)
+
+
+def finish(me, stats, proj_gain, proj_bias, blocks):
+    rows = stats.shape[1]
+    stats = jnp.broadcast_to(stats[:, :, None], (3, rows, 128))
+    out = array((rows,) + proj_gain.shape, BF16)
+    operands = (me.reshape(1), stats, proj_gain, proj_bias) + tuple(blocks)
+    return call(finish_kernel, "finish", (out,), operands, 6 * out.size, scalars=1)[0]
+
+
+def after(value, *first):
+    return lax.optimization_barrier((value,) + first)[0]
+
+
+def general_body(tokens, norm_gain, w_qkv, q_gain, k_gain, w_out, grids, owners, proj_gain, proj_bias):
     token_count = tokens.shape[0]
     slot_count = owners.shape[0]
     quarter = proj_gain.shape[1]
@@ -129,6 +387,109 @@
     return result
 
 
+def body(tokens, norm_gain, w_qkv, q_gain, k_gain, w_out, grids, owners, proj_gain, proj_bias):
+    token_count = tokens.shape[0]
+    slot_count = owners.shape[0]
+    quarter = proj_gain.shape[1]
+    head_share = q_gain.shape[0]
+    head_count = head_share // HEAD_DIM
+    head_width = HEADS * HEAD_DIM
+    feature_total = 4 * D
+    devices_req = lax.axis_size("req")
+    devices_tp = lax.axis_size("tp")
+    planes = devices_req // 2
+    capacity = max(2, (2 * slot_count + devices_req - 1) // devices_req)
+    me = lax.axis_index("req")
+    plane, side = me // 2, me % 2
+    column = lax.axis_index("tp")
+    token_ids = jnp.arange(token_count, dtype=jnp.int32)
+
+    part = array((w_qkv.shape[0], head_share), BF16)
+    w_q, w_k, w_v = call(split_kernel, "split_heads", (part,) * 3, (w_qkv,), 0)
+    w_o = w_out.T
+    q_blocks, k_blocks = [w_q], [w_k]
+    for step in range(1, planes):
+        q_blocks.append(ring(q_blocks[-1]))
+        k_blocks.append(ring(k_blocks[-1]))
+    v_blocks, o_blocks = [after(w_v, k_blocks[-2])], [after(w_o, q_blocks[-1])]
+    for step in range(1, planes):
+        v_blocks.append(ring(v_blocks[-1]))
+        o_blocks.append(ring(o_blocks[-1]))
+
+    patch_rows, is_live, segment = merge_layout(grids, token_count, slot_count)
+    ranks = owner_ranks(owners, is_live)
+    placing = (patch_rows, is_live, owners, ranks, capacity, devices_req)
+    sent_tokens = dest_tokens(*placing, me)
+    chosen = (sent_tokens.T.reshape(-1)[:, None] == token_ids[None, :]).astype(BF16)
+    row_tokens = dest_tokens(*placing, 0)
+    in_row = jnp.any(row_tokens[:, :, None] == token_ids[None, None, :], axis=1).astype(F32)
+    row_live = (row_tokens[:, 0] >= 0).astype(F32)
+    token_mine = lax.dynamic_slice_in_dim(tokens, column * quarter, quarter, 1).T
+    token_mine = token_mine.reshape(2, quarter // 2, token_count)
+
+    places = jnp.stack([plane, side, column]).astype(jnp.int32)
+    mine, others = norm_tokens(places[1:2], tokens, norm_gain)
+    theirs = swap(others, "req", 1)
+
+    def projected(blocks):
+        own, peer = project(places[0:1], mine, theirs, blocks)
+        return own, swap(peer, "req", 1)
+
+    queries = projected(q_blocks)
+    key_vecs = projected(k_blocks)
+    values = projected(v_blocks)
+    raw, sums = call(
+        scores_kernel,
+        "scores",
+        (
+            array((head_count, token_count, token_count), F32),
+            array((token_count, 2), F32),
+        ),
+        (after(queries[0], values[0]), queries[1], *key_vecs, q_gain[None], k_gain[None]),
+        12 * token_count * token_count * head_share,
+    )
+    sums = after(sums, o_blocks[-2])
+    scales = lax.rsqrt(lax.psum(sums.T, "tp") / head_width + 1e-06)
+    (attended,) = call(
+        attend_kernel,
+        "attend",
+        (array((token_count, head_share), BF16),),
+        (
+            after(raw, o_blocks[-1]),
+            scales[0][:, None],
+            scales[1][None],
+            segment[:, None],
+            segment[None],
+            *values,
+        ),
+        2 * token_count * token_count * head_share,
+    )
+
+    halves, token_sums = [], 0.0
+    others_blocks = [swap(block, "req", 1) for block in o_blocks]
+    for half, blocks in ((side, o_blocks), (1 - side, others_blocks)):
+        sent, kept_far, kept = project_out(places, attended, blocks)
+        near = swap(sent, "tp", 1)
+        (far,) = call(far_kernel, "far_sum", (array(kept.shape, BF16),), (kept_far, near), 0)
+        far = swap(far, "tp", 2)
+        token_part = lax.dynamic_index_in_dim(token_mine, half, 0, keepdims=False)
+        sums, *blocks = pack(kept, near, far, token_part, chosen, devices_req)
+        for bits in reversed(range(1, devices_req)):
+            blocks[bits] = swap(blocks[bits], "req", bits)
+        halves += blocks
+        token_sums = token_sums + sums
+
+    token_sums = token_sums + sum(swap(token_sums, "tp", bit) for bit in range(1, devices_tp))
+    row_sums = jnp.sum(in_row[None] * token_sums[:, None, :], axis=2)
+    mean_value = row_sums[0] / feature_total
+    variance = row_sums[1] / feature_total - mean_value * mean_value
+    inverse = lax.rsqrt(variance + 1e-05) * row_live
+    stats = jnp.stack([inverse, -mean_value * inverse, row_live]).reshape(3, devices_req, capacity)
+    stats = lax.all_to_all(stats, "req", split_axis=1, concat_axis=1, tiled=True)
+    stats = stats.reshape(3, devices_req * capacity)
+    return finish(me, stats, proj_gain, proj_bias, halves)
+
+
 def solution(mesh):
     placed = (
         P("req", None),
@@ -142,6 +503,8 @@
         P(None, "tp"),
         P(None, "tp"),
     )
+    planes, odd = divmod(mesh.shape["req"], 2)
+    fits = not odd and planes == mesh.shape["tp"] == 4
     return jax.shard_map(
-        body, mesh=mesh, in_specs=placed, out_specs=P("req", None, "tp"), check_vma=False
-    )
+        body if fits else general_body, mesh=mesh, in_specs=placed, out_specs=P("req", None, "tp"), check_vma=False
+    )

time: 330 us -> 216 us (0.65)
  waiting for transfers between devices: 237 us -> 101 us
  starting transfers between devices: 9.14 us -> 42.8 us
  Pallas kernels: 0 us -> 32.9 us
  matrix products: 20.3 us -> 0 us
  between operations: 13.3 us -> 0.55 us
  local copies, waits for them, and re-layouts: 25.4 us -> 17.1 us
  other arithmetic: 11.8 us -> 4.4 us
  blocking collectives: 12.6 us -> 16.6 us
    all_gather x2 -> x0, waiting for transfers between devices: 179 us -> none  [the longest x1 142 us: body(): lax.all_gather(w_qkv, 'req', axis=0, tiled=True)]
    ppermute x0 -> x41, waiting for transfers between devices: none -> 101 us  [the longest x12 76.2 us: ring(): lax.ppermute(value, 'req', [(i, (i + 2) % count) for i in range(count)])]
    ppermute x0 -> x41, starting transfers between devices: none -> 42.8 us  [the longest x29 36.6 us: swap(): return lax.ppermute(value, axis, [(i, i ^ bit) for i in range(count)])]
    pallas_call x0 -> x14, Pallas kernels: none -> 32.9 us  [call(): pl.pallas_call(kernel, grid=(1,), out_shape=tuple(out), in_specs=[pl.Bloc...]
    all_to_all x2 -> x0, waiting for transfers between devices: 32.5 us -> none  [the longest x1 32.5 us: body(): lax.all_to_all(send_slots, 'req', split_axis=0, concat_axis=0, tiled=True)]
    reduce_scatter x1 -> x0, waiting for transfers between devices: 24.3 us -> none  [body(): lax.psum_scatter(partial_sum.astype(jnp.bfloat16), 'tp', scatter_dimensio...]
    dot_general x4 -> x0, matrix products: 20.3 us -> none  [the longest x1 8.42 us: body(): jnp.dot(normed, lax.all_gather(w_qkv, 'req', axis=0, tiled=True), preferr...]
    scatter x1 -> x0, local copies, waits for them, and re-layouts: 12.7 us -> none  [body(): send_slots = send_slots.at[target_owner, ranks].set(merged, mode='drop')]
  transfers between devices with their start and end apart: 5 -> 41, of which waited for: 4 -> 17; matrix products, arithmetic and copies ran while one was open for 14% -> 6% of each run, Pallas kernels for 0% -> 13%
where the time goes in v3:
time: 216 us; the launch traced here: 215 us
  waiting for transfers between devices  101 us (47%)
  starting transfers between devices  42.8 us (20%)
  Pallas kernels  32.9 us (15%)
  local copies, waits for them, and re-layouts  17.1 us (8%)
  blocking collectives  16.6 us (8%)
  other arithmetic  4.4 us (2%)
    ppermute x12, waiting for transfers between devices, ring(): lax.ppermute(value, 'req', [(i, (i + 2) % count) for i in range(count)])  76.2 us
    ppermute x29, starting transfers between devices, swap(): return lax.ppermute(value, axis, [(i, i ^ bit) for i in range(count)])  36.6 us
    pallas_call x14, Pallas kernels, call(): pl.pallas_call(kernel, grid=(1,), out_shape=tuple(out), in_specs=[pl.Bloc...  32.9 us
    ppermute x29, waiting for transfers between devices, swap(): return lax.ppermute(value, axis, [(i, i ^ bit) for i in range(count)])  24.4 us
    unnamed x63, local copies, waits for them, and re-layouts  11.5 us
    all_to_all x1, blocking collectives, body(): lax.all_to_all(stats, 'req', split_axis=1, concat_axis=1, tiled=True)  10.4 us
    psum x1, blocking collectives, body(): scales = lax.rsqrt(lax.psum(sums.T, 'tp') / head_width + 1e-06)  6.21 us
    ppermute x12, starting transfers between devices, ring(): lax.ppermute(value, 'req', [(i, (i + 2) % count) for i in range(count)])  6.18 us
  transfers between devices with their start and end apart: 41, of which 17 were waited for; matrix products, arithmetic and copies ran while one was open for 6% of the time, Pallas kernels for 13%

profile of v3, /device:TPU:0, one launch (start us, length us, event | category | flops | bytes accessed | tf_op | source)
XLA Modules:
  0.0 214.8 jit_solution(9746458226756611481)
XLA Ops:
  2.3 3.0 %collective-permute-start.1 = (bf16[400,512]{1,0:T(8,128)(2,1)S(1)}, bf16[400,512]{1,0:T(8,128)(2,1)}, u32[]{:S(2)}, u32[]{:S(2)}) collective-permute-start(bf16[400,512]{1,0:T(8,128)(2,1)S(1)} %get-tuple-element.49.refs_0_), channel_id=1, source_target_pairs={{0,8},{4,12},{8,16},{12,20},{16,24},{20,28},{24,0},{28,4},{1,9},{5... | collective-permute-start | bytes 1228808 | tf_op jit(solution)/shard_map/ppermute | solution.py:69
  7.7 4.3 %norm_tokens.1 = (bf16[384,1600]{1,0:T(8,128)(2,1)S(1)}, bf16[384,1664]{1,0:T(8,128)(2,1)}) custom-call(s32[1]{0:T(128)} %bitcast.8.side_ref, bf16[384,3200]{1,0:T(8,128)(2,1)S(1)} %copy-done, f32[1,3200]{1,0:T(1,128)S(1)} %broadcast_in_dim.36.gain_ref), custom_call_target="tpu_custom_call" | custom-call | bytes 4977152 | tf_op jit(solution)/shard_map/norm_tokens/pallas_call | solution.py:78
  17.2 10.8 %collective-permute-done.4.refs_1_ = bf16[400,512]{1,0:T(8,128)(2,1)} collective-permute-done((bf16[400,512]{1,0:T(8,128)(2,1)}, bf16[400,512]{1,0:T(8,128)(2,1)}, u32[]{:S(2)}, u32[]{:S(2)}) %collective-permute-start.4) | collective-permute-done | bytes 409632 | tf_op jit(solution)/shard_map/ppermute | solution.py:69
  28.1 8.7 %collective-permute-done.2.refs_2_ = bf16[400,512]{1,0:T(8,128)(2,1)S(1)} collective-permute-done((bf16[400,512]{1,0:T(8,128)(2,1)}, bf16[400,512]{1,0:T(8,128)(2,1)S(1)}, u32[]{:S(2)}, u32[]{:S(2)}) %collective-permute-start.2) | collective-permute-done | bytes 409632 | tf_op jit(solution)/shard_map/ppermute | solution.py:69
  38.2 7.4 %collective-permute-done.5.refs_2_ = bf16[400,512]{1,0:T(8,128)(2,1)} collective-permute-done((bf16[400,512]{1,0:T(8,128)(2,1)}, bf16[400,512]{1,0:T(8,128)(2,1)}, u32[]{:S(2)}, u32[]{:S(2)}) %collective-permute-start.5) | collective-permute-done | bytes 409632 | tf_op jit(solution)/shard_map/ppermute | solution.py:69
  45.7 8.6 %collective-permute-done.3.refs_3_ = bf16[400,512]{1,0:T(8,128)(2,1)S(1)} collective-permute-done((bf16[400,512]{1,0:T(8,128)(2,1)S(1)}, bf16[400,512]{1,0:T(8,128)(2,1)S(1)}, u32[]{:S(2)}, u32[]{:S(2)}) %collective-permute-start.3) | collective-permute-done | bytes 409632 | tf_op jit(solution)/shard_map/ppermute | solution.py:69
  56.6 2.3 %constant_dynamic-slice_fusion = bf16[384,800]{1,0:T(8,128)(2,1)} fusion(bf16[384,3200]{1,0:T(8,128)(2,1)} %tokens_ref.1, s32[]{:T(128)S(6)} %select_n.137), kind=kLoop, calls=%fused_computation.42 | loop fusion | bytes 1228804 | tf_op jit(solution)/shard_map/dynamic_slice | solution.py:427
  59.0 4.2 %collective-permute-done.6.refs_1_ = bf16[400,512]{1,0:T(8,128)(2,1)} collective-permute-done((bf16[400,512]{1,0:T(8,128)(2,1)S(1)}, bf16[400,512]{1,0:T(8,128)(2,1)}, u32[]{:S(2)}, u32[]{:S(2)}) %collective-permute-start.6) | collective-permute-done | bytes 409632 | tf_op jit(solution)/shard_map/ppermute | solution.py:69
  63.2 8.8 %collective-permute-done.12.refs_1_ = bf16[400,512]{1,0:T(8,128)(2,1)} collective-permute-done((bf16[400,512]{1,0:T(8,128)(2,1)}, bf16[400,512]{1,0:T(8,128)(2,1)}, u32[]{:S(2)}, u32[]{:S(2)}) %collective-permute-start.12) | collective-permute-done | bytes 409632 | tf_op jit(solution)/shard_map/ppermute | solution.py:69
  72.0 8.6 %collective-permute-done.10.refs_3_ = bf16[400,512]{1,0:T(8,128)(2,1)S(1)} collective-permute-done((bf16[400,512]{1,0:T(8,128)(2,1)}, bf16[400,512]{1,0:T(8,128)(2,1)S(1)}, u32[]{:S(2)}, u32[]{:S(2)}) %collective-permute-start.10) | collective-permute-done | bytes 409632 | tf_op jit(solution)/shard_map/ppermute | solution.py:69
  80.6 3.4 %project.5 = (f32[384,512]{1,0:T(8,128)S(1)}, bf16[384,512]{1,0:T(8,128)(2,1)S(1)}) custom-call(s32[1]{0:T(128)} %bitcast.7.plane_ref, bf16[384,1600]{1,0:T(8,128)(2,1)S(1)} %get-tuple-element.47.mine_ref, bf16[384,1664]{1,0:T(8,128)(2,1)S(1)} %collective-permute-done.theirs_ref, bf16[400,512]{1,0:T(8,128)(2,1)} %get-tuple-element.52.refs_0_, ...), custom_call_target="tpu_custom_call" | custom-call | flops 1258291200 | bytes 5324800 | tf_op jit(solution)/shard_map/project/pallas_call | solution.py:78
  84.6 4.8 %collective-permute-done.7.refs_2_ = bf16[400,512]{1,0:T(8,128)(2,1)S(1)} collective-permute-done((bf16[400,512]{1,0:T(8,128)(2,1)}, bf16[400,512]{1,0:T(8,128)(2,1)S(1)}, u32[]{:S(2)}, u32[]{:S(2)}) %collective-permute-start.7) | collective-permute-done | bytes 409632 | tf_op jit(solution)/shard_map/ppermute | solution.py:69
  89.4 2.8 %project.3 = (f32[384,512]{1,0:T(8,128)S(1)}, bf16[384,512]{1,0:T(8,128)(2,1)S(1)}) custom-call(s32[1]{0:T(128)} %bitcast.7.plane_ref, bf16[384,1600]{1,0:T(8,128)(2,1)S(1)} %get-tuple-element.47.mine_ref, bf16[384,1664]{1,0:T(8,128)(2,1)S(1)} %collective-permute-done.theirs_ref, bf16[400,512]{1,0:T(8,128)(2,1)S(1)} %get-tuple-element.49.refs_0_, ...), custom_call_target="tpu_custom_call" | custom-call | flops 1258291200 | bytes 5324800 | tf_op jit(solution)/shard_map/project/pallas_call | solution.py:78
  93.1 5.2 %collective-permute-done.13.refs_2_ = bf16[400,512]{1,0:T(8,128)(2,1)} collective-permute-done((bf16[400,512]{1,0:T(8,128)(2,1)}, bf16[400,512]{1,0:T(8,128)(2,1)}, u32[]{:S(2)}, u32[]{:S(2)}) %collective-permute-start.13) | collective-permute-done | bytes 409632 | tf_op jit(solution)/shard_map/ppermute | solution.py:69
  99.4 7.6 %collective-permute-done.8.refs_3_ = bf16[400,512]{1,0:T(8,128)(2,1)S(1)} collective-permute-done((bf16[400,512]{1,0:T(8,128)(2,1)S(1)}, bf16[400,512]{1,0:T(8,128)(2,1)S(1)}, u32[]{:S(2)}, u32[]{:S(2)}) %collective-permute-start.8) | collective-permute-done | bytes 409632 | tf_op jit(solution)/shard_map/ppermute | solution.py:69
  108.8 2.8 %project.4 = (f32[384,512]{1,0:T(8,128)S(1)}, bf16[384,512]{1,0:T(8,128)(2,1)S(1)}) custom-call(s32[1]{0:T(128)} %bitcast.7.plane_ref, bf16[384,1600]{1,0:T(8,128)(2,1)S(1)} %get-tuple-element.47.mine_ref, bf16[384,1664]{1,0:T(8,128)(2,1)S(1)} %copy-done.9, bf16[400,512]{1,0:T(8,128)(2,1)S(1)} %copy-done.11, ...), custom_call_target="tpu_custom_call" | custom-call | flops 1258291200 | bytes 5324800 | tf_op jit(solution)/shard_map/project/pallas_call | solution.py:78
  116.6 6.2 %psum.7 = f32[2,384]{1,0:T(2,128)S(1)} all-reduce(f32[2,384]{1,0:T(2,128)S(1)} %bitcast.72), channel_id=1, replica_groups=mesh['req'=8,'tp'=4] {'tp'}, use_global_device_ids=true, to_apply=%region_7.8 | all-reduce | flops 768 | bytes 6144 | tf_op jit(solution)/shard_map/psum | solution.py:452
  124.5 4.3 %collective-permute-done.15.v_got_ref = bf16[384,512]{1,0:T(8,128)(2,1)} collective-permute-done((bf16[384,512]{1,0:T(8,128)(2,1)}, bf16[384,512]{1,0:T(8,128)(2,1)}, u32[]{:S(2)}, u32[]{:S(2)}) %collective-permute-start.15) | collective-permute-done | bytes 393248 | tf_op jit(solution)/shard_map/ppermute | solution.py:64
  128.8 2.7 %attend.1.attended_ref = bf16[384,512]{1,0:T(8,128)(2,1)S(1)} custom-call(f32[4,384,384]{2,1,0:T(8,128)S(1)} %get-tuple-element.61.raw_ref, f32[384,1]{1,0:T(8,128)S(1)} %copy.36.q_scale_ref, f32[1,384]{1,0:T(1,128)S(1)} %get-tuple-element.101.k_scale_ref, s32[384,1]{1,0:T(8,128)S(1)} %broadcast_in_dim.43.seg_ref, ...), custom_call_target="tpu_custom_call" | custom-call | flops 150994944 | bytes 3938304 | tf_op jit(solution)/shard_map/attend/pallas_call | solution.py:78
  131.5 3.4 %project_out.2 = (bf16[2,400,384]{2,1,0:T(8,128)(2,1)}, f32[400,384]{1,0:T(8,128)S(1)}, f32[400,384]{1,0:T(8,128)S(1)}) custom-call(s32[3]{0:T(128)S(1)} %pad_add_fusion.place_ref, bf16[384,512]{1,0:T(8,128)(2,1)S(1)} %attend.1.attended_ref, bf16[400,512]{1,0:T(8,128)(2,1)} %bitcast.12.refs_0_, bf16[400,512]{1,0:T(8,128)(2,1)} %collective-permute-done.12.refs_1_, ...), custom_call_target="tpu_custom_call" | custom-call | flops 629145600 | bytes 3874816 | tf_op jit(solution)/shard_map/project_out/pallas_call | solution.py:78
  137.6 6.3 %collective-permute-done.21.refs_3_ = bf16[400,512]{1,0:T(8,128)(2,1)} collective-permute-done((bf16[400,512]{1,0:T(8,128)(2,1)}, bf16[400,512]{1,0:T(8,128)(2,1)}, u32[]{:S(2)}, u32[]{:S(2)}) %collective-permute-start.21) | collective-permute-done | bytes 409632 | tf_op jit(solution)/shard_map/ppermute | solution.py:64
  143.9 3.5 %project_out.3 = (bf16[2,400,384]{2,1,0:T(8,128)(2,1)}, f32[400,384]{1,0:T(8,128)S(1)}, f32[400,384]{1,0:T(8,128)S(1)}) custom-call(s32[3]{0:T(128)S(1)} %pad_add_fusion.place_ref, bf16[384,512]{1,0:T(8,128)(2,1)S(1)} %attend.1.attended_ref, bf16[400,512]{1,0:T(8,128)(2,1)} %collective-permute-done.18.refs_0_, ...), custom_call_target="tpu_custom_call" | custom-call | flops 629145600 | bytes 3874816 | tf_op jit(solution)/shard_map/project_out/pallas_call | solution.py:78
  148.6 2.2 %copy.43 = bf16[384,800]{0,1:T(8,128)(2,1)} copy(bf16[384,800]{1,0:T(8,128)(2,1)} %constant_dynamic-slice_fusion) | data formatting | bytes 1228800
  157.8 6.5 %collective-permute-done.17.far_ref = bf16[400,384]{1,0:T(8,128)(2,1)} collective-permute-done((bf16[400,384]{1,0:T(8,128)(2,1)}, bf16[400,384]{1,0:T(8,128)(2,1)}, u32[]{:S(2)}, u32[]{:S(2)}) %collective-permute-start.17) | collective-permute-done | bytes 307232 | tf_op jit(solution)/shard_map/ppermute | solution.py:64
  166.1 4.3 %collective-permute-done.23.far_ref = bf16[400,384]{1,0:T(8,128)(2,1)S(1)} collective-permute-done((bf16[400,384]{1,0:T(8,128)(2,1)}, bf16[400,384]{1,0:T(8,128)(2,1)S(1)}, u32[]{:S(2)}, u32[]{:S(2)}) %collective-permute-start.23) | collective-permute-done | bytes 307232 | tf_op jit(solution)/shard_map/ppermute | solution.py:64
  176.7 2.2 %collective-permute-start.30 = (bf16[24,1600]{1,0:T(8,128)(2,1)}, bf16[24,1600]{1,0:T(8,128)(2,1)S(1)}, u32[]{:S(2)}, u32[]{:S(2)}) collective-permute-start(bf16[24,1600]{1,0:T(8,128)(2,1)} %copy-done.19), channel_id=1, source_target_pairs={{0,16},{4,20},{8,24},{12,28},{16,0},{20,4},{24,8},{28,12},{1,17},{... | collective-permute-start | bytes 230408 | tf_op jit(solution)/shard_map/ppermute | solution.py:64
  180.3 3.4 %collective-permute-start.32 = (bf16[24,1600]{1,0:T(8,128)(2,1)}, bf16[24,1600]{1,0:T(8,128)(2,1)S(1)}, u32[]{:S(2)}, u32[]{:S(2)}) collective-permute-start(bf16[24,1600]{1,0:T(8,128)(2,1)} %copy-done.17), channel_id=1, source_target_pairs={{0,24},{4,28},{8,16},{12,20},{16,8},{20,12},{24,0},{28,4},{1,25},{... | collective-permute-start | bytes 230408 | tf_op jit(solution)/shard_map/ppermute | solution.py:64
  185.7 3.6 %collective-permute-start.35 = (bf16[24,1600]{1,0:T(8,128)(2,1)S(1)}, bf16[24,1600]{1,0:T(8,128)(2,1)S(1)}, u32[]{:S(2)}, u32[]{:S(2)}) collective-permute-start(bf16[24,1600]{1,0:T(8,128)(2,1)S(1)} %get-tuple-element.83), channel_id=1, source_target_pairs={{0,8},{4,12},{8,0},{12,4},{16,24},{20,28},{24,16},{28,20},{1,9},{5... | collective-permute-start | bytes 230408 | tf_op jit(solution)/shard_map/ppermute | solution.py:64
  192.6 2.5 %collective-permute-start.37 = (bf16[24,1600]{1,0:T(8,128)(2,1)S(1)}, bf16[24,1600]{1,0:T(8,128)(2,1)S(1)}, u32[]{:S(2)}, u32[]{:S(2)}) collective-permute-start(bf16[24,1600]{1,0:T(8,128)(2,1)S(1)} %get-tuple-element.85), channel_id=1, source_target_pairs={{0,16},{4,20},{8,24},{12,28},{16,0},{20,4},{24,8},{28,12},{1,17},{... | collective-permute-start | bytes 230408 | tf_op jit(solution)/shard_map/ppermute | solution.py:64
  195.2 2.7 %collective-permute-start.38 = (bf16[24,1600]{1,0:T(8,128)(2,1)S(1)}, bf16[24,1600]{1,0:T(8,128)(2,1)S(1)}, u32[]{:S(2)}, u32[]{:S(2)}) collective-permute-start(bf16[24,1600]{1,0:T(8,128)(2,1)S(1)} %get-tuple-element.86), channel_id=1, source_target_pairs={{0,20},{4,16},{8,28},{12,24},{16,4},{20,0},{24,12},{28,8},{1,21},{... | collective-permute-start | bytes 230408 | tf_op jit(solution)/shard_map/ppermute | solution.py:64
  201.2 10.4 %all_to_all.5 = f32[3,8,24]{2,0,1:T(4,128)S(1)} all-to-all(f32[3,8,24]{2,0,1:T(4,128)S(1)} %pad_maximum_fusion), channel_id=1, replica_groups=mesh['req'=8,'tp'=4] {'req'}, dimensions={1} | all-to-all | bytes 4608 | tf_op jit(solution)/shard_map/all_to_all | solution.py:488
  211.9 2.9 %finish.1 = bf16[192,4,800]{2,1,0:T(4,128)(2,1)} custom-call(s32[1]{0:T(128)} %bitcast.place_ref, f32[3,192,128]{2,1,0:T(8,128)S(1)} %broadcast_in_dim.42.stats_ref, f32[4,800]{1,0:T(4,128)S(1)} %copy-done.6, f32[4,800]{1,0:T(4,128)S(1)} %copy-done.7, bf16[24,1600]{1,0:T(8,128)(2,1)S(1)} %get-tuple-element.73.refs_0_, ...), custom_call_target="tpu_custom_call" | custom-call | flops 3686400 | bytes 2778112 | tf_op jit(solution)/shard_map/finish/pallas_call | solution.py:78
  (172 shorter events, 53.9 us)
Async XLA Ops:
  2.3 14.6 %collective-permute-start.1 = (bf16[400,512]{1,0:T(8,128)(2,1)S(1)}, bf16[400,512]{1,0:T(8,128)(2,1)}, u32[]{:S(2)}, u32[]{:S(2)}) collective-permute-start(bf16[400,512]{1,0:T(8,128)(2,1)S(1)} %get-tuple-element.49.refs_0_), channel_id=1, source_target_pairs={{0,8},{4,12},{8,16},{12,20},{16,24},{20,28},{24,0},{28,4},{1,9},{5... | collective-permute-start | bytes 1228808 | tf_op jit(solution)/shard_map/ppermute | solution.py:69
  12.0 68.6 %collective-permute-start = (bf16[384,1664]{1,0:T(8,128)(2,1)}, bf16[384,1664]{1,0:T(8,128)(2,1)S(1)}, u32[]{:S(2)}, u32[]{:S(2)}) collective-permute-start(bf16[384,1664]{1,0:T(8,128)(2,1)} %get-tuple-element.48), channel_id=1, source_target_pairs={{0,4},{4,0},{8,12},{12,8},{16,20},{20,16},{24,28},{28,24},{1,5},{5... | collective-permute-start | bytes 3833864 | tf_op jit(solution)/shard_map/ppermute | solution.py:64
  13.6 14.5 %collective-permute-start.4 = (bf16[400,512]{1,0:T(8,128)(2,1)}, bf16[400,512]{1,0:T(8,128)(2,1)}, u32[]{:S(2)}, u32[]{:S(2)}) collective-permute-start(bf16[400,512]{1,0:T(8,128)(2,1)} %get-tuple-element.52.refs_0_), channel_id=1, source_target_pairs={{0,8},{4,12},{8,16},{12,20},{16,24},{20,28},{24,0},{28,4},{1,9},{5... | collective-permute-start | bytes 1228808 | tf_op jit(solution)/shard_map/ppermute | solution.py:69
  16.9 19.9 %collective-permute-start.2 = (bf16[400,512]{1,0:T(8,128)(2,1)}, bf16[400,512]{1,0:T(8,128)(2,1)S(1)}, u32[]{:S(2)}, u32[]{:S(2)}) collective-permute-start(bf16[400,512]{1,0:T(8,128)(2,1)} %collective-permute-done.1.refs_1_), channel_id=1, source_target_pairs={{0,8},{4,12},{8,16},{12,20},{16,24},{20,28},{24,0},{28,4},{1,9},{5... | collective-permute-start | bytes 1228808 | tf_op jit(solution)/shard_map/ppermute | solution.py:69
  28.1 17.6 %collective-permute-start.5 = (bf16[400,512]{1,0:T(8,128)(2,1)}, bf16[400,512]{1,0:T(8,128)(2,1)}, u32[]{:S(2)}, u32[]{:S(2)}) collective-permute-start(bf16[400,512]{1,0:T(8,128)(2,1)} %collective-permute-done.4.refs_1_), channel_id=1, source_target_pairs={{0,8},{4,12},{8,16},{12,20},{16,24},{20,28},{24,0},{28,4},{1,9},{5... | collective-permute-start | bytes 1228808 | tf_op jit(solution)/shard_map/ppermute | solution.py:69
  36.7 17.6 %collective-permute-start.3 = (bf16[400,512]{1,0:T(8,128)(2,1)S(1)}, bf16[400,512]{1,0:T(8,128)(2,1)S(1)}, u32[]{:S(2)}, u32[]{:S(2)}) collective-permute-start(bf16[400,512]{1,0:T(8,128)(2,1)S(1)} %collective-permute-done.2.refs_2_), channel_id=1, source_target_pairs={{0,8},{4,12},{8,16},{12,20},{16,24},{20,28},{24,0},{28,4},{1,9},{5... | collective-permute-start | bytes 1228808 | tf_op jit(solution)/shard_map/ppermute | solution.py:69
  45.6 17.6 %collective-permute-start.6 = (bf16[400,512]{1,0:T(8,128)(2,1)S(1)}, bf16[400,512]{1,0:T(8,128)(2,1)}, u32[]{:S(2)}, u32[]{:S(2)}) collective-permute-start(bf16[400,512]{1,0:T(8,128)(2,1)S(1)} %get-tuple-element.53.refs_0_), channel_id=1, source_target_pairs={{0,8},{4,12},{8,16},{12,20},{16,24},{20,28},{24,0},{28,4},{1,9},{5... | collective-permute-start | bytes 1228808 | tf_op jit(solution)/shard_map/ppermute | solution.py:69
  55.1 16.9 %collective-permute-start.12 = (bf16[400,512]{1,0:T(8,128)(2,1)}, bf16[400,512]{1,0:T(8,128)(2,1)}, u32[]{:S(2)}, u32[]{:S(2)}) collective-permute-start(bf16[400,512]{1,0:T(8,128)(2,1)} %bitcast.12.refs_0_), channel_id=1, source_target_pairs={{0,8},{4,12},{8,16},{12,20},{16,24},{20,28},{24,0},{28,4},{1,9},{5... | collective-permute-start | bytes 1228808 | tf_op jit(solution)/shard_map/ppermute | solution.py:69
  55.2 25.4 %collective-permute-start.10 = (bf16[400,512]{1,0:T(8,128)(2,1)}, bf16[400,512]{1,0:T(8,128)(2,1)S(1)}, u32[]{:S(2)}, u32[]{:S(2)}) collective-permute-start(bf16[400,512]{1,0:T(8,128)(2,1)} %collective-permute-done.5.refs_2_), channel_id=1, source_target_pairs={{0,8},{4,12},{8,16},{12,20},{16,24},{20,28},{24,0},{28,4},{1,9},{5... | collective-permute-start | bytes 1228808 | tf_op jit(solution)/shard_map/ppermute | solution.py:69
  63.2 26.2 %collective-permute-start.7 = (bf16[400,512]{1,0:T(8,128)(2,1)}, bf16[400,512]{1,0:T(8,128)(2,1)S(1)}, u32[]{:S(2)}, u32[]{:S(2)}) collective-permute-start(bf16[400,512]{1,0:T(8,128)(2,1)} %collective-permute-done.6.refs_1_), channel_id=1, source_target_pairs={{0,8},{4,12},{8,16},{12,20},{16,24},{20,28},{24,0},{28,4},{1,9},{5... | collective-permute-start | bytes 1228808 | tf_op jit(solution)/shard_map/ppermute | solution.py:69
  72.0 26.3 %collective-permute-start.13 = (bf16[400,512]{1,0:T(8,128)(2,1)}, bf16[400,512]{1,0:T(8,128)(2,1)}, u32[]{:S(2)}, u32[]{:S(2)}) collective-permute-start(bf16[400,512]{1,0:T(8,128)(2,1)} %collective-permute-done.12.refs_1_), channel_id=1, source_target_pairs={{0,8},{4,12},{8,16},{12,20},{16,24},{20,28},{24,0},{28,4},{1,9},{5... | collective-permute-start | bytes 1228808 | tf_op jit(solution)/shard_map/ppermute | solution.py:69
  84.0 27.6 %collective-permute-start.11 = (bf16[384,512]{1,0:T(8,128)(2,1)S(1)}, bf16[384,512]{1,0:T(8,128)(2,1)S(1)}, u32[]{:S(2)}, u32[]{:S(2)}) collective-permute-start(bf16[384,512]{1,0:T(8,128)(2,1)S(1)} %get-tuple-element.58), channel_id=1, source_target_pairs={{0,4},{4,0},{8,12},{12,8},{16,20},{20,16},{24,28},{28,24},{1,5},{5... | collective-permute-start | bytes 1179656 | tf_op jit(solution)/shard_map/ppermute | solution.py:64
  89.4 17.6 %collective-permute-start.8 = (bf16[400,512]{1,0:T(8,128)(2,1)S(1)}, bf16[400,512]{1,0:T(8,128)(2,1)S(1)}, u32[]{:S(2)}, u32[]{:S(2)}) collective-permute-start(bf16[400,512]{1,0:T(8,128)(2,1)S(1)} %collective-permute-done.7.refs_2_), channel_id=1, source_target_pairs={{0,8},{4,12},{8,16},{12,20},{16,24},{20,28},{24,0},{28,4},{1,9},{5... | collective-permute-start | bytes 1228808 | tf_op jit(solution)/shard_map/ppermute | solution.py:69
  92.3 19.3 %collective-permute-start.9 = (bf16[384,512]{1,0:T(8,128)(2,1)S(1)}, bf16[384,512]{1,0:T(8,128)(2,1)S(1)}, u32[]{:S(2)}, u32[]{:S(2)}) collective-permute-start(bf16[384,512]{1,0:T(8,128)(2,1)S(1)} %get-tuple-element.56), channel_id=1, source_target_pairs={{0,4},{4,0},{8,12},{12,8},{16,20},{20,16},{24,28},{28,24},{1,5},{5... | collective-permute-start | bytes 1179656 | tf_op jit(solution)/shard_map/ppermute | solution.py:64
  98.3 24.5 %collective-permute-start.14 = (bf16[400,512]{1,0:T(8,128)(2,1)}, bf16[400,512]{1,0:T(8,128)(2,1)}, u32[]{:S(2)}, u32[]{:S(2)}) collective-permute-start(bf16[400,512]{1,0:T(8,128)(2,1)} %collective-permute-done.13.refs_2_), channel_id=1, source_target_pairs={{0,8},{4,12},{8,16},{12,20},{16,24},{20,28},{24,0},{28,4},{1,9},{5... | collective-permute-start | bytes 1228808 | tf_op jit(solution)/shard_map/ppermute | solution.py:69
  98.9 36.9 %collective-permute-start.18 = (bf16[400,512]{1,0:T(8,128)(2,1)}, bf16[400,512]{1,0:T(8,128)(2,1)}, u32[]{:S(2)}, u32[]{:S(2)}) collective-permute-start(bf16[400,512]{1,0:T(8,128)(2,1)} %bitcast.12.refs_0_), channel_id=1, source_target_pairs={{0,4},{4,0},{8,12},{12,8},{16,20},{20,16},{24,28},{28,24},{1,5},{5... | collective-permute-start | bytes 1228808 | tf_op jit(solution)/shard_map/ppermute | solution.py:64
  107.0 28.8 %collective-permute-start.19 = (bf16[400,512]{1,0:T(8,128)(2,1)}, bf16[400,512]{1,0:T(8,128)(2,1)}, u32[]{:S(2)}, u32[]{:S(2)}) collective-permute-start(bf16[400,512]{1,0:T(8,128)(2,1)} %collective-permute-done.12.refs_1_), channel_id=1, source_target_pairs={{0,4},{4,0},{8,12},{12,8},{16,20},{20,16},{24,28},{28,24},{1,5},{5... | collective-permute-start | bytes 1228808 | tf_op jit(solution)/shard_map/ppermute | solution.py:64
  114.5 14.3 %collective-permute-start.15 = (bf16[384,512]{1,0:T(8,128)(2,1)}, bf16[384,512]{1,0:T(8,128)(2,1)}, u32[]{:S(2)}, u32[]{:S(2)}) collective-permute-start(bf16[384,512]{1,0:T(8,128)(2,1)} %copy-done.16), channel_id=1, source_target_pairs={{0,4},{4,0},{8,12},{12,8},{16,20},{20,16},{24,28},{28,24},{1,5},{5... | collective-permute-start | bytes 1179656 | tf_op jit(solution)/shard_map/ppermute | solution.py:64
  116.1 21.5 %collective-permute-start.20 = (bf16[400,512]{1,0:T(8,128)(2,1)}, bf16[400,512]{1,0:T(8,128)(2,1)}, u32[]{:S(2)}, u32[]{:S(2)}) collective-permute-start(bf16[400,512]{1,0:T(8,128)(2,1)} %collective-permute-done.13.refs_2_), channel_id=1, source_target_pairs={{0,4},{4,0},{8,12},{12,8},{16,20},{20,16},{24,28},{28,24},{1,5},{5... | collective-permute-start | bytes 1228808 | tf_op jit(solution)/shard_map/ppermute | solution.py:64
  122.8 21.2 %collective-permute-start.21 = (bf16[400,512]{1,0:T(8,128)(2,1)}, bf16[400,512]{1,0:T(8,128)(2,1)}, u32[]{:S(2)}, u32[]{:S(2)}) collective-permute-start(bf16[400,512]{1,0:T(8,128)(2,1)} %collective-permute-done.14.refs_3_), channel_id=1, source_target_pairs={{0,4},{4,0},{8,12},{12,8},{16,20},{20,16},{24,28},{28,24},{1,5},{5... | collective-permute-start | bytes 1228808 | tf_op jit(solution)/shard_map/ppermute | solution.py:64
  135.7 16.3 %collective-permute-start.16 = (bf16[2,400,384]{2,1,0:T(8,128)(2,1)}, bf16[2,400,384]{2,1,0:T(8,128)(2,1)S(1)}, u32[]{:S(2)}, u32[]{:S(2)}) collective-permute-start(bf16[2,400,384]{2,1,0:T(8,128)(2,1)} %get-tuple-element.66), channel_id=1, source_target_pairs={{0,1},{1,0},{2,3},{3,2},{4,5},{5,4},{6,7},{7,6},{8,9},{9,8},{10,11... | collective-permute-start | bytes 1843208 | tf_op jit(solution)/shard_map/ppermute | solution.py:64
  156.1 14.2 %collective-permute-start.23 = (bf16[400,384]{1,0:T(8,128)(2,1)}, bf16[400,384]{1,0:T(8,128)(2,1)S(1)}, u32[]{:S(2)}, u32[]{:S(2)}) collective-permute-start(bf16[400,384]{1,0:T(8,128)(2,1)} %far_sum.3), channel_id=1, source_target_pairs={{0,2},{1,3},{2,0},{3,1},{4,6},{5,7},{6,4},{7,5},{8,10},{9,11},{10,... | collective-permute-start | bytes 921608 | tf_op jit(solution)/shard_map/ppermute | solution.py:64
  178.9 12.8 %collective-permute-start.31 = (bf16[24,1600]{1,0:T(8,128)(2,1)}, bf16[24,1600]{1,0:T(8,128)(2,1)S(1)}, u32[]{:S(2)}, u32[]{:S(2)}) collective-permute-start(bf16[24,1600]{1,0:T(8,128)(2,1)} %copy-done.18), channel_id=1, source_target_pairs={{0,20},{4,16},{8,28},{12,24},{16,4},{20,0},{24,12},{28,8},{1,21},{... | collective-permute-start | bytes 230408 | tf_op jit(solution)/shard_map/ppermute | solution.py:64
  180.3 12.3 %collective-permute-start.32 = (bf16[24,1600]{1,0:T(8,128)(2,1)}, bf16[24,1600]{1,0:T(8,128)(2,1)S(1)}, u32[]{:S(2)}, u32[]{:S(2)}) collective-permute-start(bf16[24,1600]{1,0:T(8,128)(2,1)} %copy-done.17), channel_id=1, source_target_pairs={{0,24},{4,28},{8,16},{12,20},{16,8},{20,12},{24,0},{28,4},{1,25},{... | collective-permute-start | bytes 230408 | tf_op jit(solution)/shard_map/ppermute | solution.py:64
  183.8 11.4 %collective-permute-start.33 = (bf16[24,1600]{1,0:T(8,128)(2,1)S(1)}, bf16[24,1600]{1,0:T(8,128)(2,1)S(1)}, u32[]{:S(2)}, u32[]{:S(2)}) collective-permute-start(bf16[24,1600]{1,0:T(8,128)(2,1)S(1)} %get-tuple-element.80), channel_id=1, source_target_pairs={{0,28},{4,24},{8,20},{12,16},{16,12},{20,8},{24,4},{28,0},{1,29},{... | collective-permute-start | bytes 230408 | tf_op jit(solution)/shard_map/ppermute | solution.py:64
  184.6 13.2 %collective-permute-start.34 = (bf16[24,1600]{1,0:T(8,128)(2,1)S(1)}, bf16[24,1600]{1,0:T(8,128)(2,1)S(1)}, u32[]{:S(2)}, u32[]{:S(2)}) collective-permute-start(bf16[24,1600]{1,0:T(8,128)(2,1)S(1)} %get-tuple-element.82), channel_id=1, source_target_pairs={{0,4},{4,0},{8,12},{12,8},{16,20},{20,16},{24,28},{28,24},{1,5},{5... | collective-permute-start | bytes 230408 | tf_op jit(solution)/shard_map/ppermute | solution.py:64
  185.7 13.5 %collective-permute-start.35 = (bf16[24,1600]{1,0:T(8,128)(2,1)S(1)}, bf16[24,1600]{1,0:T(8,128)(2,1)S(1)}, u32[]{:S(2)}, u32[]{:S(2)}) collective-permute-start(bf16[24,1600]{1,0:T(8,128)(2,1)S(1)} %get-tuple-element.83), channel_id=1, source_target_pairs={{0,8},{4,12},{8,0},{12,4},{16,24},{20,28},{24,16},{28,20},{1,9},{5... | collective-permute-start | bytes 230408 | tf_op jit(solution)/shard_map/ppermute | solution.py:64
  191.7 20.0 %collective-permute-start.36 = (bf16[24,1600]{1,0:T(8,128)(2,1)S(1)}, bf16[24,1600]{1,0:T(8,128)(2,1)S(1)}, u32[]{:S(2)}, u32[]{:S(2)}) collective-permute-start(bf16[24,1600]{1,0:T(8,128)(2,1)S(1)} %get-tuple-element.84), channel_id=1, source_target_pairs={{0,12},{4,8},{8,4},{12,0},{16,28},{20,24},{24,20},{28,16},{1,13},{... | collective-permute-start | bytes 230408 | tf_op jit(solution)/shard_map/ppermute | solution.py:64
  192.6 19.1 %collective-permute-start.37 = (bf16[24,1600]{1,0:T(8,128)(2,1)S(1)}, bf16[24,1600]{1,0:T(8,128)(2,1)S(1)}, u32[]{:S(2)}, u32[]{:S(2)}) collective-permute-start(bf16[24,1600]{1,0:T(8,128)(2,1)S(1)} %get-tuple-element.85), channel_id=1, source_target_pairs={{0,16},{4,20},{8,24},{12,28},{16,0},{20,4},{24,8},{28,12},{1,17},{... | collective-permute-start | bytes 230408 | tf_op jit(solution)/shard_map/ppermute | solution.py:64
  195.2 16.6 %collective-permute-start.38 = (bf16[24,1600]{1,0:T(8,128)(2,1)S(1)}, bf16[24,1600]{1,0:T(8,128)(2,1)S(1)}, u32[]{:S(2)}, u32[]{:S(2)}) collective-permute-start(bf16[24,1600]{1,0:T(8,128)(2,1)S(1)} %get-tuple-element.86), channel_id=1, source_target_pairs={{0,20},{4,16},{8,28},{12,24},{16,4},{20,0},{24,12},{28,8},{1,21},{... | collective-permute-start | bytes 230408 | tf_op jit(solution)/shard_map/ppermute | solution.py:64
  197.9 13.9 %collective-permute-start.39 = (bf16[24,1600]{1,0:T(8,128)(2,1)S(1)}, bf16[24,1600]{1,0:T(8,128)(2,1)S(1)}, u32[]{:S(2)}, u32[]{:S(2)}) collective-permute-start(bf16[24,1600]{1,0:T(8,128)(2,1)S(1)} %get-tuple-element.87), channel_id=1, source_target_pairs={{0,24},{4,28},{8,16},{12,20},{16,8},{20,12},{24,0},{28,4},{1,25},{... | collective-permute-start | bytes 230408 | tf_op jit(solution)/shard_map/ppermute | solution.py:64
  199.2 12.5 %collective-permute-start.40 = (bf16[24,1600]{1,0:T(8,128)(2,1)S(1)}, bf16[24,1600]{1,0:T(8,128)(2,1)S(1)}, u32[]{:S(2)}, u32[]{:S(2)}) collective-permute-start(bf16[24,1600]{1,0:T(8,128)(2,1)S(1)} %get-tuple-element.88), channel_id=1, source_target_pairs={{0,28},{4,24},{8,20},{12,16},{16,12},{20,8},{24,4},{28,0},{1,29},{... | collective-permute-start | bytes 230408 | tf_op jit(solution)/shard_map/ppermute | solution.py:64
  (40 other events, 397.0 us)

commit v4 on v3

--- a/solution.py
+++ b/solution.py
@@ -52,8 +52,8 @@
     return jnp.sum(earlier.astype(jnp.int32), axis=1)
 
 
-def dest_tokens(patch_rows, is_live, owners, ranks, capacity, devices_req, first):
-    target = jnp.where(is_live, (owners ^ first) * capacity + ranks, -1)
+def dest_tokens(patch_rows, is_live, owners, ranks, capacity, devices_req):
+    target = jnp.where(is_live, owners * capacity + ranks, -1)
     rows = jnp.arange(devices_req * capacity, dtype=jnp.int32)
     hit = (target[None, :] == rows[:, None]).astype(jnp.int32)
     return jnp.sum(hit[:, :, None] * (patch_rows[None] + 1), axis=1) - 1
@@ -64,19 +64,26 @@
     return lax.ppermute(value, axis, [(i, i ^ bit) for i in range(count)])
 
 
-def ring(value):
+def ring(value, step=1):
     count = lax.axis_size("req")
-    return lax.ppermute(value, "req", [(i, (i + 2) % count) for i in range(count)])
-
-
-def call(kernel, name, out, operands, flops, scalars=0, raw=0, scratch=()):
+    return lax.ppermute(value, "req", [(i, (i + 2 * step) % count) for i in range(count)])
+
+
+def call(kernel, name, out, operands, flops, scalars=0, raw=0, scratch=(), ties=()):
+    used = len(operands)
+    operands = tuple(operands) + tuple(x[:8, :128] for x in ties)
+    raw = raw + len(ties)
+
+    def untied(*refs):
+        kernel(*refs[:used], *refs[used + len(ties) :])
+
     def whole(x):
         return pl.BlockSpec(x.shape, lambda i: (0,) * len(x.shape))
 
     blocks = operands[scalars : len(operands) - raw]
     moved = sum(x.size * x.dtype.itemsize for x in operands[scalars:] + tuple(out))
     return pl.pallas_call(
-        kernel,
+        untied,
         grid=(1,),
         out_shape=tuple(out),
         in_specs=[pl.BlockSpec(memory_space=pltpu.SMEM)] * scalars
@@ -84,7 +91,7 @@
         + [pl.BlockSpec(memory_space=pl.ANY)] * raw,
         out_specs=tuple(whole(x) for x in out),
         scratch_shapes=scratch,
-        compiler_params=pltpu.CompilerParams(vmem_limit_bytes=32 << 20),
+        compiler_params=pltpu.CompilerParams(vmem_limit_bytes=20 << 20),
         cost_estimate=pl.CostEstimate(flops=flops, bytes_accessed=moved, transcendentals=0),
         name=name,
     )(*operands)
@@ -169,10 +176,19 @@
 
 
 def scores_kernel(q_ref, q_got_ref, k_ref, k_got_ref, q_gain_ref, k_gain_ref, raw_ref, sums_ref):
+    share = q_ref.shape[1]
     queries = q_ref[...] + q_got_ref[...].astype(F32)
     key_vecs = k_ref[...] + k_got_ref[...].astype(F32)
-    sums_ref[:, 0:1] = jnp.sum(queries * queries, axis=1, keepdims=True)
-    sums_ref[:, 1:2] = jnp.sum(key_vecs * key_vecs, axis=1, keepdims=True)
+    ones = jnp.ones((8, share), F32)
+    for i, values in enumerate((queries, key_vecs)):
+        totals = lax.dot_general(
+            ones,
+            values * values,
+            (((1,), (1,)), ((), ())),
+            precision=lax.Precision.HIGHEST,
+            preferred_element_type=F32,
+        )
+        sums_ref[i : i + 1, :] = totals[0:1]
     queries = queries * (q_gain_ref[...] * (1.0 / math.sqrt(HEAD_DIM)))
     key_vecs = key_vecs * k_gain_ref[...]
     for head in range(raw_ref.shape[0]):
@@ -186,12 +202,17 @@
         )
 
 
-def attend_kernel(raw_ref, q_scale_ref, k_scale_ref, seg_ref, seg_row_ref, v_ref, v_got_ref, out_ref):
-    same = seg_ref[...] == seg_row_ref[...]
+def attend_kernel(raw_ref, sums_ref, segment_ref, v_ref, v_got_ref, out_ref):
+    rows = raw_ref.shape[1]
+    scales = lax.rsqrt(sums_ref[...] / (HEADS * HEAD_DIM) + 1e-06)
+    q_scale = jnp.broadcast_to(scales[0:1], (128, rows)).T[:, 0:1]
+    k_scale = scales[1:2]
+    segment = segment_ref[...]
+    same = jnp.broadcast_to(segment, (128, rows)).T[:, 0:1] == segment
     values = (v_ref[...] + v_got_ref[...].astype(F32)).astype(BF16)
     for head in range(raw_ref.shape[0]):
         part = slice(head * HEAD_DIM, (head + 1) * HEAD_DIM)
-        scores = raw_ref[head] * q_scale_ref[...] * k_scale_ref[...]
+        scores = raw_ref[head] * q_scale * k_scale
         scores = jnp.where(same, scores, -1e30)
         raised = jnp.exp(scores - jnp.max(scores, axis=1, keepdims=True))
         probs = (raised / jnp.sum(raised, axis=1, keepdims=True)).astype(BF16)
@@ -242,64 +263,65 @@
     far_ref[...] = (kept_ref[...] + near_ref[0].astype(F32)).astype(BF16)
 
 
-def pack_kernel(kept_ref, near_ref, far_ref, token_ref, chosen_ref, sums_ref, *block_refs):
+def hidden_of(kept_ref, near_ref, far_ref, token_ref):
     attn_out = kept_ref[...] + near_ref[1].astype(F32) + far_ref[...].astype(F32)
-    hidden = (token_ref[...].astype(F32) + attn_out).astype(BF16)
-    depth = hidden.shape[0]
-    rows = block_refs[0].shape[0]
+    return (token_ref[...].astype(F32) + attn_out).astype(BF16)
+
+
+def sum_tokens(hidden, sums_ref, first=0):
+    hidden = hidden.astype(F32)
+    sums_ref[first : first + 1, :] = jnp.sum(hidden, axis=0, keepdims=True)
+    sums_ref[first + 1 : first + 2, :] = jnp.sum(hidden * hidden, axis=0, keepdims=True)
+
+
+def hidden_kernel(kept_ref, near_ref, far_ref, token_ref, hidden_ref, sums_ref):
+    hidden = hidden_of(kept_ref, near_ref, far_ref, token_ref)
+    hidden_ref[...] = hidden
+    sum_tokens(hidden, sums_ref)
+
+
+def pack_kernel(
+    first_ref, first_sums_ref, kept_ref, near_ref, far_ref, token_ref, own_ref, next_ref,
+    rows_ref, sums_ref,
+):
+    halves = [first_ref[...], hidden_of(kept_ref, near_ref, far_ref, token_ref)]
+    depth = halves[0].shape[0]
+    count, rows, _ = rows_ref.shape
+    rows = rows // 2
     for patch in range(4):
-        first = patch * rows * len(block_refs)
-        picked = lax.dot_general(
-            chosen_ref[pl.ds(first, rows * len(block_refs)), :],
-            hidden,
-            (((1,), (1,)), ((), ())),
-            preferred_element_type=F32,
-        )
-        for i, ref in enumerate(block_refs):
-            part = picked[i * rows : (i + 1) * rows]
-            ref[:, pl.ds(patch * depth, depth)] = part.astype(BF16)
-    hidden = hidden.astype(F32)
-    sums_ref[0:1, :] = jnp.sum(hidden, axis=0, keepdims=True)
-    sums_ref[1:2, :] = jnp.sum(hidden * hidden, axis=0, keepdims=True)
-
-
-def pack(kept, near, far, token_part, chosen, count):
-    depth, token_count = far.shape
-    rows = chosen.shape[0] // 4 // count
-    out = (array((2, token_count), F32),) + (array((rows, 4 * depth), BF16),) * count
-    operands = (kept, near, far, token_part, chosen)
-    return call(pack_kernel, "pack", out, operands, 2 * chosen.size * depth)
-
-
-def finish_kernel(place_ref, stats_ref, gain_ref, bias_ref, *refs):
-    out_ref = refs[-1]
-    count = (len(refs) - 1) // 2
-    rows, _, quarter = out_ref.shape
-    rows = rows // count
-    depth = quarter // 2
+        for half, (hidden, chosen_ref) in enumerate(zip(halves, (own_ref, next_ref))):
+            chosen = chosen_ref[pl.ds(patch * rows * count, rows * count), :]
+            picked = lax.dot_general(
+                chosen, hidden, (((1,), (1,)), ((), ())), preferred_element_type=F32
+            )
+            picked = picked.reshape(count, rows, depth).astype(BF16)
+            rows_ref[:, pl.ds(half * rows, rows), pl.ds(patch * depth, depth)] = picked
+    sums_ref[0:2, :] = first_sums_ref[...]
+    sum_tokens(halves[1], sums_ref, 2)
+
+
+def finish_kernel(stats_ref, gain_ref, bias_ref, rows_ref, out_ref):
+    count, rows, _ = rows_ref.shape
+    rows = rows // 2
+    depth = out_ref.shape[2] // 2
     for i in range(count):
-        source = place_ref[0] ^ i
-        to = pl.ds(source * rows, rows)
-        swapped = (source & 1) == 1
+        to = pl.ds(i * rows, rows)
         scale, shift, live = (stats_ref[j, to][:, 0:1] for j in range(3))
         for patch in range(4):
             part = slice(patch * depth, (patch + 1) * depth)
-            own = refs[i][:, part].astype(F32)
-            other = refs[count + i][:, part].astype(F32)
-            values = jnp.concatenate(
-                [jnp.where(swapped, other, own), jnp.where(swapped, own, other)], axis=1
-            )
+            parts = [rows_ref[i, :rows, part].astype(F32), rows_ref[i ^ 1, rows:, part].astype(F32)]
+            values = jnp.concatenate(parts[::-1] if i % 2 else parts, axis=1)
             gain, bias = gain_ref[patch : patch + 1, :], bias_ref[patch : patch + 1, :]
             values = (values * scale + shift) * gain + live * bias
             out_ref[to, patch, :] = values.astype(BF16)
 
 
-def finish(me, stats, proj_gain, proj_bias, blocks):
+def finish(stats, proj_gain, proj_bias, arrived):
     rows = stats.shape[1]
     stats = jnp.broadcast_to(stats[:, :, None], (3, rows, 128))
     out = array((rows,) + proj_gain.shape, BF16)
-    operands = (me.reshape(1), stats, proj_gain, proj_bias) + tuple(blocks)
-    return call(finish_kernel, "finish", (out,), operands, 6 * out.size, scalars=1)[0]
+    operands = (stats, proj_gain, proj_bias, arrived)
+    return call(finish_kernel, "finish", (out,), operands, 6 * out.size)[0]
 
 
 def after(value, *first):
@@ -393,10 +415,8 @@
     quarter = proj_gain.shape[1]
     head_share = q_gain.shape[0]
     head_count = head_share // HEAD_DIM
-    head_width = HEADS * HEAD_DIM
     feature_total = 4 * D
     devices_req = lax.axis_size("req")
-    devices_tp = lax.axis_size("tp")
     planes = devices_req // 2
     capacity = max(2, (2 * slot_count + devices_req - 1) // devices_req)
     me = lax.axis_index("req")
@@ -407,87 +427,109 @@
     part = array((w_qkv.shape[0], head_share), BF16)
     w_q, w_k, w_v = call(split_kernel, "split_heads", (part,) * 3, (w_qkv,), 0)
     w_o = w_out.T
-    q_blocks, k_blocks = [w_q], [w_k]
-    for step in range(1, planes):
-        q_blocks.append(ring(q_blocks[-1]))
-        k_blocks.append(ring(k_blocks[-1]))
-    v_blocks, o_blocks = [after(w_v, k_blocks[-2])], [after(w_o, q_blocks[-1])]
-    for step in range(1, planes):
-        v_blocks.append(ring(v_blocks[-1]))
-        o_blocks.append(ring(o_blocks[-1]))
-
-    patch_rows, is_live, segment = merge_layout(grids, token_count, slot_count)
-    ranks = owner_ranks(owners, is_live)
-    placing = (patch_rows, is_live, owners, ranks, capacity, devices_req)
-    sent_tokens = dest_tokens(*placing, me)
-    chosen = (sent_tokens.T.reshape(-1)[:, None] == token_ids[None, :]).astype(BF16)
-    row_tokens = dest_tokens(*placing, 0)
-    in_row = jnp.any(row_tokens[:, :, None] == token_ids[None, None, :], axis=1).astype(F32)
-    row_live = (row_tokens[:, 0] >= 0).astype(F32)
+    q_up, q_down, k_up = ring(w_q), ring(w_q, -1), ring(w_k)
+    k_down = ring(after(w_k, q_up), -1)
+    q_far = ring(after(q_up, q_down))
+    k_far = ring(k_up)
+    v_up = ring(after(w_v, k_down))
+    v_down = ring(after(w_v, q_far), -1)
+    v_far = ring(v_up)
+    o_up = ring(after(w_o, v_up))
+    o_down = ring(after(w_o, v_down), -1)
+    o_far = ring(o_up)
+    q_blocks, k_blocks = [w_q, q_up, q_far, q_down], [w_k, k_up, k_far, k_down]
+    v_blocks, o_blocks = [w_v, v_up, v_far, v_down], [w_o, o_up, o_far, o_down]
+
+    own_routes = after(jnp.concatenate([owners, grids.reshape(-1)]), k_down)
+    chosen, in_row = [], []
+    for routes in (own_routes, swap(own_routes, "req", 1)):
+        owner_ids, grid = routes[:slot_count], routes[slot_count:].reshape(-1, 2)
+        patch_rows, is_live, tokens_of = merge_layout(grid, token_count, slot_count)
+        ranks = owner_ranks(owner_ids, is_live)
+        row_tokens = dest_tokens(
+            patch_rows, is_live, owner_ids, ranks, capacity, devices_req
+        )
+        picks = row_tokens.T.reshape(-1)[:, None] == token_ids[None, :]
+        chosen.append(picks.astype(BF16))
+        picks = row_tokens[:, :, None] == token_ids[None, None, :]
+        in_row.append(jnp.any(picks, axis=1).astype(F32))
+        if routes is own_routes:
+            segment, row_live = tokens_of, (row_tokens[:, 0] >= 0).astype(F32)
     token_mine = lax.dynamic_slice_in_dim(tokens, column * quarter, quarter, 1).T
     token_mine = token_mine.reshape(2, quarter // 2, token_count)
+    token_parts = [
+        lax.dynamic_index_in_dim(token_mine, side, 0, keepdims=False),
+        swap(lax.dynamic_index_in_dim(token_mine, 1 - side, 0, keepdims=False), "req", 1),
+    ]
 
     places = jnp.stack([plane, side, column]).astype(jnp.int32)
-    mine, others = norm_tokens(places[1:2], tokens, norm_gain)
+    mine, others = norm_tokens(places[1:2], after(tokens, w_q), norm_gain)
     theirs = swap(others, "req", 1)
 
-    def projected(blocks):
-        own, peer = project(places[0:1], mine, theirs, blocks)
-        return own, swap(peer, "req", 1)
-
-    queries = projected(q_blocks)
-    key_vecs = projected(k_blocks)
-    values = projected(v_blocks)
+    mine = after(mine, *token_parts, *chosen)
+    queries, q_peer = project(places[0:1], mine, theirs, q_blocks)
+    q_got = swap(q_peer, "req", 1)
+    key_vecs, k_peer = project(places[0:1], mine, theirs, k_blocks)
+    k_got = swap(k_peer, "req", 1)
+    values, v_peer = project(places[0:1], mine, theirs, v_blocks)
+    v_got = swap(v_peer, "req", 1)
     raw, sums = call(
         scores_kernel,
         "scores",
         (
             array((head_count, token_count, token_count), F32),
-            array((token_count, 2), F32),
+            array((2, token_count), F32),
         ),
-        (after(queries[0], values[0]), queries[1], *key_vecs, q_gain[None], k_gain[None]),
+        (queries, q_got, key_vecs, k_got, q_gain[None], k_gain[None]),
         12 * token_count * token_count * head_share,
-    )
-    sums = after(sums, o_blocks[-2])
-    scales = lax.rsqrt(lax.psum(sums.T, "tp") / head_width + 1e-06)
+        ties=(v_peer,),
+    )
     (attended,) = call(
         attend_kernel,
         "attend",
         (array((token_count, head_share), BF16),),
-        (
-            after(raw, o_blocks[-1]),
-            scales[0][:, None],
-            scales[1][None],
-            segment[:, None],
-            segment[None],
-            *values,
-        ),
+        (raw, lax.psum(sums, "tp"), segment.astype(F32)[None], values, v_got),
         2 * token_count * token_count * head_share,
     )
 
-    halves, token_sums = [], 0.0
-    others_blocks = [swap(block, "req", 1) for block in o_blocks]
-    for half, blocks in ((side, o_blocks), (1 - side, others_blocks)):
-        sent, kept_far, kept = project_out(places, attended, blocks)
+    parts = []
+    for heads_out, token_part in zip((attended, swap(attended, "req", 1)), token_parts):
+        sent, kept_far, kept = project_out(places, heads_out, o_blocks)
         near = swap(sent, "tp", 1)
         (far,) = call(far_kernel, "far_sum", (array(kept.shape, BF16),), (kept_far, near), 0)
-        far = swap(far, "tp", 2)
-        token_part = lax.dynamic_index_in_dim(token_mine, half, 0, keepdims=False)
-        sums, *blocks = pack(kept, near, far, token_part, chosen, devices_req)
-        for bits in reversed(range(1, devices_req)):
-            blocks[bits] = swap(blocks[bits], "req", bits)
-        halves += blocks
-        token_sums = token_sums + sums
-
-    token_sums = token_sums + sum(swap(token_sums, "tp", bit) for bit in range(1, devices_tp))
-    row_sums = jnp.sum(in_row[None] * token_sums[:, None, :], axis=2)
-    mean_value = row_sums[0] / feature_total
-    variance = row_sums[1] / feature_total - mean_value * mean_value
-    inverse = lax.rsqrt(variance + 1e-05) * row_live
-    stats = jnp.stack([inverse, -mean_value * inverse, row_live]).reshape(3, devices_req, capacity)
-    stats = lax.all_to_all(stats, "req", split_axis=1, concat_axis=1, tiled=True)
+        parts.append((kept, near, swap(far, "tp", 2), token_part))
+    out = (array(kept.shape, BF16), array((2, token_count), F32))
+    hidden, own_sums = call(hidden_kernel, "hidden", out, parts[0], 0)
+    rows, token_sums = call(
+        pack_kernel,
+        "pack",
+        (array((devices_req, 2 * capacity, 2 * quarter), BF16), array((4, token_count), F32)),
+        (hidden, own_sums, *parts[1], *chosen),
+        2 * chosen[0].size * quarter,
+    )
+    arrived = lax.all_to_all(rows, "req", split_axis=0, concat_axis=0, tiled=True)
+
+    token_sums = lax.psum(token_sums, "tp").reshape(2, 2, token_count)
+    own_sums, next_sums = (
+        jnp.sum(picks[None] * sums[:, None, :], axis=2) for picks, sums in zip(in_row, token_sums)
+    )
+    got = swap(next_sums, "req", 1)
+    row_sums = (own_sums + got) / feature_total
+    mean_value = row_sums[0]
+    inverse = lax.rsqrt(row_sums[1] - mean_value * mean_value + 1e-05) * row_live
+    stats = jnp.stack([inverse, -mean_value * inverse, row_live])
+    stats = stats.reshape(3, 1, devices_req, capacity)
+    bit = 1
+    while bit < devices_req:
+        got = swap(stats, "req", bit)
+        lower = (me & bit) == 0
+        stats = jnp.concatenate(
+            [jnp.where(lower, stats, got), jnp.where(lower, got, stats)], axis=1
+        )
+        bit *= 2
+    stats = lax.dynamic_index_in_dim(stats, me, 2, keepdims=False)
     stats = stats.reshape(3, devices_req * capacity)
-    return finish(me, stats, proj_gain, proj_bias, halves)
+    return finish(stats, proj_gain, proj_bias, arrived)
 
 
 def solution(mesh):

time: 216 us -> 188 us (0.87)
  waiting for transfers between devices: 101 us -> 73.6 us
  blocking collectives: 16.6 us -> 12.8 us
  local copies, waits for them, and re-layouts: 17.1 us -> 14.1 us
  starting transfers between devices: 42.8 us -> 45.5 us
  Pallas kernels: 32.9 us -> 35.4 us
    ppermute x12, waiting for transfers between devices: 76.2 us -> 33.4 us  [ring(): lax.ppermute(value, 'req', [(i, (i + 2 * step) % count) for i in range(co...]
    ppermute x29 -> x15, waiting for transfers between devices: 24.4 us -> 40.2 us  [swap(): return lax.ppermute(value, axis, [(i, i ^ bit) for i in range(count)])]
    ppermute x29 -> x15, starting transfers between devices: 36.6 us -> 21.7 us  [swap(): return lax.ppermute(value, axis, [(i, i ^ bit) for i in range(count)])]
    ppermute x12, starting transfers between devices: 6.18 us -> 19.6 us  [ring(): lax.ppermute(value, 'req', [(i, (i + 2 * step) % count) for i in range(co...]
    all_to_all x1 -> x0, blocking collectives: 10.4 us -> none  [body(): lax.all_to_all(stats, 'req', split_axis=1, concat_axis=1, tiled=True)]
    psum x1 -> x2, blocking collectives: 6.21 us -> 12.8 us  [the longest x1 6.57 us: body(): token_sums = lax.psum(token_sums, 'tp').reshape(2, 2, token_count)]
    all_to_all x0 -> x1, starting transfers between devices: none -> 4.19 us  [body(): lax.all_to_all(rows, 'req', split_axis=0, concat_axis=0, tiled=True)]
    unnamed x63 -> x42, local copies, waits for them, and re-layouts: 11.5 us -> 7.72 us
  transfers between devices with their start and end apart: 41 -> 28, of which waited for: 17 -> 14; matrix products, arithmetic and copies ran while one was open for 6% -> 7% of each run, Pallas kernels for 13% -> 16%
where the time goes in v4:
time: 188 us; the launch traced here: 187 us
  waiting for transfers between devices  73.6 us (39%)
  starting transfers between devices  45.5 us (24%)
  Pallas kernels  35.4 us (19%)
  local copies, waits for them, and re-layouts  14.1 us (8%)
  blocking collectives  12.8 us (7%)
  other arithmetic  4.93 us (3%)
    ppermute x15, waiting for transfers between devices, swap(): return lax.ppermute(value, axis, [(i, i ^ bit) for i in range(count)])  40.2 us
    pallas_call x14, Pallas kernels, call(): pl.pallas_call(untied, grid=(1,), out_shape=tuple(out), in_specs=[pl.Bloc...  35.4 us
    ppermute x12, waiting for transfers between devices, ring(): lax.ppermute(value, 'req', [(i, (i + 2 * step) % count) for i in range(co...  33.4 us
    ppermute x15, starting transfers between devices, swap(): return lax.ppermute(value, axis, [(i, i ^ bit) for i in range(count)])  21.7 us
    ppermute x12, starting transfers between devices, ring(): lax.ppermute(value, 'req', [(i, (i + 2 * step) % count) for i in range(co...  19.6 us
    unnamed x42, local copies, waits for them, and re-layouts  7.72 us
    psum x1, blocking collectives, body(): token_sums = lax.psum(token_sums, 'tp').reshape(2, 2, token_count)  6.57 us
    psum x1, blocking collectives, body(): lax.psum(sums, 'tp')  6.25 us
  transfers between devices with their start and end apart: 28, of which 14 were waited for; matrix products, arithmetic and copies ran while one was open for 7% of the time, Pallas kernels for 16%

profile of v4, /device:TPU:0, one launch (start us, length us, event | category | flops | bytes accessed | tf_op | source)
XLA Modules:
  0.0 186.9 jit_solution(7910447455184419700)
XLA Ops:
  2.4 3.0 %collective-permute-start = (bf16[400,512]{1,0:T(8,128)(2,1)}, bf16[400,512]{1,0:T(8,128)(2,1)}, u32[]{:S(2)}, u32[]{:S(2)}) collective-permute-start(bf16[400,512]{1,0:T(8,128)(2,1)} %get-tuple-element.38.refs_3_), channel_id=1, source_target_pairs={{0,8},{4,12},{8,16},{12,20},{16,24},{20,28},{24,0},{28,4},{1,9},{5... | collective-permute-start | bytes 1228808 | tf_op jit(solution)/shard_map/ppermute | solution.py:69
  5.4 2.0 %collective-permute-start.5 = (bf16[400,512]{1,0:T(8,128)(2,1)}, bf16[400,512]{1,0:T(8,128)(2,1)}, u32[]{:S(2)}, u32[]{:S(2)}) collective-permute-start(bf16[400,512]{1,0:T(8,128)(2,1)} %get-tuple-element.38.refs_3_), channel_id=1, source_target_pairs={{0,24},{4,28},{8,0},{12,4},{16,8},{20,12},{24,16},{28,20},{1,25},{... | collective-permute-start | bytes 1228808 | tf_op jit(solution)/shard_map/ppermute | solution.py:69
  7.4 10.6 %collective-permute-done.refs_4_ = bf16[400,512]{1,0:T(8,128)(2,1)} collective-permute-done((bf16[400,512]{1,0:T(8,128)(2,1)}, bf16[400,512]{1,0:T(8,128)(2,1)}, u32[]{:S(2)}, u32[]{:S(2)}) %collective-permute-start) | collective-permute-done | bytes 409632 | tf_op jit(solution)/shard_map/ppermute | solution.py:69
  18.1 10.8 %collective-permute-start.1 = (bf16[400,512]{1,0:T(8,128)(2,1)}, bf16[400,512]{1,0:T(8,128)(2,1)}, u32[]{:S(2)}, u32[]{:S(2)}) collective-permute-start(bf16[400,512]{1,0:T(8,128)(2,1)} %get-tuple-element.39.refs_3_), channel_id=1, source_target_pairs={{0,24},{4,28},{8,0},{12,4},{16,8},{20,12},{24,16},{28,20},{1,25},{... | collective-permute-start | bytes 1228808 | tf_op jit(solution)/shard_map/ppermute | solution.py:69
  28.9 2.3 %constant_dynamic-slice_fusion = bf16[384,800]{1,0:T(8,128)(2,1)} fusion(bf16[384,3200]{1,0:T(8,128)(2,1)} %refs_1_.1, s32[]{:T(128)S(6)} %select_n.277), kind=kLoop, calls=%fused_computation.73 | loop fusion | bytes 1228804 | tf_op jit(solution)/shard_map/dynamic_slice | solution.py:458
  31.2 2.3 %copy.26 = bf16[384,800]{0,1:T(8,128)(2,1)} copy(bf16[384,800]{1,0:T(8,128)(2,1)} %constant_dynamic-slice_fusion) | data formatting | bytes 1228800
  36.9 4.3 %norm_tokens.1 = (bf16[384,1600]{1,0:T(8,128)(2,1)S(1)}, bf16[384,1664]{1,0:T(8,128)(2,1)}) custom-call(s32[1]{0:T(128)} %bitcast.4.refs_0_, bf16[384,3200]{1,0:T(8,128)(2,1)S(1)} %copy-done, f32[1,3200]{1,0:T(1,128)S(1)} %broadcast_in_dim.39.refs_2_), custom_call_target="tpu_custom_call" | custom-call | bytes 4977152 | tf_op jit(solution)/shard_map/norm_tokens/pallas_call | solution.py:85
  46.0 11.5 %collective-permute-done.6.refs_5_ = bf16[400,512]{1,0:T(8,128)(2,1)S(1)} collective-permute-done((bf16[400,512]{1,0:T(8,128)(2,1)}, bf16[400,512]{1,0:T(8,128)(2,1)S(1)}, u32[]{:S(2)}, u32[]{:S(2)}) %collective-permute-start.6) | collective-permute-done | bytes 409632 | tf_op jit(solution)/shard_map/ppermute | solution.py:69
  58.2 6.3 %collective-permute-done.3 = s32[102]{0:T(128)S(1)} collective-permute-done((s32[102]{0:T(128)S(1)}, s32[102]{0:T(128)S(1)}, u32[]{:S(2)}, u32[]{:S(2)}) %collective-permute-start.3) | collective-permute-done | bytes 440 | tf_op jit(solution)/shard_map/ppermute | solution.py:64
  67.4 7.9 %collective-permute-done.11.refs_4_ = bf16[400,512]{1,0:T(8,128)(2,1)} collective-permute-done((bf16[400,512]{1,0:T(8,128)(2,1)S(1)}, bf16[400,512]{1,0:T(8,128)(2,1)}, u32[]{:S(2)}, u32[]{:S(2)}) %collective-permute-start.11) | collective-permute-done | bytes 409632 | tf_op jit(solution)/shard_map/ppermute | solution.py:69
  77.8 4.2 %project.3 = (f32[384,512]{1,0:T(8,128)S(1)}, bf16[384,512]{1,0:T(8,128)(2,1)S(1)}) custom-call(s32[1]{0:T(128)} %bitcast.3.refs_0_, bf16[384,1600]{1,0:T(8,128)(2,1)S(1)} %copy-done.10, bf16[384,1664]{1,0:T(8,128)(2,1)} %collective-permute-done.4.refs_2_, bf16[400,512]{1,0:T(8,128)(2,1)} %get-tuple-element.38.refs_3_, ...), custom_call_target="tpu_custom_call" | custom-call | flops 1258291200 | bytes 5324800 | tf_op jit(solution)/shard_map/project/pallas_call | solution.py:85
  83.6 4.3 %project.4 = (f32[384,512]{1,0:T(8,128)S(1)}, bf16[384,512]{1,0:T(8,128)(2,1)S(1)}) custom-call(s32[1]{0:T(128)} %bitcast.3.refs_0_, bf16[384,1600]{1,0:T(8,128)(2,1)S(1)} %copy-done.10, bf16[384,1664]{1,0:T(8,128)(2,1)} %collective-permute-done.4.refs_2_, bf16[400,512]{1,0:T(8,128)(2,1)} %get-tuple-element.39.refs_3_, ...), custom_call_target="tpu_custom_call" | custom-call | flops 1258291200 | bytes 5324800 | tf_op jit(solution)/shard_map/project/pallas_call | solution.py:85
  88.5 3.4 %collective-permute-done.12.refs_5_ = bf16[400,512]{1,0:T(8,128)(2,1)S(1)} collective-permute-done((bf16[400,512]{1,0:T(8,128)(2,1)}, bf16[400,512]{1,0:T(8,128)(2,1)S(1)}, u32[]{:S(2)}, u32[]{:S(2)}) %collective-permute-start.12) | collective-permute-done | bytes 409632 | tf_op jit(solution)/shard_map/ppermute | solution.py:69
  91.9 4.4 %project.5 = (f32[384,512]{1,0:T(8,128)S(1)}, bf16[384,512]{1,0:T(8,128)(2,1)}) custom-call(s32[1]{0:T(128)} %bitcast.3.refs_0_, bf16[384,1600]{1,0:T(8,128)(2,1)S(1)} %copy-done.10, bf16[384,1664]{1,0:T(8,128)(2,1)} %collective-permute-done.4.refs_2_, bf16[400,512]{1,0:T(8,128)(2,1)S(1)} %get-tuple-element.52.refs_3_, ...), custom_call_target="tpu_custom_call" | custom-call | flops 1258291200 | bytes 5324800 | tf_op jit(solution)/shard_map/project/pallas_call | solution.py:85
  98.8 2.0 %collective-permute-start.16 = (bf16[400,512]{1,0:T(8,128)(2,1)}, bf16[400,512]{1,0:T(8,128)(2,1)}, u32[]{:S(2)}, u32[]{:S(2)}) collective-permute-start(bf16[400,512]{1,0:T(8,128)(2,1)} %collective-permute-done.15.refs_3_), channel_id=1, source_target_pairs={{0,8},{4,12},{8,16},{12,20},{16,24},{20,28},{24,0},{28,4},{1,9},{5... | collective-permute-start | bytes 1228808 | tf_op jit(solution)/shard_map/ppermute | solution.py:69
  101.6 3.3 %scores.1 = (f32[4,384,384]{2,1,0:T(8,128)S(1)}, f32[2,384]{1,0:T(2,128)S(1)}) custom-call(f32[384,512]{1,0:T(8,128)S(1)} %get-tuple-element.46.refs_0_, bf16[384,512]{1,0:T(8,128)(2,1)S(1)} %collective-permute-done.7.refs_1_, f32[384,512]{1,0:T(8,128)S(1)} %get-tuple-element.48.refs_2_, bf16[384,512]{1,0:T(8,128)(2,1)S(1)} %collective-permute-done.10.refs_3_, ...), custom_call_target="tpu_custom_call" | custom-call | flops 905969664 | bytes 4727808 | tf_op jit(solution)/shard_map/scores/pallas_call | solution.py:85
  104.9 6.2 %psum.14.refs_1_ = f32[2,384]{1,0:T(2,128)S(1)} all-reduce(f32[2,384]{1,0:T(2,128)S(1)} %get-tuple-element.55), channel_id=1, replica_groups=mesh['req'=8,'tp'=4] {'tp'}, use_global_device_ids=true, to_apply=%region_13.14 | all-reduce | flops 768 | bytes 6144 | tf_op jit(solution)/shard_map/psum | solution.py:491
  112.3 2.4 %attend.1.refs_1_ = bf16[384,512]{1,0:T(8,128)(2,1)S(1)} custom-call(f32[4,384,384]{2,1,0:T(8,128)S(1)} %get-tuple-element.54.refs_0_, f32[2,384]{1,0:T(2,128)S(1)} %psum.14.refs_1_, f32[1,384]{1,0:T(1,128)S(1)} %convert_element_type.89.refs_2_, f32[384,512]{1,0:T(8,128)S(1)} %copy-done.4, bf16[384,512]{1,0:T(8,128)(2,1)} %collective-permute-done.14.refs_4_), custom_call_target="tpu_custom_call" | custom-call | flops 150994944 | bytes 3936768 | tf_op jit(solution)/shard_map/attend/pallas_call | solution.py:85
  115.3 3.0 %project_out.2 = (bf16[2,400,384]{2,1,0:T(8,128)(2,1)S(1)}, f32[400,384]{1,0:T(8,128)S(1)}, f32[400,384]{1,0:T(8,128)S(1)}) custom-call(s32[3]{0:T(128)S(1)} %pad_add_fusion.1.refs_0_, bf16[384,512]{1,0:T(8,128)(2,1)S(1)} %attend.1.refs_1_, bf16[400,512]{1,0:T(8,128)(2,1)} %bitcast.17.refs_2_, bf16[400,512]{1,0:T(8,128)(2,1)} %collective-permute-done.15.refs_3_, ...), custom_call_target="tpu_custom_call" | custom-call | flops 629145600 | bytes 3874816 | tf_op jit(solution)/shard_map/project_out/pallas_call | solution.py:85
  118.4 6.8 %collective-permute-done.20.refs_1_ = bf16[384,512]{1,0:T(8,128)(2,1)S(1)} collective-permute-done((bf16[384,512]{1,0:T(8,128)(2,1)S(1)}, bf16[384,512]{1,0:T(8,128)(2,1)S(1)}, u32[]{:S(2)}, u32[]{:S(2)}) %collective-permute-start.20) | collective-permute-done | bytes 393248 | tf_op jit(solution)/shard_map/ppermute | solution.py:64
  125.2 3.0 %project_out.3 = (bf16[2,400,384]{2,1,0:T(8,128)(2,1)S(1)}, f32[400,384]{1,0:T(8,128)S(1)}, f32[400,384]{1,0:T(8,128)S(1)}) custom-call(s32[3]{0:T(128)S(1)} %pad_add_fusion.1.refs_0_, bf16[384,512]{1,0:T(8,128)(2,1)S(1)} %collective-permute-done.20.refs_1_, bf16[400,512]{1,0:T(8,128)(2,1)} %bitcast.17.refs_2_, ...), custom_call_target="tpu_custom_call" | custom-call | flops 629145600 | bytes 3874816 | tf_op jit(solution)/shard_map/project_out/pallas_call | solution.py:85
  132.4 6.1 %collective-permute-done.19.refs_2_ = bf16[400,384]{1,0:T(8,128)(2,1)S(1)} collective-permute-done((bf16[400,384]{1,0:T(8,128)(2,1)S(1)}, bf16[400,384]{1,0:T(8,128)(2,1)S(1)}, u32[]{:S(2)}, u32[]{:S(2)}) %collective-permute-start.19) | collective-permute-done | bytes 307232 | tf_op jit(solution)/shard_map/ppermute | solution.py:64
  138.8 5.9 %collective-permute-done.22.refs_4_ = bf16[400,384]{1,0:T(8,128)(2,1)S(1)} collective-permute-done((bf16[400,384]{1,0:T(8,128)(2,1)S(1)}, bf16[400,384]{1,0:T(8,128)(2,1)S(1)}, u32[]{:S(2)}, u32[]{:S(2)}) %collective-permute-start.22) | collective-permute-done | bytes 307232 | tf_op jit(solution)/shard_map/ppermute | solution.py:64
  144.7 2.3 %pack.1 = (bf16[8,48,1600]{2,1,0:T(8,128)(2,1)}, f32[4,384]{1,0:T(4,128)S(1)}) custom-call(bf16[400,384]{1,0:T(8,128)(2,1)S(1)} %get-tuple-element.62.refs_0_, f32[2,384]{1,0:T(2,128)S(1)} %get-tuple-element.63.refs_1_, f32[400,384]{1,0:T(8,128)S(1)} %get-tuple-element.64.refs_2_, bf16[2,400,384]{2,1,0:T(8,128)(2,1)S(1)} %collective-permute-done.21.refs_1_.refs_3_, ...), custom_call_target="tpu_custom_call" | custom-call | flops 471859200 | bytes 4568064 | tf_op jit(solution)/shard_map/pack/pallas_call | solution.py:85
  147.0 4.2 %all-to-all-start = ((bf16[8,48,1600]{2,1,0:T(8,128)(2,1)}), bf16[8,48,1600]{2,1,0:T(8,128)(2,1)S(1)}, u32[]{:S(2)}, u32[]{:S(2)}) async-start(bf16[8,48,1600]{2,1,0:T(8,128)(2,1)} %get-tuple-element.68), calls=%async_computation | async-start | bytes 2555904 | tf_op jit(solution)/shard_map/all_to_all | solution.py:510
  151.3 6.6 %psum.15 = f32[4,384]{1,0:T(4,128)S(1)} all-reduce(f32[4,384]{1,0:T(4,128)S(1)} %get-tuple-element.67), channel_id=1, replica_groups=mesh['req'=8,'tp'=4] {'tp'}, use_global_device_ids=true, to_apply=%region_15.16 | all-reduce | flops 1536 | bytes 12288 | tf_op jit(solution)/shard_map/psum | solution.py:512
  165.0 2.1 %collective-permute-done.24 = f32[3,1,8,24]{3,2,1,0:T(8,128)S(1)} collective-permute-done((f32[3,1,8,24]{3,2,1,0:T(8,128)S(1)}, f32[3,1,8,24]{3,2,1,0:T(8,128)S(1)}, u32[]{:S(2)}, u32[]{:S(2)}) %collective-permute-start.24) | collective-permute-done | bytes 2336 | tf_op jit(solution)/shard_map/ppermute | solution.py:64
  167.1 2.4 %collective-permute-start.25 = (f32[3,2,8,24]{3,2,1,0:T(8,128)S(1)}, f32[3,2,8,24]{3,2,1,0:T(8,128)S(1)}, u32[]{:S(2)}, u32[]{:S(2)}) collective-permute-start(f32[3,2,8,24]{3,2,1,0:T(8,128)S(1)} %pad_maximum_fusion.1), channel_id=1, source_target_pairs={{0,8},{4,12},{8,0},{12,4},{16,24},{20,28},{24,16},{28,20},{1,9},{5... | collective-permute-start | bytes 13832 | tf_op jit(solution)/shard_map/ppermute | solution.py:64
  169.4 3.1 %collective-permute-done.25 = f32[3,2,8,24]{3,2,1,0:T(8,128)S(1)} collective-permute-done((f32[3,2,8,24]{3,2,1,0:T(8,128)S(1)}, f32[3,2,8,24]{3,2,1,0:T(8,128)S(1)}, u32[]{:S(2)}, u32[]{:S(2)}) %collective-permute-start.25) | collective-permute-done | bytes 4640 | tf_op jit(solution)/shard_map/ppermute | solution.py:64
  172.6 4.4 %collective-permute-start.26 = (f32[3,4,8,24]{3,2,1,0:T(8,128)S(1)}, f32[3,4,8,24]{3,2,1,0:T(8,128)S(1)}, u32[]{:S(2)}, u32[]{:S(2)}) collective-permute-start(f32[3,4,8,24]{3,2,1,0:T(8,128)S(1)} %pad_maximum_fusion), channel_id=1, source_target_pairs={{0,16},{4,20},{8,24},{12,28},{16,0},{20,4},{24,8},{28,12},{1,17},{... | collective-permute-start | bytes 27656 | tf_op jit(solution)/shard_map/ppermute | solution.py:64
  177.0 6.9 %collective-permute-done.26 = f32[3,4,8,24]{3,2,1,0:T(8,128)S(1)} collective-permute-done((f32[3,4,8,24]{3,2,1,0:T(8,128)S(1)}, f32[3,4,8,24]{3,2,1,0:T(8,128)S(1)}, u32[]{:S(2)}, u32[]{:S(2)}) %collective-permute-start.26) | collective-permute-done | bytes 9248 | tf_op jit(solution)/shard_map/ppermute | solution.py:64
  184.1 2.8 %finish.1 = bf16[192,4,800]{2,1,0:T(4,128)(2,1)} custom-call(f32[3,192,128]{2,1,0:T(8,128)S(1)} %broadcast_in_dim.44.refs_0_, f32[4,800]{1,0:T(4,128)S(1)} %copy-done.7, f32[4,800]{1,0:T(4,128)S(1)} %copy-done.8, bf16[8,48,1600]{2,1,0:T(8,128)(2,1)S(1)} %all-to-all-done.refs_3_), custom_call_target="tpu_custom_call" | custom-call | flops 3686400 | bytes 2778112 | tf_op jit(solution)/shard_map/finish/pallas_call | solution.py:85
  (152 shorter events, 35.6 us)
Async XLA Ops:
  2.4 15.7 %collective-permute-start = (bf16[400,512]{1,0:T(8,128)(2,1)}, bf16[400,512]{1,0:T(8,128)(2,1)}, u32[]{:S(2)}, u32[]{:S(2)}) collective-permute-start(bf16[400,512]{1,0:T(8,128)(2,1)} %get-tuple-element.38.refs_3_), channel_id=1, source_target_pairs={{0,8},{4,12},{8,16},{12,20},{16,24},{20,28},{24,0},{28,4},{1,9},{5... | collective-permute-start | bytes 1228808 | tf_op jit(solution)/shard_map/ppermute | solution.py:69
  5.4 37.6 %collective-permute-start.5 = (bf16[400,512]{1,0:T(8,128)(2,1)}, bf16[400,512]{1,0:T(8,128)(2,1)}, u32[]{:S(2)}, u32[]{:S(2)}) collective-permute-start(bf16[400,512]{1,0:T(8,128)(2,1)} %get-tuple-element.38.refs_3_), channel_id=1, source_target_pairs={{0,24},{4,28},{8,0},{12,4},{16,8},{20,12},{24,16},{28,20},{1,25},{... | collective-permute-start | bytes 1228808 | tf_op jit(solution)/shard_map/ppermute | solution.py:69
  7.4 35.6 %collective-permute-start.8 = (bf16[400,512]{1,0:T(8,128)(2,1)}, bf16[400,512]{1,0:T(8,128)(2,1)}, u32[]{:S(2)}, u32[]{:S(2)}) collective-permute-start(bf16[400,512]{1,0:T(8,128)(2,1)} %get-tuple-element.39.refs_3_), channel_id=1, source_target_pairs={{0,8},{4,12},{8,16},{12,20},{16,24},{20,28},{24,0},{28,4},{1,9},{5... | collective-permute-start | bytes 1228808 | tf_op jit(solution)/shard_map/ppermute | solution.py:69
  18.1 25.1 %collective-permute-start.1 = (bf16[400,512]{1,0:T(8,128)(2,1)}, bf16[400,512]{1,0:T(8,128)(2,1)}, u32[]{:S(2)}, u32[]{:S(2)}) collective-permute-start(bf16[400,512]{1,0:T(8,128)(2,1)} %get-tuple-element.39.refs_3_), channel_id=1, source_target_pairs={{0,24},{4,28},{8,0},{12,4},{16,8},{20,12},{24,16},{28,20},{1,25},{... | collective-permute-start | bytes 1228808 | tf_op jit(solution)/shard_map/ppermute | solution.py:69
  35.3 40.1 %collective-permute-start.2 = (bf16[400,384]{1,0:T(8,128)(2,1)S(1)}, bf16[400,384]{1,0:T(8,128)(2,1)S(1)}, u32[]{:S(2)}, u32[]{:S(2)}) collective-permute-start(bf16[400,384]{1,0:T(8,128)(2,1)S(1)} %get-tuple-element.87), channel_id=1, source_target_pairs={{0,4},{4,0},{8,12},{12,8},{16,20},{20,16},{24,28},{28,24},{1,5},{5... | collective-permute-start | bytes 921608 | tf_op jit(solution)/shard_map/ppermute | solution.py:64
  42.3 34.5 %copy-start.10 = (bf16[384,1600]{1,0:T(8,128)(2,1)S(1)}, bf16[384,1600]{1,0:T(8,128)(2,1)}, u32[]{:S(2)}) copy-start(bf16[384,1600]{1,0:T(8,128)(2,1)} %copy-done.9) | copy-start | bytes 3686404
  42.3 34.5 %collective-permute-start.4 = (bf16[384,1664]{1,0:T(8,128)(2,1)}, bf16[384,1664]{1,0:T(8,128)(2,1)}, u32[]{:S(2)}, u32[]{:S(2)}) collective-permute-start(bf16[384,1664]{1,0:T(8,128)(2,1)} %get-tuple-element.44), channel_id=1, source_target_pairs={{0,4},{4,0},{8,12},{12,8},{16,20},{20,16},{24,28},{28,24},{1,5},{5... | collective-permute-start | bytes 3833864 | tf_op jit(solution)/shard_map/ppermute | solution.py:64
  43.0 14.4 %collective-permute-start.6 = (bf16[400,512]{1,0:T(8,128)(2,1)}, bf16[400,512]{1,0:T(8,128)(2,1)S(1)}, u32[]{:S(2)}, u32[]{:S(2)}) collective-permute-start(bf16[400,512]{1,0:T(8,128)(2,1)} %collective-permute-done.refs_4_), channel_id=1, source_target_pairs={{0,8},{4,12},{8,16},{12,20},{16,24},{20,28},{24,0},{28,4},{1,9},{5... | collective-permute-start | bytes 1228808 | tf_op jit(solution)/shard_map/ppermute | solution.py:69
  43.1 40.6 %collective-permute-start.9 = (bf16[400,512]{1,0:T(8,128)(2,1)}, bf16[400,512]{1,0:T(8,128)(2,1)}, u32[]{:S(2)}, u32[]{:S(2)}) collective-permute-start(bf16[400,512]{1,0:T(8,128)(2,1)} %collective-permute-done.8.refs_4_), channel_id=1, source_target_pairs={{0,8},{4,12},{8,16},{12,20},{16,24},{20,28},{24,0},{28,4},{1,9},{5... | collective-permute-start | bytes 1228808 | tf_op jit(solution)/shard_map/ppermute | solution.py:69
  43.2 21.3 %collective-permute-start.3 = (s32[102]{0:T(128)S(1)}, s32[102]{0:T(128)S(1)}, u32[]{:S(2)}, u32[]{:S(2)}) collective-permute-start(s32[102]{0:T(128)S(1)} %pad_add_fusion), channel_id=1, source_target_pairs={{0,4},{4,0},{8,12},{12,8},{16,20},{20,16},{24,28},{28,24},{1,5},{5... | collective-permute-start | bytes 1232 | tf_op jit(solution)/shard_map/ppermute | solution.py:64
  58.2 17.1 %collective-permute-start.11 = (bf16[400,512]{1,0:T(8,128)(2,1)S(1)}, bf16[400,512]{1,0:T(8,128)(2,1)}, u32[]{:S(2)}, u32[]{:S(2)}) collective-permute-start(bf16[400,512]{1,0:T(8,128)(2,1)S(1)} %get-tuple-element.52.refs_3_), channel_id=1, source_target_pairs={{0,8},{4,12},{8,16},{12,20},{16,24},{20,28},{24,0},{28,4},{1,9},{5... | collective-permute-start | bytes 1228808 | tf_op jit(solution)/shard_map/ppermute | solution.py:69
  64.6 24.0 %collective-permute-start.13 = (bf16[400,512]{1,0:T(8,128)(2,1)S(1)}, bf16[400,512]{1,0:T(8,128)(2,1)}, u32[]{:S(2)}, u32[]{:S(2)}) collective-permute-start(bf16[400,512]{1,0:T(8,128)(2,1)S(1)} %get-tuple-element.52.refs_3_), channel_id=1, source_target_pairs={{0,24},{4,28},{8,0},{12,4},{16,8},{20,12},{24,16},{28,20},{1,25},{... | collective-permute-start | bytes 1228808 | tf_op jit(solution)/shard_map/ppermute | solution.py:69
  75.3 16.6 %collective-permute-start.12 = (bf16[400,512]{1,0:T(8,128)(2,1)}, bf16[400,512]{1,0:T(8,128)(2,1)S(1)}, u32[]{:S(2)}, u32[]{:S(2)}) collective-permute-start(bf16[400,512]{1,0:T(8,128)(2,1)} %collective-permute-done.11.refs_4_), channel_id=1, source_target_pairs={{0,8},{4,12},{8,16},{12,20},{16,24},{20,28},{24,0},{28,4},{1,9},{5... | collective-permute-start | bytes 1228808 | tf_op jit(solution)/shard_map/ppermute | solution.py:69
  75.5 23.3 %collective-permute-start.15 = (bf16[400,512]{1,0:T(8,128)(2,1)}, bf16[400,512]{1,0:T(8,128)(2,1)}, u32[]{:S(2)}, u32[]{:S(2)}) collective-permute-start(bf16[400,512]{1,0:T(8,128)(2,1)} %bitcast.17.refs_2_), channel_id=1, source_target_pairs={{0,8},{4,12},{8,16},{12,20},{16,24},{20,28},{24,0},{28,4},{1,9},{5... | collective-permute-start | bytes 1228808 | tf_op jit(solution)/shard_map/ppermute | solution.py:69
  82.0 18.7 %collective-permute-start.7 = (bf16[384,512]{1,0:T(8,128)(2,1)S(1)}, bf16[384,512]{1,0:T(8,128)(2,1)S(1)}, u32[]{:S(2)}, u32[]{:S(2)}) collective-permute-start(bf16[384,512]{1,0:T(8,128)(2,1)S(1)} %get-tuple-element.47), channel_id=1, source_target_pairs={{0,4},{4,0},{8,12},{12,8},{16,20},{20,16},{24,28},{28,24},{1,5},{5... | collective-permute-start | bytes 1179656 | tf_op jit(solution)/shard_map/ppermute | solution.py:64
  87.9 13.7 %copy-start.13 = (f32[512]{0:T(512)S(1)}, f32[512]{0:T(512)}, u32[]{:S(2)}) copy-start(f32[512]{0:T(512)} %param.13) | copy-start | bytes 6148
  87.9 13.7 %collective-permute-start.10 = (bf16[384,512]{1,0:T(8,128)(2,1)S(1)}, bf16[384,512]{1,0:T(8,128)(2,1)S(1)}, u32[]{:S(2)}, u32[]{:S(2)}) collective-permute-start(bf16[384,512]{1,0:T(8,128)(2,1)S(1)} %get-tuple-element.49), channel_id=1, source_target_pairs={{0,4},{4,0},{8,12},{12,8},{16,20},{20,16},{24,28},{28,24},{1,5},{5... | collective-permute-start | bytes 1179656 | tf_op jit(solution)/shard_map/ppermute | solution.py:64
  96.3 14.8 %collective-permute-start.14 = (bf16[384,512]{1,0:T(8,128)(2,1)}, bf16[384,512]{1,0:T(8,128)(2,1)}, u32[]{:S(2)}, u32[]{:S(2)}) collective-permute-start(bf16[384,512]{1,0:T(8,128)(2,1)} %get-tuple-element.53), channel_id=1, source_target_pairs={{0,4},{4,0},{8,12},{12,8},{16,20},{20,16},{24,28},{28,24},{1,5},{5... | collective-permute-start | bytes 1179656 | tf_op jit(solution)/shard_map/ppermute | solution.py:64
  98.0 17.3 %collective-permute-start.17 = (bf16[400,512]{1,0:T(8,128)(2,1)}, bf16[400,512]{1,0:T(8,128)(2,1)}, u32[]{:S(2)}, u32[]{:S(2)}) collective-permute-start(bf16[400,512]{1,0:T(8,128)(2,1)} %bitcast.17.refs_2_), channel_id=1, source_target_pairs={{0,24},{4,28},{8,0},{12,4},{16,8},{20,12},{24,16},{28,20},{1,25},{... | collective-permute-start | bytes 1228808 | tf_op jit(solution)/shard_map/ppermute | solution.py:69
  98.8 16.5 %collective-permute-start.16 = (bf16[400,512]{1,0:T(8,128)(2,1)}, bf16[400,512]{1,0:T(8,128)(2,1)}, u32[]{:S(2)}, u32[]{:S(2)}) collective-permute-start(bf16[400,512]{1,0:T(8,128)(2,1)} %collective-permute-done.15.refs_3_), channel_id=1, source_target_pairs={{0,8},{4,12},{8,16},{12,20},{16,24},{20,28},{24,0},{28,4},{1,9},{5... | collective-permute-start | bytes 1228808 | tf_op jit(solution)/shard_map/ppermute | solution.py:69
  114.7 10.5 %collective-permute-start.20 = (bf16[384,512]{1,0:T(8,128)(2,1)S(1)}, bf16[384,512]{1,0:T(8,128)(2,1)S(1)}, u32[]{:S(2)}, u32[]{:S(2)}) collective-permute-start(bf16[384,512]{1,0:T(8,128)(2,1)S(1)} %attend.1.refs_1_), channel_id=1, source_target_pairs={{0,4},{4,0},{8,12},{12,8},{16,20},{20,16},{24,28},{28,24},{1,5},{5... | collective-permute-start | bytes 1179656 | tf_op jit(solution)/shard_map/ppermute | solution.py:64
  118.3 10.0 %collective-permute-start.18 = (bf16[2,400,384]{2,1,0:T(8,128)(2,1)S(1)}, bf16[2,400,384]{2,1,0:T(8,128)(2,1)S(1)}, u32[]{:S(2)}, u32[]{:S(2)}) collective-permute-start(bf16[2,400,384]{2,1,0:T(8,128)(2,1)S(1)} %get-tuple-element.60), channel_id=1, source_target_pairs={{0,1},{1,0},{2,3},{3,2},{4,5},{5,4},{6,7},{7,6},{8,9},{9,8},{10,11... | collective-permute-start | bytes 1843208 | tf_op jit(solution)/shard_map/ppermute | solution.py:64
  128.2 2.1 %collective-permute-start.21 = (bf16[2,400,384]{2,1,0:T(8,128)(2,1)S(1)}, bf16[2,400,384]{2,1,0:T(8,128)(2,1)S(1)}, u32[]{:S(2)}, u32[]{:S(2)}) collective-permute-start(bf16[2,400,384]{2,1,0:T(8,128)(2,1)S(1)} %get-tuple-element.65), channel_id=1, source_target_pairs={{0,1},{1,0},{2,3},{3,2},{4,5},{5,4},{6,7},{7,6},{8,9},{9,8},{10,11... | collective-permute-start | bytes 1843208 | tf_op jit(solution)/shard_map/ppermute | solution.py:64
  128.4 10.1 %collective-permute-start.19 = (bf16[400,384]{1,0:T(8,128)(2,1)S(1)}, bf16[400,384]{1,0:T(8,128)(2,1)S(1)}, u32[]{:S(2)}, u32[]{:S(2)}) collective-permute-start(bf16[400,384]{1,0:T(8,128)(2,1)S(1)} %far_sum.2), channel_id=1, source_target_pairs={{0,2},{1,3},{2,0},{3,1},{4,6},{5,7},{6,4},{7,5},{8,10},{9,11},{10,... | collective-permute-start | bytes 921608 | tf_op jit(solution)/shard_map/ppermute | solution.py:64
  130.4 14.3 %collective-permute-start.22 = (bf16[400,384]{1,0:T(8,128)(2,1)S(1)}, bf16[400,384]{1,0:T(8,128)(2,1)S(1)}, u32[]{:S(2)}, u32[]{:S(2)}) collective-permute-start(bf16[400,384]{1,0:T(8,128)(2,1)S(1)} %far_sum.3), channel_id=1, source_target_pairs={{0,2},{1,3},{2,0},{3,1},{4,6},{5,7},{6,4},{7,5},{8,10},{9,11},{10,... | collective-permute-start | bytes 921608 | tf_op jit(solution)/shard_map/ppermute | solution.py:64
  147.0 37.0 %all-to-all-start = ((bf16[8,48,1600]{2,1,0:T(8,128)(2,1)}), bf16[8,48,1600]{2,1,0:T(8,128)(2,1)S(1)}, u32[]{:S(2)}, u32[]{:S(2)}) async-start(bf16[8,48,1600]{2,1,0:T(8,128)(2,1)} %get-tuple-element.68), calls=%async_computation | async-start | bytes 2555904 | tf_op jit(solution)/shard_map/all_to_all | solution.py:510
  151.1 33.0 %copy-start.7 = (f32[4,800]{1,0:T(4,128)S(1)}, f32[4,800]{1,0:T(4,128)}, u32[]{:S(2)}) copy-start(f32[4,800]{1,0:T(4,128)} %refs_1_.2) | copy-start | bytes 38404
  151.1 33.0 %copy-start.8 = (f32[4,800]{1,0:T(4,128)S(1)}, f32[4,800]{1,0:T(4,128)}, u32[]{:S(2)}) copy-start(f32[4,800]{1,0:T(4,128)} %refs_2_.1) | copy-start | bytes 38404
  158.0 3.7 %collective-permute-start.23 = (f32[2,192]{1,0:T(2,128)S(1)}, f32[2,192]{1,0:T(2,128)S(1)}, u32[]{:S(2)}, u32[]{:S(2)}) collective-permute-start(f32[2,192]{1,0:T(2,128)S(1)} %multiply_reduce_fusion), channel_id=1, source_target_pairs={{0,4},{4,0},{8,12},{12,8},{16,20},{20,16},{24,28},{28,24},{1,5},{5... | collective-permute-start | bytes 4616 | tf_op jit(solution)/shard_map/ppermute | solution.py:64
  163.2 3.9 %collective-permute-start.24 = (f32[3,1,8,24]{3,2,1,0:T(8,128)S(1)}, f32[3,1,8,24]{3,2,1,0:T(8,128)S(1)}, u32[]{:S(2)}, u32[]{:S(2)}) collective-permute-start(f32[3,1,8,24]{3,2,1,0:T(8,128)S(1)} %constant_dynamic-update-slice_fusion), channel_id=1, source_target_pairs={{0,4},{4,0},{8,12},{12,8},{16,20},{20,16},{24,28},{28,24},{1,5},{5... | collective-permute-start | bytes 6920 | tf_op jit(solution)/shard_map/ppermute | solution.py:64
  167.1 5.5 %collective-permute-start.25 = (f32[3,2,8,24]{3,2,1,0:T(8,128)S(1)}, f32[3,2,8,24]{3,2,1,0:T(8,128)S(1)}, u32[]{:S(2)}, u32[]{:S(2)}) collective-permute-start(f32[3,2,8,24]{3,2,1,0:T(8,128)S(1)} %pad_maximum_fusion.1), channel_id=1, source_target_pairs={{0,8},{4,12},{8,0},{12,4},{16,24},{20,28},{24,16},{28,20},{1,9},{5... | collective-permute-start | bytes 13832 | tf_op jit(solution)/shard_map/ppermute | solution.py:64
  172.6 11.2 %collective-permute-start.26 = (f32[3,4,8,24]{3,2,1,0:T(8,128)S(1)}, f32[3,4,8,24]{3,2,1,0:T(8,128)S(1)}, u32[]{:S(2)}, u32[]{:S(2)}) collective-permute-start(f32[3,4,8,24]{3,2,1,0:T(8,128)S(1)} %pad_maximum_fusion), channel_id=1, source_target_pairs={{0,16},{4,20},{8,24},{12,28},{16,0},{20,4},{24,8},{28,12},{1,17},{... | collective-permute-start | bytes 27656 | tf_op jit(solution)/shard_map/ppermute | solution.py:64
  (15 other events, 87.0 us)

commit v5 on v4

--- a/solution.py
+++ b/solution.py
@@ -274,42 +274,46 @@
     sums_ref[first + 1 : first + 2, :] = jnp.sum(hidden * hidden, axis=0, keepdims=True)
 
 
-def hidden_kernel(kept_ref, near_ref, far_ref, token_ref, hidden_ref, sums_ref):
+def pack_rows(hidden, chosen_ref, rows_ref, half):
+    depth = hidden.shape[0]
+    count, _, rows, _ = rows_ref.shape
+    for patch in range(4):
+        picked = lax.dot_general(
+            chosen_ref[pl.ds(patch * rows * count, rows * count), :],
+            hidden,
+            (((1,), (1,)), ((), ())),
+            preferred_element_type=F32,
+        )
+        picked = picked.reshape(count, rows, depth).astype(BF16)
+        rows_ref[:, half, :, pl.ds(patch * depth, depth)] = picked
+
+
+def first_pack_kernel(kept_ref, near_ref, far_ref, token_ref, chosen_ref, rows_ref, sums_ref):
     hidden = hidden_of(kept_ref, near_ref, far_ref, token_ref)
-    hidden_ref[...] = hidden
+    pack_rows(hidden, chosen_ref, rows_ref, 0)
     sum_tokens(hidden, sums_ref)
 
 
-def pack_kernel(
-    first_ref, first_sums_ref, kept_ref, near_ref, far_ref, token_ref, own_ref, next_ref,
+def second_pack_kernel(
+    first_ref, first_sums_ref, kept_ref, near_ref, far_ref, token_ref, chosen_ref,
     rows_ref, sums_ref,
 ):
-    halves = [first_ref[...], hidden_of(kept_ref, near_ref, far_ref, token_ref)]
-    depth = halves[0].shape[0]
-    count, rows, _ = rows_ref.shape
-    rows = rows // 2
-    for patch in range(4):
-        for half, (hidden, chosen_ref) in enumerate(zip(halves, (own_ref, next_ref))):
-            chosen = chosen_ref[pl.ds(patch * rows * count, rows * count), :]
-            picked = lax.dot_general(
-                chosen, hidden, (((1,), (1,)), ((), ())), preferred_element_type=F32
-            )
-            picked = picked.reshape(count, rows, depth).astype(BF16)
-            rows_ref[:, pl.ds(half * rows, rows), pl.ds(patch * depth, depth)] = picked
+    hidden = hidden_of(kept_ref, near_ref, far_ref, token_ref)
+    rows_ref[:, 0] = first_ref[:, 0]
+    pack_rows(hidden, chosen_ref, rows_ref, 1)
     sums_ref[0:2, :] = first_sums_ref[...]
-    sum_tokens(halves[1], sums_ref, 2)
+    sum_tokens(hidden, sums_ref, 2)
 
 
 def finish_kernel(stats_ref, gain_ref, bias_ref, rows_ref, out_ref):
-    count, rows, _ = rows_ref.shape
-    rows = rows // 2
+    count, _, rows, _ = rows_ref.shape
     depth = out_ref.shape[2] // 2
     for i in range(count):
         to = pl.ds(i * rows, rows)
         scale, shift, live = (stats_ref[j, to][:, 0:1] for j in range(3))
         for patch in range(4):
             part = slice(patch * depth, (patch + 1) * depth)
-            parts = [rows_ref[i, :rows, part].astype(F32), rows_ref[i ^ 1, rows:, part].astype(F32)]
+            parts = [rows_ref[i, 0, :, part].astype(F32), rows_ref[i ^ 1, 1, :, part].astype(F32)]
             values = jnp.concatenate(parts[::-1] if i % 2 else parts, axis=1)
             gain, bias = gain_ref[patch : patch + 1, :], bias_ref[patch : patch + 1, :]
             values = (values * scale + shift) * gain + live * bias
@@ -434,11 +438,12 @@
     v_up = ring(after(w_v, k_down))
     v_down = ring(after(w_v, q_far), -1)
     v_far = ring(v_up)
-    o_up = ring(after(w_o, v_up))
-    o_down = ring(after(w_o, v_down), -1)
-    o_far = ring(o_up)
     q_blocks, k_blocks = [w_q, q_up, q_far, q_down], [w_k, k_up, k_far, k_down]
-    v_blocks, o_blocks = [w_v, v_up, v_far, v_down], [w_o, o_up, o_far, o_down]
+    v_blocks = [w_v, v_up, v_far, v_down]
+
+    places = jnp.stack([plane, side, column]).astype(jnp.int32)
+    mine, others = norm_tokens(places[1:2], after(tokens, w_q), norm_gain)
+    theirs = swap(others, "req", 1)
 
     own_routes = after(jnp.concatenate([owners, grids.reshape(-1)]), k_down)
     chosen, in_row = [], []
@@ -455,22 +460,20 @@
         in_row.append(jnp.any(picks, axis=1).astype(F32))
         if routes is own_routes:
             segment, row_live = tokens_of, (row_tokens[:, 0] >= 0).astype(F32)
-    token_mine = lax.dynamic_slice_in_dim(tokens, column * quarter, quarter, 1).T
+    token_mine = lax.dynamic_slice_in_dim(after(tokens, k_down), column * quarter, quarter, 1).T
     token_mine = token_mine.reshape(2, quarter // 2, token_count)
     token_parts = [
         lax.dynamic_index_in_dim(token_mine, side, 0, keepdims=False),
         swap(lax.dynamic_index_in_dim(token_mine, 1 - side, 0, keepdims=False), "req", 1),
     ]
 
-    places = jnp.stack([plane, side, column]).astype(jnp.int32)
-    mine, others = norm_tokens(places[1:2], after(tokens, w_q), norm_gain)
-    theirs = swap(others, "req", 1)
-
     mine = after(mine, *token_parts, *chosen)
     queries, q_peer = project(places[0:1], mine, theirs, q_blocks)
     q_got = swap(q_peer, "req", 1)
     key_vecs, k_peer = project(places[0:1], mine, theirs, k_blocks)
     k_got = swap(k_peer, "req", 1)
+    o_up, o_down = ring(after(w_o, v_up, q_peer)), ring(after(w_o, v_down, k_peer), -1)
+    o_blocks = [w_o, o_up, ring(o_up), o_down]
     values, v_peer = project(places[0:1], mine, theirs, v_blocks)
     v_got = swap(v_peer, "req", 1)
     raw, sums = call(
@@ -498,14 +501,21 @@
         near = swap(sent, "tp", 1)
         (far,) = call(far_kernel, "far_sum", (array(kept.shape, BF16),), (kept_far, near), 0)
         parts.append((kept, near, swap(far, "tp", 2), token_part))
-    out = (array(kept.shape, BF16), array((2, token_count), F32))
-    hidden, own_sums = call(hidden_kernel, "hidden", out, parts[0], 0)
+    packed = array((devices_req, 2, capacity, 2 * quarter), BF16)
+    flops = 2 * chosen[0].size * quarter
+    first_rows, own_sums = call(
+        first_pack_kernel,
+        "first_pack",
+        (packed, array((2, token_count), F32)),
+        (*parts[0], chosen[0]),
+        flops,
+    )
     rows, token_sums = call(
-        pack_kernel,
-        "pack",
-        (array((devices_req, 2 * capacity, 2 * quarter), BF16), array((4, token_count), F32)),
-        (hidden, own_sums, *parts[1], *chosen),
-        2 * chosen[0].size * quarter,
+        second_pack_kernel,
+        "second_pack",
+        (packed, array((4, token_count), F32)),
+        (first_rows, own_sums, *parts[1], chosen[1]),
+        flops,
     )
     arrived = lax.all_to_all(rows, "req", split_axis=0, concat_axis=0, tiled=True)
 

time: 188 us -> 184 us (0.979)
  waiting for transfers between devices: 73.6 us -> 61.6 us
  starting transfers between devices: 45.5 us -> 50.9 us
  local copies, waits for them, and re-layouts: 14.1 us -> 16.9 us
    ppermute x12, waiting for transfers between devices: 33.4 us -> 27.4 us  [ring(): lax.ppermute(value, 'req', [(i, (i + 2 * step) % count) for i in range(co...]
    ppermute x15, waiting for transfers between devices: 40.2 us -> 34.2 us  [swap(): return lax.ppermute(value, axis, [(i, i ^ bit) for i in range(count)])]
    ppermute x12, starting transfers between devices: 19.6 us -> 24.7 us  [ring(): lax.ppermute(value, 'req', [(i, (i + 2 * step) % count) for i in range(co...]
    optimization_barrier x0 -> x1, local copies, waits for them, and re-layouts: none -> 2.73 us  [after(): return lax.optimization_barrier((value,) + first)[0]]
    unnamed x42 -> x49, local copies, waits for them, and re-layouts: 7.72 us -> 9.03 us
  transfers between devices with their start and end apart: 28 -> 28, of which waited for: 14 -> 15; matrix products, arithmetic and copies ran while one was open for 7% -> 7% of each run, Pallas kernels for 16% -> 16%
where the time goes in v5:
time: 184 us; the launch traced here: 183 us
  waiting for transfers between devices  61.6 us (33%)
  starting transfers between devices  50.9 us (28%)
  Pallas kernels  35.5 us (19%)
  local copies, waits for them, and re-layouts  16.9 us (9%)
  blocking collectives  12.8 us (7%)
  other arithmetic  4.93 us (3%)
    pallas_call x14, Pallas kernels, call(): pl.pallas_call(untied, grid=(1,), out_shape=tuple(out), in_specs=[pl.Bloc...  35.5 us
    ppermute x15, waiting for transfers between devices, swap(): return lax.ppermute(value, axis, [(i, i ^ bit) for i in range(count)])  34.2 us
    ppermute x12, waiting for transfers between devices, ring(): lax.ppermute(value, 'req', [(i, (i + 2 * step) % count) for i in range(co...  27.4 us
    ppermute x12, starting transfers between devices, ring(): lax.ppermute(value, 'req', [(i, (i + 2 * step) % count) for i in range(co...  24.7 us
    ppermute x15, starting transfers between devices, swap(): return lax.ppermute(value, axis, [(i, i ^ bit) for i in range(count)])  21.4 us
    unnamed x49, local copies, waits for them, and re-layouts  9.03 us
    psum x1, blocking collectives, body(): token_sums = lax.psum(token_sums, 'tp').reshape(2, 2, token_count)  6.56 us
    psum x1, blocking collectives, body(): lax.psum(sums, 'tp')  6.25 us
  transfers between devices with their start and end apart: 28, of which 15 were waited for; matrix products, arithmetic and copies ran while one was open for 7% of the time, Pallas kernels for 16%

profile of v5, /device:TPU:0, one launch (start us, length us, event | category | flops | bytes accessed | tf_op | source)
XLA Modules:
  0.0 183.1 jit_solution(17643567388668266853)
XLA Ops:
  2.3 3.0 %collective-permute-start = (bf16[400,512]{1,0:T(8,128)(2,1)S(1)}, bf16[400,512]{1,0:T(8,128)(2,1)}, u32[]{:S(2)}, u32[]{:S(2)}) collective-permute-start(bf16[400,512]{1,0:T(8,128)(2,1)S(1)} %get-tuple-element.39.refs_3_), channel_id=1, source_target_pairs={{0,8},{4,12},{8,16},{12,20},{16,24},{20,28},{24,0},{28,4},{1,9},{5... | collective-permute-start | bytes 1228808 | tf_op jit(solution)/shard_map/ppermute | solution.py:69
  5.3 2.0 %collective-permute-start.5 = (bf16[400,512]{1,0:T(8,128)(2,1)S(1)}, bf16[400,512]{1,0:T(8,128)(2,1)}, u32[]{:S(2)}, u32[]{:S(2)}) collective-permute-start(bf16[400,512]{1,0:T(8,128)(2,1)S(1)} %get-tuple-element.39.refs_3_), channel_id=1, source_target_pairs={{0,24},{4,28},{8,0},{12,4},{16,8},{20,12},{24,16},{28,20},{1,25},{... | collective-permute-start | bytes 1228808 | tf_op jit(solution)/shard_map/ppermute | solution.py:69
  7.3 10.4 %collective-permute-done.refs_4_ = bf16[400,512]{1,0:T(8,128)(2,1)} collective-permute-done((bf16[400,512]{1,0:T(8,128)(2,1)S(1)}, bf16[400,512]{1,0:T(8,128)(2,1)}, u32[]{:S(2)}, u32[]{:S(2)}) %collective-permute-start) | collective-permute-done | bytes 409632 | tf_op jit(solution)/shard_map/ppermute | solution.py:69
  17.8 10.8 %collective-permute-start.1 = (bf16[400,512]{1,0:T(8,128)(2,1)S(1)}, bf16[400,512]{1,0:T(8,128)(2,1)}, u32[]{:S(2)}, u32[]{:S(2)}) collective-permute-start(bf16[400,512]{1,0:T(8,128)(2,1)S(1)} %get-tuple-element.40.refs_3_), channel_id=1, source_target_pairs={{0,24},{4,28},{8,0},{12,4},{16,8},{20,12},{24,16},{28,20},{1,25},{... | collective-permute-start | bytes 1228808 | tf_op jit(solution)/shard_map/ppermute | solution.py:69
  31.0 4.3 %norm_tokens.1 = (bf16[384,1600]{1,0:T(8,128)(2,1)S(1)}, bf16[384,1664]{1,0:T(8,128)(2,1)}) custom-call(s32[1]{0:T(128)} %bitcast.4.refs_0_, bf16[384,3200]{1,0:T(8,128)(2,1)S(1)} %copy-done, f32[1,3200]{1,0:T(1,128)S(1)} %broadcast_in_dim.39.refs_2_), custom_call_target="tpu_custom_call" | custom-call | bytes 4977152 | tf_op jit(solution)/shard_map/norm_tokens/pallas_call | solution.py:85
  38.2 4.4 %collective-permute-start.9 = (bf16[400,512]{1,0:T(8,128)(2,1)}, bf16[400,512]{1,0:T(8,128)(2,1)}, u32[]{:S(2)}, u32[]{:S(2)}) collective-permute-start(bf16[400,512]{1,0:T(8,128)(2,1)} %collective-permute-done.8.refs_4_), channel_id=1, source_target_pairs={{0,8},{4,12},{8,16},{12,20},{16,24},{20,28},{24,0},{28,4},{1,9},{5... | collective-permute-start | bytes 1228808 | tf_op jit(solution)/shard_map/ppermute | solution.py:69
  44.7 2.7 %copy.25 = bf16[384,3200]{0,1:T(8,128)(2,1)} copy(bf16[384,3200]{1,0:T(8,128)(2,1)S(1)} %copy-done.1) | data formatting | bytes 4915200 | tf_op jit(solution)/shard_map/optimization_barrier | solution.py:332
  50.7 2.1 %collective-permute-done.6.refs_5_ = bf16[400,512]{1,0:T(8,128)(2,1)S(1)} collective-permute-done((bf16[400,512]{1,0:T(8,128)(2,1)}, bf16[400,512]{1,0:T(8,128)(2,1)S(1)}, u32[]{:S(2)}, u32[]{:S(2)}) %collective-permute-start.6) | collective-permute-done | bytes 409632 | tf_op jit(solution)/shard_map/ppermute | solution.py:69
  54.3 4.6 %collective-permute-done.3 = s32[102]{0:T(128)S(1)} collective-permute-done((s32[102]{0:T(128)S(1)}, s32[102]{0:T(128)S(1)}, u32[]{:S(2)}, u32[]{:S(2)}) %collective-permute-start.3) | collective-permute-done | bytes 440 | tf_op jit(solution)/shard_map/ppermute | solution.py:64
  61.5 9.0 %collective-permute-done.11.refs_4_ = bf16[400,512]{1,0:T(8,128)(2,1)} collective-permute-done((bf16[400,512]{1,0:T(8,128)(2,1)}, bf16[400,512]{1,0:T(8,128)(2,1)}, u32[]{:S(2)}, u32[]{:S(2)}) %collective-permute-start.11) | collective-permute-done | bytes 409632 | tf_op jit(solution)/shard_map/ppermute | solution.py:69
  72.8 4.4 %project.3 = (f32[384,512]{1,0:T(8,128)S(1)}, bf16[384,512]{1,0:T(8,128)(2,1)S(1)}) custom-call(s32[1]{0:T(128)} %bitcast.3.refs_0_, bf16[384,1600]{1,0:T(8,128)(2,1)S(1)} %copy-done.11, bf16[384,1664]{1,0:T(8,128)(2,1)} %collective-permute-done.4.refs_2_, bf16[400,512]{1,0:T(8,128)(2,1)S(1)} %copy-done.15, bf16[400,512]{1,0:T(8,128)(2,1)} %collective-permute-done.refs_4_, ...), custom_call_target="tpu_custom_call" | custom-call | flops 1258291200 | bytes 5324800 | tf_op jit(solution)/shard_map/project/pallas_call | solution.py:85
  77.3 1.8 %collective-permute-start.7 = (bf16[384,512]{1,0:T(8,128)(2,1)S(1)}, bf16[384,512]{1,0:T(8,128)(2,1)S(1)}, u32[]{:S(2)}, u32[]{:S(2)}) collective-permute-start(bf16[384,512]{1,0:T(8,128)(2,1)S(1)} %get-tuple-element.49), channel_id=1, source_target_pairs={{0,4},{4,0},{8,12},{12,8},{16,20},{20,16},{24,28},{28,24},{1,5},{5... | collective-permute-start | bytes 1179656 | tf_op jit(solution)/shard_map/ppermute | solution.py:64
  79.1 4.4 %project.4 = (f32[384,512]{1,0:T(8,128)S(1)}, bf16[384,512]{1,0:T(8,128)(2,1)S(1)}) custom-call(s32[1]{0:T(128)} %bitcast.3.refs_0_, bf16[384,1600]{1,0:T(8,128)(2,1)S(1)} %copy-done.11, bf16[384,1664]{1,0:T(8,128)(2,1)} %collective-permute-done.4.refs_2_, bf16[400,512]{1,0:T(8,128)(2,1)S(1)} %copy-done.13, bf16[400,512]{1,0:T(8,128)(2,1)} %collective-permute-done.8.refs_4_, ...), custom_call_target="tpu_custom_call" | custom-call | flops 1258291200 | bytes 5324800 | tf_op jit(solution)/shard_map/project/pallas_call | solution.py:85
  85.3 2.5 %collective-permute-done.12.refs_5_ = bf16[400,512]{1,0:T(8,128)(2,1)S(1)} collective-permute-done((bf16[400,512]{1,0:T(8,128)(2,1)}, bf16[400,512]{1,0:T(8,128)(2,1)S(1)}, u32[]{:S(2)}, u32[]{:S(2)}) %collective-permute-start.12) | collective-permute-done | bytes 409632 | tf_op jit(solution)/shard_map/ppermute | solution.py:69
  87.8 4.3 %project.5 = (f32[384,512]{1,0:T(8,128)S(1)}, bf16[384,512]{1,0:T(8,128)(2,1)}) custom-call(s32[1]{0:T(128)} %bitcast.3.refs_0_, bf16[384,1600]{1,0:T(8,128)(2,1)S(1)} %copy-done.11, bf16[384,1664]{1,0:T(8,128)(2,1)} %collective-permute-done.4.refs_2_, bf16[400,512]{1,0:T(8,128)(2,1)} %get-tuple-element.54.refs_3_, ...), custom_call_target="tpu_custom_call" | custom-call | flops 1258291200 | bytes 5324800 | tf_op jit(solution)/shard_map/project/pallas_call | solution.py:85
  97.6 3.3 %scores.1 = (f32[4,384,384]{2,1,0:T(8,128)S(1)}, f32[2,384]{1,0:T(2,128)S(1)}) custom-call(f32[384,512]{1,0:T(8,128)S(1)} %get-tuple-element.48.refs_0_, bf16[384,512]{1,0:T(8,128)(2,1)S(1)} %collective-permute-done.7.refs_1_, f32[384,512]{1,0:T(8,128)S(1)} %get-tuple-element.50.refs_2_, bf16[384,512]{1,0:T(8,128)(2,1)S(1)} %collective-permute-done.10.refs_3_, ...), custom_call_target="tpu_custom_call" | custom-call | flops 905969664 | bytes 4727808 | tf_op jit(solution)/shard_map/scores/pallas_call | solution.py:85
  100.9 6.2 %psum.14.refs_1_ = f32[2,384]{1,0:T(2,128)S(1)} all-reduce(f32[2,384]{1,0:T(2,128)S(1)} %get-tuple-element.57), channel_id=1, replica_groups=mesh['req'=8,'tp'=4] {'tp'}, use_global_device_ids=true, to_apply=%region_13.14 | all-reduce | flops 768 | bytes 6144 | tf_op jit(solution)/shard_map/psum | solution.py:494
  108.3 2.4 %attend.1.refs_1_ = bf16[384,512]{1,0:T(8,128)(2,1)S(1)} custom-call(f32[4,384,384]{2,1,0:T(8,128)S(1)} %get-tuple-element.56.refs_0_, f32[2,384]{1,0:T(2,128)S(1)} %psum.14.refs_1_, f32[1,384]{1,0:T(1,128)S(1)} %convert_element_type.89.refs_2_, f32[384,512]{1,0:T(8,128)S(1)} %copy-done.5, bf16[384,512]{1,0:T(8,128)(2,1)} %collective-permute-done.14.refs_4_), custom_call_target="tpu_custom_call" | custom-call | flops 150994944 | bytes 3936768 | tf_op jit(solution)/shard_map/attend/pallas_call | solution.py:85
  111.1 3.1 %collective-permute-done.16.refs_4_ = bf16[400,512]{1,0:T(8,128)(2,1)} collective-permute-done((bf16[400,512]{1,0:T(8,128)(2,1)}, bf16[400,512]{1,0:T(8,128)(2,1)}, u32[]{:S(2)}, u32[]{:S(2)}) %collective-permute-start.16) | collective-permute-done | bytes 409632 | tf_op jit(solution)/shard_map/ppermute | solution.py:69
  114.2 3.0 %project_out.2 = (bf16[2,400,384]{2,1,0:T(8,128)(2,1)S(1)}, f32[400,384]{1,0:T(8,128)S(1)}, f32[400,384]{1,0:T(8,128)S(1)}) custom-call(s32[3]{0:T(128)S(1)} %pad_add_fusion.1.refs_0_, bf16[384,512]{1,0:T(8,128)(2,1)S(1)} %attend.1.refs_1_, bf16[400,512]{1,0:T(8,128)(2,1)} %bitcast.17.refs_2_, bf16[400,512]{1,0:T(8,128)(2,1)} %collective-permute-done.15.refs_3_, ...), custom_call_target="tpu_custom_call" | custom-call | flops 629145600 | bytes 3874816 | tf_op jit(solution)/shard_map/project_out/pallas_call | solution.py:85
  117.3 3.9 %collective-permute-done.20.refs_1_ = bf16[384,512]{1,0:T(8,128)(2,1)S(1)} collective-permute-done((bf16[384,512]{1,0:T(8,128)(2,1)S(1)}, bf16[384,512]{1,0:T(8,128)(2,1)S(1)}, u32[]{:S(2)}, u32[]{:S(2)}) %collective-permute-start.20) | collective-permute-done | bytes 393248 | tf_op jit(solution)/shard_map/ppermute | solution.py:64
  121.2 3.0 %project_out.3 = (bf16[2,400,384]{2,1,0:T(8,128)(2,1)S(1)}, f32[400,384]{1,0:T(8,128)S(1)}, f32[400,384]{1,0:T(8,128)S(1)}) custom-call(s32[3]{0:T(128)S(1)} %pad_add_fusion.1.refs_0_, bf16[384,512]{1,0:T(8,128)(2,1)S(1)} %collective-permute-done.20.refs_1_, bf16[400,512]{1,0:T(8,128)(2,1)} %bitcast.17.refs_2_, ...), custom_call_target="tpu_custom_call" | custom-call | flops 629145600 | bytes 3874816 | tf_op jit(solution)/shard_map/project_out/pallas_call | solution.py:85
  128.4 6.1 %collective-permute-done.19.refs_2_ = bf16[400,384]{1,0:T(8,128)(2,1)S(1)} collective-permute-done((bf16[400,384]{1,0:T(8,128)(2,1)S(1)}, bf16[400,384]{1,0:T(8,128)(2,1)S(1)}, u32[]{:S(2)}, u32[]{:S(2)}) %collective-permute-start.19) | collective-permute-done | bytes 307232 | tf_op jit(solution)/shard_map/ppermute | solution.py:64
  135.3 5.4 %collective-permute-done.22.refs_4_ = bf16[400,384]{1,0:T(8,128)(2,1)S(1)} collective-permute-done((bf16[400,384]{1,0:T(8,128)(2,1)S(1)}, bf16[400,384]{1,0:T(8,128)(2,1)S(1)}, u32[]{:S(2)}, u32[]{:S(2)}) %collective-permute-start.22) | collective-permute-done | bytes 307232 | tf_op jit(solution)/shard_map/ppermute | solution.py:64
  142.5 4.8 %all-to-all-start = ((bf16[8,2,24,1600]{3,2,1,0:T(8,128)(2,1)}), bf16[8,2,24,1600]{3,2,1,0:T(8,128)(2,1)S(1)}, u32[]{:S(2)}, u32[]{:S(2)}) async-start(bf16[8,2,24,1600]{3,2,1,0:T(8,128)(2,1)} %get-tuple-element.70), calls=%async_computation | async-start | bytes 2555904 | tf_op jit(solution)/shard_map/all_to_all | solution.py:520
  147.4 6.6 %psum.15 = f32[4,384]{1,0:T(4,128)S(1)} all-reduce(f32[4,384]{1,0:T(4,128)S(1)} %get-tuple-element.69), channel_id=1, replica_groups=mesh['req'=8,'tp'=4] {'tp'}, use_global_device_ids=true, to_apply=%region_15.16 | all-reduce | flops 1536 | bytes 12288 | tf_op jit(solution)/shard_map/psum | solution.py:522
  161.1 2.1 %collective-permute-done.24 = f32[3,1,8,24]{3,2,1,0:T(8,128)S(1)} collective-permute-done((f32[3,1,8,24]{3,2,1,0:T(8,128)S(1)}, f32[3,1,8,24]{3,2,1,0:T(8,128)S(1)}, u32[]{:S(2)}, u32[]{:S(2)}) %collective-permute-start.24) | collective-permute-done | bytes 2336 | tf_op jit(solution)/shard_map/ppermute | solution.py:64
  163.2 2.3 %collective-permute-start.25 = (f32[3,2,8,24]{3,2,1,0:T(8,128)S(1)}, f32[3,2,8,24]{3,2,1,0:T(8,128)S(1)}, u32[]{:S(2)}, u32[]{:S(2)}) collective-permute-start(f32[3,2,8,24]{3,2,1,0:T(8,128)S(1)} %pad_maximum_fusion.1), channel_id=1, source_target_pairs={{0,8},{4,12},{8,0},{12,4},{16,24},{20,28},{24,16},{28,20},{1,9},{5... | collective-permute-start | bytes 13832 | tf_op jit(solution)/shard_map/ppermute | solution.py:64
  165.5 3.2 %collective-permute-done.25 = f32[3,2,8,24]{3,2,1,0:T(8,128)S(1)} collective-permute-done((f32[3,2,8,24]{3,2,1,0:T(8,128)S(1)}, f32[3,2,8,24]{3,2,1,0:T(8,128)S(1)}, u32[]{:S(2)}, u32[]{:S(2)}) %collective-permute-start.25) | collective-permute-done | bytes 4640 | tf_op jit(solution)/shard_map/ppermute | solution.py:64
  168.7 4.4 %collective-permute-start.26 = (f32[3,4,8,24]{3,2,1,0:T(8,128)S(1)}, f32[3,4,8,24]{3,2,1,0:T(8,128)S(1)}, u32[]{:S(2)}, u32[]{:S(2)}) collective-permute-start(f32[3,4,8,24]{3,2,1,0:T(8,128)S(1)} %pad_maximum_fusion), channel_id=1, source_target_pairs={{0,16},{4,20},{8,24},{12,28},{16,0},{20,4},{24,8},{28,12},{1,17},{... | collective-permute-start | bytes 27656 | tf_op jit(solution)/shard_map/ppermute | solution.py:64
  173.1 6.9 %collective-permute-done.26 = f32[3,4,8,24]{3,2,1,0:T(8,128)S(1)} collective-permute-done((f32[3,4,8,24]{3,2,1,0:T(8,128)S(1)}, f32[3,4,8,24]{3,2,1,0:T(8,128)S(1)}, u32[]{:S(2)}, u32[]{:S(2)}) %collective-permute-start.26) | collective-permute-done | bytes 9248 | tf_op jit(solution)/shard_map/ppermute | solution.py:64
  180.3 2.8 %finish.1 = bf16[192,4,800]{2,1,0:T(4,128)(2,1)} custom-call(f32[3,192,128]{2,1,0:T(8,128)S(1)} %broadcast_in_dim.44.refs_0_, f32[4,800]{1,0:T(4,128)S(1)} %copy-done.8, f32[4,800]{1,0:T(4,128)S(1)} %copy-done.9, bf16[8,2,24,1600]{3,2,1,0:T(8,128)(2,1)S(1)} %all-to-all-done.refs_3_), custom_call_target="tpu_custom_call" | custom-call | flops 3686400 | bytes 2778112 | tf_op jit(solution)/shard_map/finish/pallas_call | solution.py:85
  (160 shorter events, 42.4 us)
Async XLA Ops:
  2.3 35.6 %copy-start.12 = (bf16[400,512]{1,0:T(8,128)(2,1)}, bf16[400,512]{1,0:T(8,128)(2,1)S(1)}, u32[]{:S(2)}) copy-start(bf16[400,512]{1,0:T(8,128)(2,1)S(1)} %get-tuple-element.40.refs_3_) | copy-start | bytes 1228804
  2.3 35.6 %copy-start.14 = (bf16[400,512]{1,0:T(8,128)(2,1)}, bf16[400,512]{1,0:T(8,128)(2,1)S(1)}, u32[]{:S(2)}) copy-start(bf16[400,512]{1,0:T(8,128)(2,1)S(1)} %get-tuple-element.39.refs_3_) | copy-start | bytes 1228804
  2.3 15.5 %collective-permute-start = (bf16[400,512]{1,0:T(8,128)(2,1)S(1)}, bf16[400,512]{1,0:T(8,128)(2,1)}, u32[]{:S(2)}, u32[]{:S(2)}) collective-permute-start(bf16[400,512]{1,0:T(8,128)(2,1)S(1)} %get-tuple-element.39.refs_3_), channel_id=1, source_target_pairs={{0,8},{4,12},{8,16},{12,20},{16,24},{20,28},{24,0},{28,4},{1,9},{5... | collective-permute-start | bytes 1228808 | tf_op jit(solution)/shard_map/ppermute | solution.py:69
  5.3 32.9 %collective-permute-start.5 = (bf16[400,512]{1,0:T(8,128)(2,1)S(1)}, bf16[400,512]{1,0:T(8,128)(2,1)}, u32[]{:S(2)}, u32[]{:S(2)}) collective-permute-start(bf16[400,512]{1,0:T(8,128)(2,1)S(1)} %get-tuple-element.39.refs_3_), channel_id=1, source_target_pairs={{0,24},{4,28},{8,0},{12,4},{16,8},{20,12},{24,16},{28,20},{1,25},{... | collective-permute-start | bytes 1228808 | tf_op jit(solution)/shard_map/ppermute | solution.py:69
  7.3 30.9 %collective-permute-start.8 = (bf16[400,512]{1,0:T(8,128)(2,1)S(1)}, bf16[400,512]{1,0:T(8,128)(2,1)}, u32[]{:S(2)}, u32[]{:S(2)}) collective-permute-start(bf16[400,512]{1,0:T(8,128)(2,1)S(1)} %get-tuple-element.40.refs_3_), channel_id=1, source_target_pairs={{0,8},{4,12},{8,16},{12,20},{16,24},{20,28},{24,0},{28,4},{1,9},{5... | collective-permute-start | bytes 1228808 | tf_op jit(solution)/shard_map/ppermute | solution.py:69
  17.8 25.1 %collective-permute-start.1 = (bf16[400,512]{1,0:T(8,128)(2,1)S(1)}, bf16[400,512]{1,0:T(8,128)(2,1)}, u32[]{:S(2)}, u32[]{:S(2)}) collective-permute-start(bf16[400,512]{1,0:T(8,128)(2,1)S(1)} %get-tuple-element.40.refs_3_), channel_id=1, source_target_pairs={{0,24},{4,28},{8,0},{12,4},{16,8},{20,12},{24,16},{28,20},{1,25},{... | collective-permute-start | bytes 1228808 | tf_op jit(solution)/shard_map/ppermute | solution.py:69
  36.4 34.3 %collective-permute-start.4 = (bf16[384,1664]{1,0:T(8,128)(2,1)}, bf16[384,1664]{1,0:T(8,128)(2,1)}, u32[]{:S(2)}, u32[]{:S(2)}) collective-permute-start(bf16[384,1664]{1,0:T(8,128)(2,1)} %get-tuple-element.46), channel_id=1, source_target_pairs={{0,4},{4,0},{8,12},{12,8},{16,20},{20,16},{24,28},{28,24},{1,5},{5... | collective-permute-start | bytes 3833864 | tf_op jit(solution)/shard_map/ppermute | solution.py:64
  38.2 14.6 %collective-permute-start.6 = (bf16[400,512]{1,0:T(8,128)(2,1)}, bf16[400,512]{1,0:T(8,128)(2,1)S(1)}, u32[]{:S(2)}, u32[]{:S(2)}) collective-permute-start(bf16[400,512]{1,0:T(8,128)(2,1)} %collective-permute-done.refs_4_), channel_id=1, source_target_pairs={{0,8},{4,12},{8,16},{12,20},{16,24},{20,28},{24,0},{28,4},{1,9},{5... | collective-permute-start | bytes 1228808 | tf_op jit(solution)/shard_map/ppermute | solution.py:69
  38.2 40.9 %collective-permute-start.9 = (bf16[400,512]{1,0:T(8,128)(2,1)}, bf16[400,512]{1,0:T(8,128)(2,1)}, u32[]{:S(2)}, u32[]{:S(2)}) collective-permute-start(bf16[400,512]{1,0:T(8,128)(2,1)} %collective-permute-done.8.refs_4_), channel_id=1, source_target_pairs={{0,8},{4,12},{8,16},{12,20},{16,24},{20,28},{24,0},{28,4},{1,9},{5... | collective-permute-start | bytes 1228808 | tf_op jit(solution)/shard_map/ppermute | solution.py:69
  42.9 16.0 %collective-permute-start.3 = (s32[102]{0:T(128)S(1)}, s32[102]{0:T(128)S(1)}, u32[]{:S(2)}, u32[]{:S(2)}) collective-permute-start(s32[102]{0:T(128)S(1)} %pad_add_fusion), channel_id=1, source_target_pairs={{0,4},{4,0},{8,12},{12,8},{16,20},{20,16},{24,28},{28,24},{1,5},{5... | collective-permute-start | bytes 1232 | tf_op jit(solution)/shard_map/ppermute | solution.py:64
  49.5 21.2 %collective-permute-start.2 = (bf16[400,384]{1,0:T(8,128)(2,1)}, bf16[400,384]{1,0:T(8,128)(2,1)S(1)}, u32[]{:S(2)}, u32[]{:S(2)}) collective-permute-start(bf16[400,384]{1,0:T(8,128)(2,1)} %get-tuple-element.89), channel_id=1, source_target_pairs={{0,4},{4,0},{8,12},{12,8},{16,20},{20,16},{24,28},{28,24},{1,5},{5... | collective-permute-start | bytes 921608 | tf_op jit(solution)/shard_map/ppermute | solution.py:64
  53.5 17.0 %collective-permute-start.11 = (bf16[400,512]{1,0:T(8,128)(2,1)}, bf16[400,512]{1,0:T(8,128)(2,1)}, u32[]{:S(2)}, u32[]{:S(2)}) collective-permute-start(bf16[400,512]{1,0:T(8,128)(2,1)} %get-tuple-element.54.refs_3_), channel_id=1, source_target_pairs={{0,8},{4,12},{8,16},{12,20},{16,24},{20,28},{24,0},{28,4},{1,9},{5... | collective-permute-start | bytes 1228808 | tf_op jit(solution)/shard_map/ppermute | solution.py:69
  58.9 26.4 %collective-permute-start.13 = (bf16[400,512]{1,0:T(8,128)(2,1)}, bf16[400,512]{1,0:T(8,128)(2,1)}, u32[]{:S(2)}, u32[]{:S(2)}) collective-permute-start(bf16[400,512]{1,0:T(8,128)(2,1)} %get-tuple-element.54.refs_3_), channel_id=1, source_target_pairs={{0,24},{4,28},{8,0},{12,4},{16,8},{20,12},{24,16},{28,20},{1,25},{... | collective-permute-start | bytes 1228808 | tf_op jit(solution)/shard_map/ppermute | solution.py:69
  70.5 17.3 %collective-permute-start.12 = (bf16[400,512]{1,0:T(8,128)(2,1)}, bf16[400,512]{1,0:T(8,128)(2,1)S(1)}, u32[]{:S(2)}, u32[]{:S(2)}) collective-permute-start(bf16[400,512]{1,0:T(8,128)(2,1)} %collective-permute-done.11.refs_4_), channel_id=1, source_target_pairs={{0,8},{4,12},{8,16},{12,20},{16,24},{20,28},{24,0},{28,4},{1,9},{5... | collective-permute-start | bytes 1228808 | tf_op jit(solution)/shard_map/ppermute | solution.py:69
  77.3 20.3 %collective-permute-start.7 = (bf16[384,512]{1,0:T(8,128)(2,1)S(1)}, bf16[384,512]{1,0:T(8,128)(2,1)S(1)}, u32[]{:S(2)}, u32[]{:S(2)}) collective-permute-start(bf16[384,512]{1,0:T(8,128)(2,1)S(1)} %get-tuple-element.49), channel_id=1, source_target_pairs={{0,4},{4,0},{8,12},{12,8},{16,20},{20,16},{24,28},{28,24},{1,5},{5... | collective-permute-start | bytes 1179656 | tf_op jit(solution)/shard_map/ppermute | solution.py:64
  83.5 14.1 %collective-permute-start.10 = (bf16[384,512]{1,0:T(8,128)(2,1)S(1)}, bf16[384,512]{1,0:T(8,128)(2,1)S(1)}, u32[]{:S(2)}, u32[]{:S(2)}) collective-permute-start(bf16[384,512]{1,0:T(8,128)(2,1)S(1)} %get-tuple-element.51), channel_id=1, source_target_pairs={{0,4},{4,0},{8,12},{12,8},{16,20},{20,16},{24,28},{28,24},{1,5},{5... | collective-permute-start | bytes 1179656 | tf_op jit(solution)/shard_map/ppermute | solution.py:64
  83.8 12.4 %collective-permute-start.15 = (bf16[400,512]{1,0:T(8,128)(2,1)}, bf16[400,512]{1,0:T(8,128)(2,1)}, u32[]{:S(2)}, u32[]{:S(2)}) collective-permute-start(bf16[400,512]{1,0:T(8,128)(2,1)} %bitcast.17.refs_2_), channel_id=1, source_target_pairs={{0,8},{4,12},{8,16},{12,20},{16,24},{20,28},{24,0},{28,4},{1,9},{5... | collective-permute-start | bytes 1228808 | tf_op jit(solution)/shard_map/ppermute | solution.py:69
  93.0 14.2 %collective-permute-start.14 = (bf16[384,512]{1,0:T(8,128)(2,1)}, bf16[384,512]{1,0:T(8,128)(2,1)}, u32[]{:S(2)}, u32[]{:S(2)}) collective-permute-start(bf16[384,512]{1,0:T(8,128)(2,1)} %get-tuple-element.55), channel_id=1, source_target_pairs={{0,4},{4,0},{8,12},{12,8},{16,20},{20,16},{24,28},{28,24},{1,5},{5... | collective-permute-start | bytes 1179656 | tf_op jit(solution)/shard_map/ppermute | solution.py:64
  94.9 16.2 %collective-permute-start.17 = (bf16[400,512]{1,0:T(8,128)(2,1)}, bf16[400,512]{1,0:T(8,128)(2,1)}, u32[]{:S(2)}, u32[]{:S(2)}) collective-permute-start(bf16[400,512]{1,0:T(8,128)(2,1)} %bitcast.17.refs_2_), channel_id=1, source_target_pairs={{0,24},{4,28},{8,0},{12,4},{16,8},{20,12},{24,16},{28,20},{1,25},{... | collective-permute-start | bytes 1228808 | tf_op jit(solution)/shard_map/ppermute | solution.py:69
  96.3 18.0 %collective-permute-start.16 = (bf16[400,512]{1,0:T(8,128)(2,1)}, bf16[400,512]{1,0:T(8,128)(2,1)}, u32[]{:S(2)}, u32[]{:S(2)}) collective-permute-start(bf16[400,512]{1,0:T(8,128)(2,1)} %collective-permute-done.15.refs_3_), channel_id=1, source_target_pairs={{0,8},{4,12},{8,16},{12,20},{16,24},{20,28},{24,0},{28,4},{1,9},{5... | collective-permute-start | bytes 1228808 | tf_op jit(solution)/shard_map/ppermute | solution.py:69
  110.7 10.5 %collective-permute-start.20 = (bf16[384,512]{1,0:T(8,128)(2,1)S(1)}, bf16[384,512]{1,0:T(8,128)(2,1)S(1)}, u32[]{:S(2)}, u32[]{:S(2)}) collective-permute-start(bf16[384,512]{1,0:T(8,128)(2,1)S(1)} %attend.1.refs_1_), channel_id=1, source_target_pairs={{0,4},{4,0},{8,12},{12,8},{16,20},{20,16},{24,28},{28,24},{1,5},{5... | collective-permute-start | bytes 1179656 | tf_op jit(solution)/shard_map/ppermute | solution.py:64
  117.2 7.1 %collective-permute-start.18 = (bf16[2,400,384]{2,1,0:T(8,128)(2,1)S(1)}, bf16[2,400,384]{2,1,0:T(8,128)(2,1)S(1)}, u32[]{:S(2)}, u32[]{:S(2)}) collective-permute-start(bf16[2,400,384]{2,1,0:T(8,128)(2,1)S(1)} %get-tuple-element.62), channel_id=1, source_target_pairs={{0,1},{1,0},{2,3},{3,2},{4,5},{5,4},{6,7},{7,6},{8,9},{9,8},{10,11... | collective-permute-start | bytes 1843208 | tf_op jit(solution)/shard_map/ppermute | solution.py:64
  124.2 2.1 %collective-permute-start.21 = (bf16[2,400,384]{2,1,0:T(8,128)(2,1)S(1)}, bf16[2,400,384]{2,1,0:T(8,128)(2,1)S(1)}, u32[]{:S(2)}, u32[]{:S(2)}) collective-permute-start(bf16[2,400,384]{2,1,0:T(8,128)(2,1)S(1)} %get-tuple-element.67), channel_id=1, source_target_pairs={{0,1},{1,0},{2,3},{3,2},{4,5},{5,4},{6,7},{7,6},{8,9},{9,8},{10,11... | collective-permute-start | bytes 1843208 | tf_op jit(solution)/shard_map/ppermute | solution.py:64
  124.4 10.1 %collective-permute-start.19 = (bf16[400,384]{1,0:T(8,128)(2,1)S(1)}, bf16[400,384]{1,0:T(8,128)(2,1)S(1)}, u32[]{:S(2)}, u32[]{:S(2)}) collective-permute-start(bf16[400,384]{1,0:T(8,128)(2,1)S(1)} %far_sum.2), channel_id=1, source_target_pairs={{0,2},{1,3},{2,0},{3,1},{4,6},{5,7},{6,4},{7,5},{8,10},{9,11},{10,... | collective-permute-start | bytes 921608 | tf_op jit(solution)/shard_map/ppermute | solution.py:64
  126.4 14.3 %collective-permute-start.22 = (bf16[400,384]{1,0:T(8,128)(2,1)S(1)}, bf16[400,384]{1,0:T(8,128)(2,1)S(1)}, u32[]{:S(2)}, u32[]{:S(2)}) collective-permute-start(bf16[400,384]{1,0:T(8,128)(2,1)S(1)} %far_sum.3), channel_id=1, source_target_pairs={{0,2},{1,3},{2,0},{3,1},{4,6},{5,7},{6,4},{7,5},{8,10},{9,11},{10,... | collective-permute-start | bytes 921608 | tf_op jit(solution)/shard_map/ppermute | solution.py:64
  142.5 37.6 %all-to-all-start = ((bf16[8,2,24,1600]{3,2,1,0:T(8,128)(2,1)}), bf16[8,2,24,1600]{3,2,1,0:T(8,128)(2,1)S(1)}, u32[]{:S(2)}, u32[]{:S(2)}) async-start(bf16[8,2,24,1600]{3,2,1,0:T(8,128)(2,1)} %get-tuple-element.70), calls=%async_computation | async-start | bytes 2555904 | tf_op jit(solution)/shard_map/all_to_all | solution.py:520
  147.3 33.0 %copy-start.8 = (f32[4,800]{1,0:T(4,128)S(1)}, f32[4,800]{1,0:T(4,128)}, u32[]{:S(2)}) copy-start(f32[4,800]{1,0:T(4,128)} %refs_1_.2) | copy-start | bytes 38404
  147.3 33.0 %copy-start.9 = (f32[4,800]{1,0:T(4,128)S(1)}, f32[4,800]{1,0:T(4,128)}, u32[]{:S(2)}) copy-start(f32[4,800]{1,0:T(4,128)} %refs_2_.1) | copy-start | bytes 38404
  154.2 3.7 %collective-permute-start.23 = (f32[2,192]{1,0:T(2,128)S(1)}, f32[2,192]{1,0:T(2,128)S(1)}, u32[]{:S(2)}, u32[]{:S(2)}) collective-permute-start(f32[2,192]{1,0:T(2,128)S(1)} %multiply_reduce_fusion), channel_id=1, source_target_pairs={{0,4},{4,0},{8,12},{12,8},{16,20},{20,16},{24,28},{28,24},{1,5},{5... | collective-permute-start | bytes 4616 | tf_op jit(solution)/shard_map/ppermute | solution.py:64
  159.3 3.9 %collective-permute-start.24 = (f32[3,1,8,24]{3,2,1,0:T(8,128)S(1)}, f32[3,1,8,24]{3,2,1,0:T(8,128)S(1)}, u32[]{:S(2)}, u32[]{:S(2)}) collective-permute-start(f32[3,1,8,24]{3,2,1,0:T(8,128)S(1)} %constant_dynamic-update-slice_fusion), channel_id=1, source_target_pairs={{0,4},{4,0},{8,12},{12,8},{16,20},{20,16},{24,28},{28,24},{1,5},{5... | collective-permute-start | bytes 6920 | tf_op jit(solution)/shard_map/ppermute | solution.py:64
  163.2 5.5 %collective-permute-start.25 = (f32[3,2,8,24]{3,2,1,0:T(8,128)S(1)}, f32[3,2,8,24]{3,2,1,0:T(8,128)S(1)}, u32[]{:S(2)}, u32[]{:S(2)}) collective-permute-start(f32[3,2,8,24]{3,2,1,0:T(8,128)S(1)} %pad_maximum_fusion.1), channel_id=1, source_target_pairs={{0,8},{4,12},{8,0},{12,4},{16,24},{20,28},{24,16},{28,20},{1,9},{5... | collective-permute-start | bytes 13832 | tf_op jit(solution)/shard_map/ppermute | solution.py:64
  168.7 11.3 %collective-permute-start.26 = (f32[3,4,8,24]{3,2,1,0:T(8,128)S(1)}, f32[3,4,8,24]{3,2,1,0:T(8,128)S(1)}, u32[]{:S(2)}, u32[]{:S(2)}) collective-permute-start(f32[3,4,8,24]{3,2,1,0:T(8,128)S(1)} %pad_maximum_fusion), channel_id=1, source_target_pairs={{0,16},{4,20},{8,24},{12,28},{16,0},{20,4},{24,8},{28,12},{1,17},{... | collective-permute-start | bytes 27656 | tf_op jit(solution)/shard_map/ppermute | solution.py:64
  (19 other events, 130.3 us)

commit v6 on v5

--- a/solution.py
+++ b/solution.py
@@ -305,12 +305,13 @@
     sum_tokens(hidden, sums_ref, 2)
 
 
-def finish_kernel(stats_ref, gain_ref, bias_ref, rows_ref, out_ref):
+def finish_kernel(plane_ref, stats_ref, gain_ref, bias_ref, rows_ref, out_ref):
     count, _, rows, _ = rows_ref.shape
     depth = out_ref.shape[2] // 2
     for i in range(count):
         to = pl.ds(i * rows, rows)
-        scale, shift, live = (stats_ref[j, to][:, 0:1] for j in range(3))
+        place = pl.ds(((plane_ref[0] ^ (i // 2)) * 2 + i % 2) * rows, rows)
+        scale, shift, live = (stats_ref[j, place][:, 0:1] for j in range(3))
         for patch in range(4):
             part = slice(patch * depth, (patch + 1) * depth)
             parts = [rows_ref[i, 0, :, part].astype(F32), rows_ref[i ^ 1, 1, :, part].astype(F32)]
@@ -320,12 +321,12 @@
             out_ref[to, patch, :] = values.astype(BF16)
 
 
-def finish(stats, proj_gain, proj_bias, arrived):
+def finish(plane, stats, proj_gain, proj_bias, arrived):
     rows = stats.shape[1]
     stats = jnp.broadcast_to(stats[:, :, None], (3, rows, 128))
     out = array((rows,) + proj_gain.shape, BF16)
-    operands = (stats, proj_gain, proj_bias, arrived)
-    return call(finish_kernel, "finish", (out,), operands, 6 * out.size)[0]
+    operands = (plane.reshape(1), stats, proj_gain, proj_bias, arrived)
+    return call(finish_kernel, "finish", (out,), operands, 6 * out.size, scalars=1)[0]
 
 
 def after(value, *first):
@@ -435,8 +436,8 @@
     k_down = ring(after(w_k, q_up), -1)
     q_far = ring(after(q_up, q_down))
     k_far = ring(k_up)
-    v_up = ring(after(w_v, k_down))
-    v_down = ring(after(w_v, q_far), -1)
+    v_up = ring(after(w_v, q_far))
+    v_down = ring(after(w_v, k_far), -1)
     v_far = ring(v_up)
     q_blocks, k_blocks = [w_q, q_up, q_far, q_down], [w_k, k_up, k_far, k_down]
     v_blocks = [w_v, v_up, v_far, v_down]
@@ -529,17 +530,17 @@
     inverse = lax.rsqrt(row_sums[1] - mean_value * mean_value + 1e-05) * row_live
     stats = jnp.stack([inverse, -mean_value * inverse, row_live])
     stats = stats.reshape(3, 1, devices_req, capacity)
-    bit = 1
-    while bit < devices_req:
-        got = swap(stats, "req", bit)
-        lower = (me & bit) == 0
-        stats = jnp.concatenate(
-            [jnp.where(lower, stats, got), jnp.where(lower, got, stats)], axis=1
-        )
-        bit *= 2
+    got = swap(stats, "req", 1)
+    lower = side == 0
+    stats = jnp.concatenate(
+        [jnp.where(lower, stats, got), jnp.where(lower, got, stats)], axis=1
+    )
+    stats = jnp.concatenate(
+        [stats] + [swap(stats, "req", 2 * bits) for bits in range(1, planes)], axis=1
+    )
     stats = lax.dynamic_index_in_dim(stats, me, 2, keepdims=False)
     stats = stats.reshape(3, devices_req * capacity)
-    return finish(stats, proj_gain, proj_bias, arrived)
+    return finish(plane, stats, proj_gain, proj_bias, arrived)
 
 
 def solution(mesh):

time: 184 us -> 184 us (level)
    ppermute x12, waiting for transfers between devices: 27.4 us -> 31.4 us  [ring(): lax.ppermute(value, 'req', [(i, (i + 2 * step) % count) for i in range(co...]
    ppermute x15 -> x16, waiting for transfers between devices: 34.2 us -> 31.5 us  [swap(): return lax.ppermute(value, axis, [(i, i ^ bit) for i in range(count)])]
    ppermute x15 -> x16, starting transfers between devices: 21.4 us -> 19.4 us  [swap(): return lax.ppermute(value, axis, [(i, i ^ bit) for i in range(count)])]
    unnamed x49 -> x51, local copies, waits for them, and re-layouts: 9.03 us -> 8.03 us
  transfers between devices with their start and end apart: 28 -> 29, of which waited for: 15 -> 15; matrix products, arithmetic and copies ran while one was open for 7% -> 7% of each run, Pallas kernels for 16% -> 16%
where the time goes in v6:
time: 184 us; the launch traced here: 183 us
  waiting for transfers between devices  62.9 us (34%)
  starting transfers between devices  50.3 us (27%)
  Pallas kernels  35.6 us (19%)
  local copies, waits for them, and re-layouts  15.9 us (9%)
  blocking collectives  12.8 us (7%)
  other arithmetic  4.8 us (3%)
    pallas_call x14, Pallas kernels, call(): pl.pallas_call(untied, grid=(1,), out_shape=tuple(out), in_specs=[pl.Bloc...  35.6 us
    ppermute x16, waiting for transfers between devices, swap(): return lax.ppermute(value, axis, [(i, i ^ bit) for i in range(count)])  31.5 us
    ppermute x12, waiting for transfers between devices, ring(): lax.ppermute(value, 'req', [(i, (i + 2 * step) % count) for i in range(co...  31.4 us
    ppermute x12, starting transfers between devices, ring(): lax.ppermute(value, 'req', [(i, (i + 2 * step) % count) for i in range(co...  26.3 us
    ppermute x16, starting transfers between devices, swap(): return lax.ppermute(value, axis, [(i, i ^ bit) for i in range(count)])  19.4 us
    unnamed x51, local copies, waits for them, and re-layouts  8.03 us
    psum x1, blocking collectives, body(): token_sums = lax.psum(token_sums, 'tp').reshape(2, 2, token_count)  6.55 us
    psum x1, blocking collectives, body(): lax.psum(sums, 'tp')  6.25 us
  transfers between devices with their start and end apart: 29, of which 15 were waited for; matrix products, arithmetic and copies ran while one was open for 7% of the time, Pallas kernels for 16%

profile of v6, /device:TPU:0, one launch (start us, length us, event | category | flops | bytes accessed | tf_op | source)
XLA Modules:
  0.0 182.8 jit_solution(16081830809473512778)
XLA Ops:
  2.3 3.0 %collective-permute-start = (bf16[400,512]{1,0:T(8,128)(2,1)S(1)}, bf16[400,512]{1,0:T(8,128)(2,1)}, u32[]{:S(2)}, u32[]{:S(2)}) collective-permute-start(bf16[400,512]{1,0:T(8,128)(2,1)S(1)} %get-tuple-element.39.refs_3_), channel_id=1, source_target_pairs={{0,8},{4,12},{8,16},{12,20},{16,24},{20,28},{24,0},{28,4},{1,9},{5... | collective-permute-start | bytes 1228808 | tf_op jit(solution)/shard_map/ppermute | solution.py:69
  5.3 2.0 %collective-permute-start.5 = (bf16[400,512]{1,0:T(8,128)(2,1)S(1)}, bf16[400,512]{1,0:T(8,128)(2,1)}, u32[]{:S(2)}, u32[]{:S(2)}) collective-permute-start(bf16[400,512]{1,0:T(8,128)(2,1)S(1)} %get-tuple-element.39.refs_3_), channel_id=1, source_target_pairs={{0,24},{4,28},{8,0},{12,4},{16,8},{20,12},{24,16},{28,20},{1,25},{... | collective-permute-start | bytes 1228808 | tf_op jit(solution)/shard_map/ppermute | solution.py:69
  7.3 10.4 %collective-permute-done.refs_4_ = bf16[400,512]{1,0:T(8,128)(2,1)} collective-permute-done((bf16[400,512]{1,0:T(8,128)(2,1)S(1)}, bf16[400,512]{1,0:T(8,128)(2,1)}, u32[]{:S(2)}, u32[]{:S(2)}) %collective-permute-start) | collective-permute-done | bytes 409632 | tf_op jit(solution)/shard_map/ppermute | solution.py:69
  17.8 10.8 %collective-permute-start.1 = (bf16[400,512]{1,0:T(8,128)(2,1)S(1)}, bf16[400,512]{1,0:T(8,128)(2,1)}, u32[]{:S(2)}, u32[]{:S(2)}) collective-permute-start(bf16[400,512]{1,0:T(8,128)(2,1)S(1)} %get-tuple-element.40.refs_3_), channel_id=1, source_target_pairs={{0,24},{4,28},{8,0},{12,4},{16,8},{20,12},{24,16},{28,20},{1,25},{... | collective-permute-start | bytes 1228808 | tf_op jit(solution)/shard_map/ppermute | solution.py:69
  31.0 4.3 %norm_tokens.1 = (bf16[384,1600]{1,0:T(8,128)(2,1)S(1)}, bf16[384,1664]{1,0:T(8,128)(2,1)}) custom-call(s32[1]{0:T(128)} %bitcast.4.refs_0_, bf16[384,3200]{1,0:T(8,128)(2,1)S(1)} %copy-done, f32[1,3200]{1,0:T(1,128)S(1)} %broadcast_in_dim.39.refs_2_), custom_call_target="tpu_custom_call" | custom-call | bytes 4977152 | tf_op jit(solution)/shard_map/norm_tokens/pallas_call | solution.py:85
  38.2 4.4 %collective-permute-start.9 = (bf16[400,512]{1,0:T(8,128)(2,1)}, bf16[400,512]{1,0:T(8,128)(2,1)S(1)}, u32[]{:S(2)}, u32[]{:S(2)}) collective-permute-start(bf16[400,512]{1,0:T(8,128)(2,1)} %collective-permute-done.8.refs_4_), channel_id=1, source_target_pairs={{0,8},{4,12},{8,16},{12,20},{16,24},{20,28},{24,0},{28,4},{1,9},{5... | collective-permute-start | bytes 1228808 | tf_op jit(solution)/shard_map/ppermute | solution.py:69
  44.7 2.7 %copy.25 = bf16[384,3200]{0,1:T(8,128)(2,1)} copy(bf16[384,3200]{1,0:T(8,128)(2,1)S(1)} %copy-done.1) | data formatting | bytes 4915200 | tf_op jit(solution)/shard_map/optimization_barrier | solution.py:333
  50.5 2.4 %collective-permute-done.6.refs_5_ = bf16[400,512]{1,0:T(8,128)(2,1)} collective-permute-done((bf16[400,512]{1,0:T(8,128)(2,1)}, bf16[400,512]{1,0:T(8,128)(2,1)}, u32[]{:S(2)}, u32[]{:S(2)}) %collective-permute-start.6) | collective-permute-done | bytes 409632 | tf_op jit(solution)/shard_map/ppermute | solution.py:69
  53.5 8.1 %collective-permute-done.9.refs_5_ = bf16[400,512]{1,0:T(8,128)(2,1)S(1)} collective-permute-done((bf16[400,512]{1,0:T(8,128)(2,1)}, bf16[400,512]{1,0:T(8,128)(2,1)S(1)}, u32[]{:S(2)}, u32[]{:S(2)}) %collective-permute-start.9) | collective-permute-done | bytes 409632 | tf_op jit(solution)/shard_map/ppermute | solution.py:69
  62.3 2.0 %collective-permute-start.13 = (bf16[400,512]{1,0:T(8,128)(2,1)}, bf16[400,512]{1,0:T(8,128)(2,1)}, u32[]{:S(2)}, u32[]{:S(2)}) collective-permute-start(bf16[400,512]{1,0:T(8,128)(2,1)} %get-tuple-element.54.refs_3_), channel_id=1, source_target_pairs={{0,24},{4,28},{8,0},{12,4},{16,8},{20,12},{24,16},{28,20},{1,25},{... | collective-permute-start | bytes 1228808 | tf_op jit(solution)/shard_map/ppermute | solution.py:69
  66.9 3.7 %collective-permute-done.11.refs_4_ = bf16[400,512]{1,0:T(8,128)(2,1)} collective-permute-done((bf16[400,512]{1,0:T(8,128)(2,1)}, bf16[400,512]{1,0:T(8,128)(2,1)}, u32[]{:S(2)}, u32[]{:S(2)}) %collective-permute-start.11) | collective-permute-done | bytes 409632 | tf_op jit(solution)/shard_map/ppermute | solution.py:69
  71.9 4.5 %project.3 = (f32[384,512]{1,0:T(8,128)S(1)}, bf16[384,512]{1,0:T(8,128)(2,1)S(1)}) custom-call(s32[1]{0:T(128)} %bitcast.refs_0_, bf16[384,1600]{1,0:T(8,128)(2,1)S(1)} %copy-done.11, bf16[384,1664]{1,0:T(8,128)(2,1)} %collective-permute-done.4.refs_2_, bf16[400,512]{1,0:T(8,128)(2,1)S(1)} %copy-done.15, bf16[400,512]{1,0:T(8,128)(2,1)} %collective-permute-done.refs_4_, ...), custom_call_target="tpu_custom_call" | custom-call | flops 1258291200 | bytes 5324800 | tf_op jit(solution)/shard_map/project/pallas_call | solution.py:85
  78.2 4.4 %project.4 = (f32[384,512]{1,0:T(8,128)S(1)}, bf16[384,512]{1,0:T(8,128)(2,1)S(1)}) custom-call(s32[1]{0:T(128)} %bitcast.refs_0_, bf16[384,1600]{1,0:T(8,128)(2,1)S(1)} %copy-done.11, bf16[384,1664]{1,0:T(8,128)(2,1)} %collective-permute-done.4.refs_2_, bf16[400,512]{1,0:T(8,128)(2,1)S(1)} %copy-done.13, bf16[400,512]{1,0:T(8,128)(2,1)} %collective-permute-done.8.refs_4_, ...), custom_call_target="tpu_custom_call" | custom-call | flops 1258291200 | bytes 5324800 | tf_op jit(solution)/shard_map/project/pallas_call | solution.py:85
  84.4 3.6 %collective-permute-done.12.refs_5_ = bf16[400,512]{1,0:T(8,128)(2,1)S(1)} collective-permute-done((bf16[400,512]{1,0:T(8,128)(2,1)}, bf16[400,512]{1,0:T(8,128)(2,1)S(1)}, u32[]{:S(2)}, u32[]{:S(2)}) %collective-permute-start.12) | collective-permute-done | bytes 409632 | tf_op jit(solution)/shard_map/ppermute | solution.py:69
  88.0 4.3 %project.5 = (f32[384,512]{1,0:T(8,128)S(1)}, bf16[384,512]{1,0:T(8,128)(2,1)}) custom-call(s32[1]{0:T(128)} %bitcast.refs_0_, bf16[384,1600]{1,0:T(8,128)(2,1)S(1)} %copy-done.11, bf16[384,1664]{1,0:T(8,128)(2,1)} %collective-permute-done.4.refs_2_, bf16[400,512]{1,0:T(8,128)(2,1)} %get-tuple-element.54.refs_3_, ...), custom_call_target="tpu_custom_call" | custom-call | flops 1258291200 | bytes 5324800 | tf_op jit(solution)/shard_map/project/pallas_call | solution.py:85
  97.8 3.3 %scores.1 = (f32[4,384,384]{2,1,0:T(8,128)S(1)}, f32[2,384]{1,0:T(2,128)S(1)}) custom-call(f32[384,512]{1,0:T(8,128)S(1)} %get-tuple-element.48.refs_0_, bf16[384,512]{1,0:T(8,128)(2,1)S(1)} %collective-permute-done.7.refs_1_, f32[384,512]{1,0:T(8,128)S(1)} %get-tuple-element.50.refs_2_, bf16[384,512]{1,0:T(8,128)(2,1)S(1)} %collective-permute-done.10.refs_3_, ...), custom_call_target="tpu_custom_call" | custom-call | flops 905969664 | bytes 4727808 | tf_op jit(solution)/shard_map/scores/pallas_call | solution.py:85
  101.1 6.2 %psum.14.refs_1_ = f32[2,384]{1,0:T(2,128)S(1)} all-reduce(f32[2,384]{1,0:T(2,128)S(1)} %get-tuple-element.57), channel_id=1, replica_groups=mesh['req'=8,'tp'=4] {'tp'}, use_global_device_ids=true, to_apply=%region_13.14 | all-reduce | flops 768 | bytes 6144 | tf_op jit(solution)/shard_map/psum | solution.py:495
  108.5 2.4 %attend.1.refs_1_ = bf16[384,512]{1,0:T(8,128)(2,1)S(1)} custom-call(f32[4,384,384]{2,1,0:T(8,128)S(1)} %get-tuple-element.56.refs_0_, f32[2,384]{1,0:T(2,128)S(1)} %psum.14.refs_1_, f32[1,384]{1,0:T(1,128)S(1)} %convert_element_type.89.refs_2_, f32[384,512]{1,0:T(8,128)S(1)} %copy-done.5, bf16[384,512]{1,0:T(8,128)(2,1)} %collective-permute-done.14.refs_4_), custom_call_target="tpu_custom_call" | custom-call | flops 150994944 | bytes 3936768 | tf_op jit(solution)/shard_map/attend/pallas_call | solution.py:85
  111.3 3.0 %collective-permute-done.16.refs_4_ = bf16[400,512]{1,0:T(8,128)(2,1)} collective-permute-done((bf16[400,512]{1,0:T(8,128)(2,1)}, bf16[400,512]{1,0:T(8,128)(2,1)}, u32[]{:S(2)}, u32[]{:S(2)}) %collective-permute-start.16) | collective-permute-done | bytes 409632 | tf_op jit(solution)/shard_map/ppermute | solution.py:69
  114.2 3.0 %project_out.2 = (bf16[2,400,384]{2,1,0:T(8,128)(2,1)S(1)}, f32[400,384]{1,0:T(8,128)S(1)}, f32[400,384]{1,0:T(8,128)S(1)}) custom-call(s32[3]{0:T(128)S(1)} %pad_add_fusion.1.refs_0_, bf16[384,512]{1,0:T(8,128)(2,1)S(1)} %attend.1.refs_1_, bf16[400,512]{1,0:T(8,128)(2,1)} %bitcast.17.refs_2_, bf16[400,512]{1,0:T(8,128)(2,1)} %collective-permute-done.15.refs_3_, ...), custom_call_target="tpu_custom_call" | custom-call | flops 629145600 | bytes 3874816 | tf_op jit(solution)/shard_map/project_out/pallas_call | solution.py:85
  117.3 4.1 %collective-permute-done.20.refs_1_ = bf16[384,512]{1,0:T(8,128)(2,1)S(1)} collective-permute-done((bf16[384,512]{1,0:T(8,128)(2,1)S(1)}, bf16[384,512]{1,0:T(8,128)(2,1)S(1)}, u32[]{:S(2)}, u32[]{:S(2)}) %collective-permute-start.20) | collective-permute-done | bytes 393248 | tf_op jit(solution)/shard_map/ppermute | solution.py:64
  121.4 3.0 %project_out.3 = (bf16[2,400,384]{2,1,0:T(8,128)(2,1)S(1)}, f32[400,384]{1,0:T(8,128)S(1)}, f32[400,384]{1,0:T(8,128)S(1)}) custom-call(s32[3]{0:T(128)S(1)} %pad_add_fusion.1.refs_0_, bf16[384,512]{1,0:T(8,128)(2,1)S(1)} %collective-permute-done.20.refs_1_, bf16[400,512]{1,0:T(8,128)(2,1)} %bitcast.17.refs_2_, ...), custom_call_target="tpu_custom_call" | custom-call | flops 629145600 | bytes 3874816 | tf_op jit(solution)/shard_map/project_out/pallas_call | solution.py:85
  128.6 6.1 %collective-permute-done.19.refs_2_ = bf16[400,384]{1,0:T(8,128)(2,1)S(1)} collective-permute-done((bf16[400,384]{1,0:T(8,128)(2,1)S(1)}, bf16[400,384]{1,0:T(8,128)(2,1)S(1)}, u32[]{:S(2)}, u32[]{:S(2)}) %collective-permute-start.19) | collective-permute-done | bytes 307232 | tf_op jit(solution)/shard_map/ppermute | solution.py:64
  135.5 5.4 %collective-permute-done.22.refs_4_ = bf16[400,384]{1,0:T(8,128)(2,1)S(1)} collective-permute-done((bf16[400,384]{1,0:T(8,128)(2,1)S(1)}, bf16[400,384]{1,0:T(8,128)(2,1)S(1)}, u32[]{:S(2)}, u32[]{:S(2)}) %collective-permute-start.22) | collective-permute-done | bytes 307232 | tf_op jit(solution)/shard_map/ppermute | solution.py:64
  140.9 1.8 second_pack.1
  142.7 4.6 %all-to-all-start = ((bf16[8,2,24,1600]{3,2,1,0:T(8,128)(2,1)}), bf16[8,2,24,1600]{3,2,1,0:T(8,128)(2,1)S(1)}, u32[]{:S(2)}, u32[]{:S(2)}) async-start(bf16[8,2,24,1600]{3,2,1,0:T(8,128)(2,1)} %get-tuple-element.70), calls=%async_computation | async-start | bytes 2555904 | tf_op jit(solution)/shard_map/all_to_all | solution.py:521
  147.4 6.6 %psum.15 = f32[4,384]{1,0:T(4,128)S(1)} all-reduce(f32[4,384]{1,0:T(4,128)S(1)} %get-tuple-element.69), channel_id=1, replica_groups=mesh['req'=8,'tp'=4] {'tp'}, use_global_device_ids=true, to_apply=%region_15.16 | all-reduce | flops 1536 | bytes 12288 | tf_op jit(solution)/shard_map/psum | solution.py:523
  161.1 2.1 %collective-permute-done.24 = f32[3,1,8,24]{3,2,1,0:T(8,128)S(1)} collective-permute-done((f32[3,1,8,24]{3,2,1,0:T(8,128)S(1)}, f32[3,1,8,24]{3,2,1,0:T(8,128)S(1)}, u32[]{:S(2)}, u32[]{:S(2)}) %collective-permute-start.24) | collective-permute-done | bytes 2336 | tf_op jit(solution)/shard_map/ppermute | solution.py:64
  163.2 2.3 %collective-permute-start.25 = (f32[3,2,8,24]{3,2,1,0:T(8,128)S(1)}, f32[3,2,8,24]{3,2,1,0:T(8,128)S(1)}, u32[]{:S(2)}, u32[]{:S(2)}) collective-permute-start(f32[3,2,8,24]{3,2,1,0:T(8,128)S(1)} %pad_maximum_fusion), channel_id=1, source_target_pairs={{0,8},{4,12},{8,0},{12,4},{16,24},{20,28},{24,16},{28,20},{1,9},{5... | collective-permute-start | bytes 13832 | tf_op jit(solution)/shard_map/ppermute | solution.py:64
  165.6 2.1 %collective-permute-start.26 = (f32[3,2,8,24]{3,2,1,0:T(8,128)S(1)}, f32[3,2,8,24]{3,2,1,0:T(8,128)S(1)}, u32[]{:S(2)}, u32[]{:S(2)}) collective-permute-start(f32[3,2,8,24]{3,2,1,0:T(8,128)S(1)} %pad_maximum_fusion), channel_id=1, source_target_pairs={{0,16},{4,20},{8,24},{12,28},{16,0},{20,4},{24,8},{28,12},{1,17},{... | collective-permute-start | bytes 13832 | tf_op jit(solution)/shard_map/ppermute | solution.py:64
  169.2 10.5 %collective-permute-done.26 = f32[3,2,8,24]{3,2,1,0:T(8,128)S(1)} collective-permute-done((f32[3,2,8,24]{3,2,1,0:T(8,128)S(1)}, f32[3,2,8,24]{3,2,1,0:T(8,128)S(1)}, u32[]{:S(2)}, u32[]{:S(2)}) %collective-permute-start.26) | collective-permute-done | bytes 4640 | tf_op jit(solution)/shard_map/ppermute | solution.py:64
  180.0 2.8 %finish.1 = bf16[192,4,800]{2,1,0:T(4,128)(2,1)} custom-call(s32[1]{0:T(128)} %bitcast.refs_0_, f32[3,192,128]{2,1,0:T(8,128)S(1)} %broadcast_in_dim.44.refs_1_, f32[4,800]{1,0:T(4,128)S(1)} %copy-done.8, f32[4,800]{1,0:T(4,128)S(1)} %copy-done.9, bf16[8,2,24,1600]{3,2,1,0:T(8,128)(2,1)S(1)} %all-to-all-done.refs_4_), custom_call_target="tpu_custom_call" | custom-call | flops 3686400 | bytes 2778112 | tf_op jit(solution)/shard_map/finish/pallas_call | solution.py:85
  (163 shorter events, 42.5 us)
Async XLA Ops:
  2.3 35.6 %copy-start.12 = (bf16[400,512]{1,0:T(8,128)(2,1)}, bf16[400,512]{1,0:T(8,128)(2,1)S(1)}, u32[]{:S(2)}) copy-start(bf16[400,512]{1,0:T(8,128)(2,1)S(1)} %get-tuple-element.40.refs_3_) | copy-start | bytes 1228804
  2.3 35.6 %copy-start.14 = (bf16[400,512]{1,0:T(8,128)(2,1)}, bf16[400,512]{1,0:T(8,128)(2,1)S(1)}, u32[]{:S(2)}) copy-start(bf16[400,512]{1,0:T(8,128)(2,1)S(1)} %get-tuple-element.39.refs_3_) | copy-start | bytes 1228804
  2.3 15.5 %collective-permute-start = (bf16[400,512]{1,0:T(8,128)(2,1)S(1)}, bf16[400,512]{1,0:T(8,128)(2,1)}, u32[]{:S(2)}, u32[]{:S(2)}) collective-permute-start(bf16[400,512]{1,0:T(8,128)(2,1)S(1)} %get-tuple-element.39.refs_3_), channel_id=1, source_target_pairs={{0,8},{4,12},{8,16},{12,20},{16,24},{20,28},{24,0},{28,4},{1,9},{5... | collective-permute-start | bytes 1228808 | tf_op jit(solution)/shard_map/ppermute | solution.py:69
  5.3 32.9 %collective-permute-start.5 = (bf16[400,512]{1,0:T(8,128)(2,1)S(1)}, bf16[400,512]{1,0:T(8,128)(2,1)}, u32[]{:S(2)}, u32[]{:S(2)}) collective-permute-start(bf16[400,512]{1,0:T(8,128)(2,1)S(1)} %get-tuple-element.39.refs_3_), channel_id=1, source_target_pairs={{0,24},{4,28},{8,0},{12,4},{16,8},{20,12},{24,16},{28,20},{1,25},{... | collective-permute-start | bytes 1228808 | tf_op jit(solution)/shard_map/ppermute | solution.py:69
  7.3 30.9 %collective-permute-start.8 = (bf16[400,512]{1,0:T(8,128)(2,1)S(1)}, bf16[400,512]{1,0:T(8,128)(2,1)}, u32[]{:S(2)}, u32[]{:S(2)}) collective-permute-start(bf16[400,512]{1,0:T(8,128)(2,1)S(1)} %get-tuple-element.40.refs_3_), channel_id=1, source_target_pairs={{0,8},{4,12},{8,16},{12,20},{16,24},{20,28},{24,0},{28,4},{1,9},{5... | collective-permute-start | bytes 1228808 | tf_op jit(solution)/shard_map/ppermute | solution.py:69
  17.8 25.1 %collective-permute-start.1 = (bf16[400,512]{1,0:T(8,128)(2,1)S(1)}, bf16[400,512]{1,0:T(8,128)(2,1)}, u32[]{:S(2)}, u32[]{:S(2)}) collective-permute-start(bf16[400,512]{1,0:T(8,128)(2,1)S(1)} %get-tuple-element.40.refs_3_), channel_id=1, source_target_pairs={{0,24},{4,28},{8,0},{12,4},{16,8},{20,12},{24,16},{28,20},{1,25},{... | collective-permute-start | bytes 1228808 | tf_op jit(solution)/shard_map/ppermute | solution.py:69
  36.4 34.4 %collective-permute-start.4 = (bf16[384,1664]{1,0:T(8,128)(2,1)}, bf16[384,1664]{1,0:T(8,128)(2,1)}, u32[]{:S(2)}, u32[]{:S(2)}) collective-permute-start(bf16[384,1664]{1,0:T(8,128)(2,1)} %get-tuple-element.46), channel_id=1, source_target_pairs={{0,4},{4,0},{8,12},{12,8},{16,20},{20,16},{24,28},{28,24},{1,5},{5... | collective-permute-start | bytes 3833864 | tf_op jit(solution)/shard_map/ppermute | solution.py:64
  38.2 14.7 %collective-permute-start.6 = (bf16[400,512]{1,0:T(8,128)(2,1)}, bf16[400,512]{1,0:T(8,128)(2,1)}, u32[]{:S(2)}, u32[]{:S(2)}) collective-permute-start(bf16[400,512]{1,0:T(8,128)(2,1)} %collective-permute-done.refs_4_), channel_id=1, source_target_pairs={{0,8},{4,12},{8,16},{12,20},{16,24},{20,28},{24,0},{28,4},{1,9},{5... | collective-permute-start | bytes 1228808 | tf_op jit(solution)/shard_map/ppermute | solution.py:69
  38.2 23.4 %collective-permute-start.9 = (bf16[400,512]{1,0:T(8,128)(2,1)}, bf16[400,512]{1,0:T(8,128)(2,1)S(1)}, u32[]{:S(2)}, u32[]{:S(2)}) collective-permute-start(bf16[400,512]{1,0:T(8,128)(2,1)} %collective-permute-done.8.refs_4_), channel_id=1, source_target_pairs={{0,8},{4,12},{8,16},{12,20},{16,24},{20,28},{24,0},{28,4},{1,9},{5... | collective-permute-start | bytes 1228808 | tf_op jit(solution)/shard_map/ppermute | solution.py:69
  42.8 21.5 %collective-permute-start.3 = (s32[102]{0:T(128)S(1)}, s32[102]{0:T(128)S(1)}, u32[]{:S(2)}, u32[]{:S(2)}) collective-permute-start(s32[102]{0:T(128)S(1)} %pad_add_fusion), channel_id=1, source_target_pairs={{0,4},{4,0},{8,12},{12,8},{16,20},{20,16},{24,28},{28,24},{1,5},{5... | collective-permute-start | bytes 1232 | tf_op jit(solution)/shard_map/ppermute | solution.py:64
  49.5 21.2 %collective-permute-start.2 = (bf16[400,384]{1,0:T(8,128)(2,1)}, bf16[400,384]{1,0:T(8,128)(2,1)S(1)}, u32[]{:S(2)}, u32[]{:S(2)}) collective-permute-start(bf16[400,384]{1,0:T(8,128)(2,1)} %get-tuple-element.93), channel_id=1, source_target_pairs={{0,4},{4,0},{8,12},{12,8},{16,20},{20,16},{24,28},{28,24},{1,5},{5... | collective-permute-start | bytes 921608 | tf_op jit(solution)/shard_map/ppermute | solution.py:64
  52.9 17.6 %collective-permute-start.11 = (bf16[400,512]{1,0:T(8,128)(2,1)}, bf16[400,512]{1,0:T(8,128)(2,1)}, u32[]{:S(2)}, u32[]{:S(2)}) collective-permute-start(bf16[400,512]{1,0:T(8,128)(2,1)} %get-tuple-element.54.refs_3_), channel_id=1, source_target_pairs={{0,8},{4,12},{8,16},{12,20},{16,24},{20,28},{24,0},{28,4},{1,9},{5... | collective-permute-start | bytes 1228808 | tf_op jit(solution)/shard_map/ppermute | solution.py:69
  62.3 22.0 %collective-permute-start.13 = (bf16[400,512]{1,0:T(8,128)(2,1)}, bf16[400,512]{1,0:T(8,128)(2,1)}, u32[]{:S(2)}, u32[]{:S(2)}) collective-permute-start(bf16[400,512]{1,0:T(8,128)(2,1)} %get-tuple-element.54.refs_3_), channel_id=1, source_target_pairs={{0,24},{4,28},{8,0},{12,4},{16,8},{20,12},{24,16},{28,20},{1,25},{... | collective-permute-start | bytes 1228808 | tf_op jit(solution)/shard_map/ppermute | solution.py:69
  70.5 17.5 %collective-permute-start.12 = (bf16[400,512]{1,0:T(8,128)(2,1)}, bf16[400,512]{1,0:T(8,128)(2,1)S(1)}, u32[]{:S(2)}, u32[]{:S(2)}) collective-permute-start(bf16[400,512]{1,0:T(8,128)(2,1)} %collective-permute-done.11.refs_4_), channel_id=1, source_target_pairs={{0,8},{4,12},{8,16},{12,20},{16,24},{20,28},{24,0},{28,4},{1,9},{5... | collective-permute-start | bytes 1228808 | tf_op jit(solution)/shard_map/ppermute | solution.py:69
  76.4 21.4 %collective-permute-start.7 = (bf16[384,512]{1,0:T(8,128)(2,1)S(1)}, bf16[384,512]{1,0:T(8,128)(2,1)S(1)}, u32[]{:S(2)}, u32[]{:S(2)}) collective-permute-start(bf16[384,512]{1,0:T(8,128)(2,1)S(1)} %get-tuple-element.49), channel_id=1, source_target_pairs={{0,4},{4,0},{8,12},{12,8},{16,20},{20,16},{24,28},{28,24},{1,5},{5... | collective-permute-start | bytes 1179656 | tf_op jit(solution)/shard_map/ppermute | solution.py:64
  82.6 15.2 %collective-permute-start.10 = (bf16[384,512]{1,0:T(8,128)(2,1)S(1)}, bf16[384,512]{1,0:T(8,128)(2,1)S(1)}, u32[]{:S(2)}, u32[]{:S(2)}) collective-permute-start(bf16[384,512]{1,0:T(8,128)(2,1)S(1)} %get-tuple-element.51), channel_id=1, source_target_pairs={{0,4},{4,0},{8,12},{12,8},{16,20},{20,16},{24,28},{28,24},{1,5},{5... | collective-permute-start | bytes 1179656 | tf_op jit(solution)/shard_map/ppermute | solution.py:64
  82.9 13.3 %collective-permute-start.15 = (bf16[400,512]{1,0:T(8,128)(2,1)}, bf16[400,512]{1,0:T(8,128)(2,1)}, u32[]{:S(2)}, u32[]{:S(2)}) collective-permute-start(bf16[400,512]{1,0:T(8,128)(2,1)} %bitcast.17.refs_2_), channel_id=1, source_target_pairs={{0,8},{4,12},{8,16},{12,20},{16,24},{20,28},{24,0},{28,4},{1,9},{5... | collective-permute-start | bytes 1228808 | tf_op jit(solution)/shard_map/ppermute | solution.py:69
  93.2 14.2 %collective-permute-start.14 = (bf16[384,512]{1,0:T(8,128)(2,1)}, bf16[384,512]{1,0:T(8,128)(2,1)}, u32[]{:S(2)}, u32[]{:S(2)}) collective-permute-start(bf16[384,512]{1,0:T(8,128)(2,1)} %get-tuple-element.55), channel_id=1, source_target_pairs={{0,4},{4,0},{8,12},{12,8},{16,20},{20,16},{24,28},{28,24},{1,5},{5... | collective-permute-start | bytes 1179656 | tf_op jit(solution)/shard_map/ppermute | solution.py:64
  95.0 16.2 %collective-permute-start.17 = (bf16[400,512]{1,0:T(8,128)(2,1)}, bf16[400,512]{1,0:T(8,128)(2,1)}, u32[]{:S(2)}, u32[]{:S(2)}) collective-permute-start(bf16[400,512]{1,0:T(8,128)(2,1)} %bitcast.17.refs_2_), channel_id=1, source_target_pairs={{0,24},{4,28},{8,0},{12,4},{16,8},{20,12},{24,16},{28,20},{1,25},{... | collective-permute-start | bytes 1228808 | tf_op jit(solution)/shard_map/ppermute | solution.py:69
  96.3 18.0 %collective-permute-start.16 = (bf16[400,512]{1,0:T(8,128)(2,1)}, bf16[400,512]{1,0:T(8,128)(2,1)}, u32[]{:S(2)}, u32[]{:S(2)}) collective-permute-start(bf16[400,512]{1,0:T(8,128)(2,1)} %collective-permute-done.15.refs_3_), channel_id=1, source_target_pairs={{0,8},{4,12},{8,16},{12,20},{16,24},{20,28},{24,0},{28,4},{1,9},{5... | collective-permute-start | bytes 1228808 | tf_op jit(solution)/shard_map/ppermute | solution.py:69
  110.8 10.5 %collective-permute-start.20 = (bf16[384,512]{1,0:T(8,128)(2,1)S(1)}, bf16[384,512]{1,0:T(8,128)(2,1)S(1)}, u32[]{:S(2)}, u32[]{:S(2)}) collective-permute-start(bf16[384,512]{1,0:T(8,128)(2,1)S(1)} %attend.1.refs_1_), channel_id=1, source_target_pairs={{0,4},{4,0},{8,12},{12,8},{16,20},{20,16},{24,28},{28,24},{1,5},{5... | collective-permute-start | bytes 1179656 | tf_op jit(solution)/shard_map/ppermute | solution.py:64
  117.2 7.3 %collective-permute-start.18 = (bf16[2,400,384]{2,1,0:T(8,128)(2,1)S(1)}, bf16[2,400,384]{2,1,0:T(8,128)(2,1)S(1)}, u32[]{:S(2)}, u32[]{:S(2)}) collective-permute-start(bf16[2,400,384]{2,1,0:T(8,128)(2,1)S(1)} %get-tuple-element.62), channel_id=1, source_target_pairs={{0,1},{1,0},{2,3},{3,2},{4,5},{5,4},{6,7},{7,6},{8,9},{9,8},{10,11... | collective-permute-start | bytes 1843208 | tf_op jit(solution)/shard_map/ppermute | solution.py:64
  124.4 2.1 %collective-permute-start.21 = (bf16[2,400,384]{2,1,0:T(8,128)(2,1)S(1)}, bf16[2,400,384]{2,1,0:T(8,128)(2,1)S(1)}, u32[]{:S(2)}, u32[]{:S(2)}) collective-permute-start(bf16[2,400,384]{2,1,0:T(8,128)(2,1)S(1)} %get-tuple-element.67), channel_id=1, source_target_pairs={{0,1},{1,0},{2,3},{3,2},{4,5},{5,4},{6,7},{7,6},{8,9},{9,8},{10,11... | collective-permute-start | bytes 1843208 | tf_op jit(solution)/shard_map/ppermute | solution.py:64
  124.6 10.1 %collective-permute-start.19 = (bf16[400,384]{1,0:T(8,128)(2,1)S(1)}, bf16[400,384]{1,0:T(8,128)(2,1)S(1)}, u32[]{:S(2)}, u32[]{:S(2)}) collective-permute-start(bf16[400,384]{1,0:T(8,128)(2,1)S(1)} %far_sum.2), channel_id=1, source_target_pairs={{0,2},{1,3},{2,0},{3,1},{4,6},{5,7},{6,4},{7,5},{8,10},{9,11},{10,... | collective-permute-start | bytes 921608 | tf_op jit(solution)/shard_map/ppermute | solution.py:64
  126.6 14.3 %collective-permute-start.22 = (bf16[400,384]{1,0:T(8,128)(2,1)S(1)}, bf16[400,384]{1,0:T(8,128)(2,1)S(1)}, u32[]{:S(2)}, u32[]{:S(2)}) collective-permute-start(bf16[400,384]{1,0:T(8,128)(2,1)S(1)} %far_sum.3), channel_id=1, source_target_pairs={{0,2},{1,3},{2,0},{3,1},{4,6},{5,7},{6,4},{7,5},{8,10},{9,11},{10,... | collective-permute-start | bytes 921608 | tf_op jit(solution)/shard_map/ppermute | solution.py:64
  142.7 37.2 %all-to-all-start = ((bf16[8,2,24,1600]{3,2,1,0:T(8,128)(2,1)}), bf16[8,2,24,1600]{3,2,1,0:T(8,128)(2,1)S(1)}, u32[]{:S(2)}, u32[]{:S(2)}) async-start(bf16[8,2,24,1600]{3,2,1,0:T(8,128)(2,1)} %get-tuple-element.70), calls=%async_computation | async-start | bytes 2555904 | tf_op jit(solution)/shard_map/all_to_all | solution.py:521
  147.3 32.7 %copy-start.9 = (f32[4,800]{1,0:T(4,128)S(1)}, f32[4,800]{1,0:T(4,128)}, u32[]{:S(2)}) copy-start(f32[4,800]{1,0:T(4,128)} %refs_3_.1) | copy-start | bytes 38404
  154.2 3.7 %collective-permute-start.23 = (f32[2,192]{1,0:T(2,128)S(1)}, f32[2,192]{1,0:T(2,128)S(1)}, u32[]{:S(2)}, u32[]{:S(2)}) collective-permute-start(f32[2,192]{1,0:T(2,128)S(1)} %multiply_reduce_fusion), channel_id=1, source_target_pairs={{0,4},{4,0},{8,12},{12,8},{16,20},{20,16},{24,28},{28,24},{1,5},{5... | collective-permute-start | bytes 4616 | tf_op jit(solution)/shard_map/ppermute | solution.py:64
  159.3 3.9 %collective-permute-start.24 = (f32[3,1,8,24]{3,2,1,0:T(8,128)S(1)}, f32[3,1,8,24]{3,2,1,0:T(8,128)S(1)}, u32[]{:S(2)}, u32[]{:S(2)}) collective-permute-start(f32[3,1,8,24]{3,2,1,0:T(8,128)S(1)} %constant_dynamic-update-slice_fusion), channel_id=1, source_target_pairs={{0,4},{4,0},{8,12},{12,8},{16,20},{20,16},{24,28},{28,24},{1,5},{5... | collective-permute-start | bytes 6920 | tf_op jit(solution)/shard_map/ppermute | solution.py:64
  163.2 6.0 %collective-permute-start.25 = (f32[3,2,8,24]{3,2,1,0:T(8,128)S(1)}, f32[3,2,8,24]{3,2,1,0:T(8,128)S(1)}, u32[]{:S(2)}, u32[]{:S(2)}) collective-permute-start(f32[3,2,8,24]{3,2,1,0:T(8,128)S(1)} %pad_maximum_fusion), channel_id=1, source_target_pairs={{0,8},{4,12},{8,0},{12,4},{16,24},{20,28},{24,16},{28,20},{1,9},{5... | collective-permute-start | bytes 13832 | tf_op jit(solution)/shard_map/ppermute | solution.py:64
  165.6 14.2 %collective-permute-start.26 = (f32[3,2,8,24]{3,2,1,0:T(8,128)S(1)}, f32[3,2,8,24]{3,2,1,0:T(8,128)S(1)}, u32[]{:S(2)}, u32[]{:S(2)}) collective-permute-start(f32[3,2,8,24]{3,2,1,0:T(8,128)S(1)} %pad_maximum_fusion), channel_id=1, source_target_pairs={{0,16},{4,20},{8,24},{12,28},{16,0},{20,4},{24,8},{28,12},{1,17},{... | collective-permute-start | bytes 13832 | tf_op jit(solution)/shard_map/ppermute | solution.py:64
  167.7 12.1 %collective-permute-start.27 = (f32[3,2,8,24]{3,2,1,0:T(8,128)S(1)}, f32[3,2,8,24]{3,2,1,0:T(8,128)S(1)}, u32[]{:S(2)}, u32[]{:S(2)}) collective-permute-start(f32[3,2,8,24]{3,2,1,0:T(8,128)S(1)} %pad_maximum_fusion), channel_id=1, source_target_pairs={{0,24},{4,28},{8,16},{12,20},{16,8},{20,12},{24,0},{28,4},{1,25},{... | collective-permute-start | bytes 13832 | tf_op jit(solution)/shard_map/ppermute | solution.py:64
  (20 other events, 169.6 us)
